TPU v7x, 256 devices: a whole 4x4x8 slice. The times are simulated.
256 devices in a mesh: shard: 64 (over z, y, core), dim: 4 (over x).
Axes of the slice: x: 4, y: 4, z: 8, core: 2. Of those that a mesh axis runs over, the one named last changes fastest.
Arguments:
- queries: bfloat16 [128, 16384], P('dim', 'shard'), may hold values from -0.69921875 to 0.69921875
- passages: bfloat16 [128, 524288], P('dim', 'shard'), may hold values from -0.69921875 to 0.69921875
- cand_ids: int32 [512, 2048], P('dim', 'shard'), may hold values from 0 to 127
- counts: int32 [512, 64], P('dim', 'shard'), may hold values from 16 to 32, as said below
Outputs:
- cand_scores: float32 [512, 2048], P('dim', 'shard')
- top_scores: float32 [512, 100], P('dim')
Inputs may be any that keep to these rules, and one draw needn't show every extreme that they name: `counts`: every shard's block of every query has between 16 and 32 live slots, and query 0 has all 32 live on every shard.
All inputs are finite; a program needn't handle non-finite values.
Results may differ from a plain program's by a relative error of at most 0.0003.
Values may be sent and summed in bfloat16 or wider, within the bound.
No kernel may reach another device: no remote copies, remote signals or barrier semaphores. Data moves between devices by JAX's collectives and lax.ppermute only.
A program may use at most 64 MiB of HBM per device.

v0:
```python
import math

import jax
import jax.numpy as jnp
from jax import lax
from jax.sharding import PartitionSpec as P

DOC_TOK = 64
TOPK = 100


def shards(queries, passages, cand_ids, counts):
    doc_full = lax.all_gather(passages, "dim", axis=0, tiled=True)
    all_queries = lax.all_gather(queries, "shard", axis=1, tiled=True)
    own_queries = lax.all_to_all(all_queries, "dim", split_axis=1, concat_axis=0, tiled=True)
    rows, slots = cand_ids.shape
    width = doc_full.shape[0]
    doc_count = doc_full.shape[1] // DOC_TOK
    qtok = own_queries.shape[1] // rows
    block = math.gcd(rows, 16)
    query_blocks = jnp.transpose(own_queries).reshape(rows // block, block * qtok, width)
    passage_ids = lax.broadcasted_iota(jnp.int32, (1, 1, doc_count), 2)

    def score_block(items):
        query_block, id_block = items
        tokens = jnp.dot(query_block, doc_full, preferred_element_type=jnp.float32)
        best_tok = jnp.max(tokens.reshape(block, qtok, doc_count, DOC_TOK), axis=3)
        selector = (id_block[:, :, None] == passage_ids).astype(jnp.float32)
        chosen = jnp.einsum("qtp,qcp->qct", best_tok, selector, precision=lax.Precision.HIGHEST)
        return jnp.mean(chosen, axis=2)

    scores = lax.map(
        score_block, (query_blocks, cand_ids.reshape(rows // block, block, slots))
    ).reshape(rows, slots)
    live = lax.broadcasted_iota(jnp.int32, (rows, slots), 1) < counts
    cand_scores = jnp.where(live, scores, jnp.float32(0.0))
    masked = jnp.where(live, scores, jnp.float32(-1e30))
    every_slot = lax.all_gather(masked, "shard", axis=1, tiled=True)
    top_scores = lax.top_k(every_slot, TOPK)[0]
    return (cand_scores, top_scores)


def solution(mesh):
    return jax.shard_map(
        shards,
        mesh=mesh,
        in_specs=(P("dim", "shard"), P("dim", "shard"), P("dim", "shard"), P("dim", "shard")),
        out_specs=(P("dim", "shard"), P("dim", None)),
        check_vma=False,
    )
```

profile of v0, /device:TPU:1, one launch (start us, length us, event | category | flops | bytes accessed | tf_op | source)
XLA Modules:
  0.0 283.6 jit_solution(12582634190313066073)
XLA Ops:
  7.2 0.7 all-gather.4.cloned.1.call-update
  7.9 0.7 all-gather.6.cloned.1.call-update
  8.6 76.7 %all-gather.4.cloned.1.call-done = bf16[32,16384]{1,0:T(8,128)(2,1)} async-done(((bf16[32,256]{1,0:T(8,128)(2,1)}), bf16[32,16384]{1,0:T(8,128)(2,1)}) %all-gather.4.cloned.1.call-update) | async-done | bytes 1048592 | tf_op jit(solution)/shard_map/all_gather | solution.py:14
  85.3 2.3 copy.42
  87.6 3.9 %all-to-all-start = ((bf16[32,4,4096]{2,0,1:T(8,128)(2,1)}), bf16[32,4,4096]{2,0,1:T(8,128)(2,1)S(1)}, u32[]{:S(2)}, u32[]{:S(2)}) async-start(bf16[32,4,4096]{2,0,1:T(8,128)(2,1)} %bitcast.31), calls=%async_computation | async-start | bytes 2097152 | tf_op jit(solution)/shard_map/all_to_all | solution.py:15
  91.6 18.1 %all-to-all-done = bf16[32,4,4096]{2,0,1:T(8,128)(2,1)S(1)} async-done(((bf16[32,4,4096]{2,0,1:T(8,128)(2,1)}), bf16[32,4,4096]{2,0,1:T(8,128)(2,1)S(1)}, u32[]{:S(2)}, u32[]{:S(2)}) %all-to-all-start) | async-done | bytes 1048608 | tf_op jit(solution)/shard_map/all_to_all | solution.py:15
  109.8 0.7 copy.31
  110.4 13.7 %all-gather.6.cloned.1.call-done = bf16[128,8192]{1,0:T(8,128)(2,1)} async-done(((bf16[32,8192]{1,0:T(8,128)(2,1)}), bf16[128,8192]{1,0:T(8,128)(2,1)}) %all-gather.6.cloned.1.call-update) | async-done | bytes 2097168 | tf_op jit(solution)/shard_map/all_gather | solution.py:13
  124.1 3.2 %copy.25 = bf16[128,8192]{0,1:T(8,128)(2,1)S(1)} copy(bf16[128,8192]{1,0:T(8,128)(2,1)} %all-gather.6.cloned.1.call-done) | data formatting | bytes 4194304
  127.4 23.8 %while.11 = (s32[]{:T(128)}, f32[8,16,32]{2,1,0:T(8,128)S(1)}, s32[8,16,32]{2,1,0:T(8,128)S(1)}, bf16[8,512,128]{2,1,0:T(8,128)(2,1)S(1)}, bf16[128,8192]{0,1:T(8,128)(2,1)S(1)}, /*index=5*/s32[]{:T(128)}) while((s32[]{:T(128)}, f32[8,16,32]{2,1,0:T(8,128)S(1)}, s32[8,16,32]{2,1,0:T(8,128)S(1)}, ...), condition=%wide.region_3.4_spmd.clone, body=%wide.region_0.3_spmd.clone.sunk | while | flops 1103118336 | bytes 3039313 | solution.py:32
  127.4 2.5 convolution_reduce_fusion.4
  129.9 0.4 convolution_reduce_fusion.5
  130.4 2.5 convolution_reduce_fusion.4
  132.9 0.4 convolution_reduce_fusion.5
  133.4 2.5 convolution_reduce_fusion.4
  135.9 0.4 convolution_reduce_fusion.5
  136.3 2.5 convolution_reduce_fusion.4
  138.8 0.4 convolution_reduce_fusion.5
  139.3 2.5 convolution_reduce_fusion.4
  141.8 0.4 convolution_reduce_fusion.5
  142.3 2.5 convolution_reduce_fusion.4
  144.8 0.4 convolution_reduce_fusion.5
  145.3 2.5 convolution_reduce_fusion.4
  147.8 0.4 convolution_reduce_fusion.5
  148.2 2.5 convolution_reduce_fusion.4
  150.7 0.4 convolution_reduce_fusion.5
  151.3 0.7 copy.26
  152.0 0.7 copy.28
  152.7 73.6 %all-gather.8.cloned.1.call-done = f32[128,2048]{0,1:T(8,128)} async-done(((f32[128,32]{0,1:T(8,128)}), f32[128,2048]{0,1:T(8,128)}) %all-gather.8.cloned.1.call-update) | async-done | bytes 1048592 | tf_op jit(solution)/shard_map/all_gather | solution.py:38
  226.3 49.7 %top_k.9 = (f32[128,2048]{0,1:T(8,128)S(1)}, s32[128,2048]{0,1:T(8,128)}) sort(f32[128,2048]{0,1:T(8,128)} %all-gather.8.cloned.1.call-done, s32[128,2048]{0,1:T(8,128)S(1)} %iota.15.clone), dimensions={1}, to_apply=%region_4.5 | sort | flops 4718592 | bytes 4194304 | tf_op jit(solution)/shard_map/top_k | solution.py:39
  276.0 0.3 copy.34
  276.3 0.7 copy.29
  (37 shorter events, 0.6 us)
Async XLA Ops:
  7.2 78.1 %all-gather.4.cloned.1.call-start = ((), (), s32[]{:S(2)}) async-start(), calls=%async_computation.1 | async-start | bytes 1064960 | tf_op jit(solution)/shard_map/all_gather | solution.py:14
  7.9 116.2 %all-gather.6.cloned.1.call-start = ((), (), s32[]{:S(2)}) async-start(), calls=%async_computation.2 | async-start | bytes 2621440 | tf_op jit(solution)/shard_map/all_gather | solution.py:13
  85.3 6.2 %copy-start = (s32[128,32]{0,1:T(8,128)S(1)}, s32[128,32]{0,1:T(8,128)}, u32[]{:S(2)}) copy-start(s32[128,32]{0,1:T(8,128)} %param.8) | copy-start | bytes 49156
  87.6 22.1 %all-to-all-start = ((bf16[32,4,4096]{2,0,1:T(8,128)(2,1)}), bf16[32,4,4096]{2,0,1:T(8,128)(2,1)S(1)}, u32[]{:S(2)}, u32[]{:S(2)}) async-start(bf16[32,4,4096]{2,0,1:T(8,128)(2,1)} %bitcast.31), calls=%async_computation | async-start | bytes 2097152 | tf_op jit(solution)/shard_map/all_to_all | solution.py:15
  91.5 134.7 %all-gather.8.cloned.1.call-start = ((), (), s32[]{:S(2)}) async-start(), calls=%async_computation.3 | async-start | bytes 1064960 | tf_op jit(solution)/shard_map/all_gather | solution.py:38
  127.4 23.8 %copy-start.1 = (s32[128,1]{0,1:T(1,128)S(1)}, s32[128,1]{0,1:T(1,128)}, u32[]{:S(2)}) copy-start(s32[128,1]{0,1:T(1,128)} %param.9) | copy-start | bytes 1540
Sparse Core Ops, SparseCore 0:
  10.6 74.6 all-gather.3
  87.1 36.9 all-gather.5
  152.1 74.0 all-gather.7
where the time goes:
time: 284 us
  waiting for transfers between devices  183 us (64%)
  other arithmetic  49.8 us (18%)
  matrix products  23.2 us (8%)
  between operations  13.8 us (5%)
  local copies, waits for them, and re-layouts  8.98 us (3%)
  starting transfers between devices  3.97 us (1%)
    all_gather x1, waiting for transfers between devices, shards(): all_queries = lax.all_gather(queries, 'shard', axis=1, tiled=True)  76.7 us
    all_gather x1, waiting for transfers between devices, shards(): every_slot = lax.all_gather(masked, 'shard', axis=1, tiled=True)  73.6 us
    top_k x1, other arithmetic, shards(): top_scores = lax.top_k(every_slot, TOPK)[0]  49.7 us
    dot_general x8, matrix products, score_block(): tokens = jnp.dot(query_block, doc_full, preferred_element_type=jnp.float32)  19.9 us
    all_to_all x1, waiting for transfers between devices, shards(): lax.all_to_all(all_queries, 'dim', split_axis=1, concat_axis=0, tiled=True)  18.1 us
    all_gather x1, waiting for transfers between devices, shards(): doc_full = lax.all_gather(passages, 'dim', axis=0, tiled=True)  13.7 us
  transfers between devices with their start and end apart: 4, of which 4 were waited for; matrix products, arithmetic and copies ran while one was open for 1% of the time, Pallas kernels for 0%

commit v1 on v0

v1 whole, which is shorter than its diff:
```python
import jax
import jax.numpy as jnp
from jax import lax
from jax.experimental import pallas as pl
from jax.experimental.pallas import tpu as pltpu
from jax.sharding import Mesh, PartitionSpec as P

DOC_TOK = 64
QTOK = 32
TOPK = 100
LOWEST = -1e30
SHARD = ("zh", "zl", "y", "core")
ALL = SHARD + ("dim",)


def transpose_docs(d0, d1, d2, d3, out):
    rows = d0.shape[0]
    step = 512
    for start in range(0, d0.shape[1], step):
        cols = slice(start, start + step)
        block = jnp.concatenate([d[:, cols] for d in (d0, d1, d2, d3)], axis=0)
        out[cols, :] = jnp.transpose(block)


def docs_kernel(d0, d1, d2, d3, out):
    transpose_docs(d0, d1, d2, d3, out)


def score_kernel(docs, qa, qb, ids, counts, cand, send, best, kept):
    core = lax.axis_index("core")
    turn = lax.rem(lax.axis_index("zh") - lax.axis_index("dim") + 4, 4)
    docs_n = best.shape[0]
    sources = qa.shape[0]
    slots = ids.shape[1]
    tile = 512
    per = tile // DOC_TOK

    def one(source, q, side):
        weights = jnp.concatenate([q[source, lax.rem(turn + k, 4)] for k in range(4)], axis=0)
        for t in range(docs_n // per):
            tokens = jnp.dot(docs[t * tile : (t + 1) * tile, :], weights, preferred_element_type=jnp.float32)
            best[t * per : (t + 1) * per, :] = jnp.max(tokens.reshape(per, DOC_TOK, tokens.shape[1]), axis=1)
        turned = jnp.transpose(best[...])
        mean = jnp.sum(turned.reshape(-1, QTOK, docs_n), axis=1) * (1.0 / QTOK)
        queries = mean.shape[0]
        rows = pl.ds(pl.multiple_of((source * 2 + side) * queries, queries), queries)
        index = jnp.concatenate([ids[rows, :], jnp.zeros((queries, docs_n - slots), jnp.int32)], axis=1)
        kept[rows, :] = jnp.take_along_axis(mean, index, axis=1)

    def pair(source, carry):
        one(source, qa, core)
        one(source, qb, 1 - core)
        return carry

    lax.fori_loop(0, sources, pair, 0)
    scores = kept[...]
    live = lax.broadcasted_iota(jnp.int32, scores.shape, 1) < counts[...]
    cand[...] = jnp.where(live, scores, 0.0)[:, :slots]
    masked = jnp.transpose(jnp.where(live, scores, LOWEST))[:slots, :]
    half = masked.shape[1] // 2
    send[...] = jnp.where(core == 0, masked, pltpu.roll(masked, half, 1))


def exchange(values, i, j):
    a, b = values[i], values[j]
    values[i] = jnp.maximum(a, b)
    values[j] = jnp.minimum(a, b)


def odd_even_merge(values, lo, n, r):
    m = r * 2
    if m < n:
        odd_even_merge(values, lo, n, m)
        odd_even_merge(values, lo + r, n, m)
        for i in range(lo + r, lo + n - r, m):
            exchange(values, i, i + r)
    else:
        exchange(values, lo, lo + r)


def odd_even_sort(values, lo, n):
    if n > 1:
        m = n // 2
        odd_even_sort(values, lo, m)
        odd_even_sort(values, lo + m, m)
        odd_even_merge(values, lo, n, 1)


def clean(values, lo, n):
    if n > 1:
        m = n // 2
        for i in range(m):
            exchange(values, lo + i, lo + i + m)
        clean(values, lo, m)
        clean(values, lo + m, m)


def top_kernel(pieces, out):
    count = pieces.shape[0]
    values = [pieces[i] for i in range(count)]
    odd_even_sort(values, 0, count)
    for axis, shift in ((1, 64), (0, 4), (0, 2), (0, 1)):
        other = [pltpu.roll(v, shift, axis) for v in values]
        values = [jnp.maximum(values[i], other[count - 1 - i]) for i in range(count)]
        clean(values, 0, count)
    stacked = jnp.concatenate([v[0:1, :] for v in values], axis=0)
    out[...] = jnp.transpose(stacked)


def vmem(n):
    return [pl.BlockSpec(memory_space=pltpu.VMEM)] * n


def shards(queries, passages, cand_ids, counts):
    sizes = {a: lax.axis_size(a) for a in ALL}
    flat = lambda zh, zl, y, c, x: (((zh * 2 + zl) * 4 + y) * 2 + c) * 4 + x
    moves = [
        [
            (flat(zh, zl, y, c, x), flat((x + j) % 4, zl, y, c, zh))
            for zh in range(4)
            for zl in range(2)
            for y in range(4)
            for c in range(2)
            for x in range(4)
        ]
        for j in range(4)
    ]
    parts = jnp.stack([lax.ppermute(queries, ALL, moves[j]) for j in range(4)])
    doc_parts = [passages] + [
        lax.ppermute(passages, "dim", [(i, (i + k) % 4) for i in range(4)]) for k in (1, 2, 3)
    ]
    mine = lax.all_to_all(jnp.broadcast_to(parts[None], (8,) + parts.shape), ("zl", "y"), 0, 0, tiled=True)
    swap = [(0, 1), (1, 0)]
    theirs = lax.ppermute(mine, "core", swap)
    width, doc_cols = 4 * passages.shape[0], passages.shape[1]
    docs = pl.pallas_call(
        docs_kernel,
        out_shape=jax.ShapeDtypeStruct((doc_cols, width), passages.dtype),
        in_specs=vmem(4),
        out_specs=vmem(1)[0],
        name="docs",
    )(*doc_parts)
    rows, slots = cand_ids.shape
    doc_count = doc_cols // DOC_TOK
    cand_scores, send = pl.pallas_call(
        score_kernel,
        out_shape=(
            jax.ShapeDtypeStruct((rows, slots), jnp.float32),
            jax.ShapeDtypeStruct((slots, rows), jnp.float32),
        ),
        in_specs=vmem(5),
        out_specs=tuple(vmem(2)),
        scratch_shapes=[
            pltpu.VMEM((doc_count, queries.shape[1]), jnp.float32),
            pltpu.VMEM((rows, doc_count), jnp.float32),
        ],
        name="score",
    )(docs, mine, theirs, cand_ids, counts)
    got = lax.ppermute(send, "core", swap)
    lane = lax.broadcasted_iota(jnp.int32, send.shape, 1)
    piece = jnp.where(lane < rows // 2, send, got)
    pieces = lax.all_to_all(
        jnp.broadcast_to(piece[None], (32,) + piece.shape), ("zh", "zl", "y"), 0, 0, tiled=True
    )
    top = pl.pallas_call(
        top_kernel,
        out_shape=jax.ShapeDtypeStruct((rows, rows), jnp.float32),
        in_specs=vmem(1),
        out_specs=vmem(1)[0],
        name="top",
    )(pieces.reshape(-1, 8, rows))
    other = lax.ppermute(top, "core", swap)
    row = lax.broadcasted_iota(jnp.int32, top.shape, 0)
    top_scores = jnp.where((row // (rows // 2)) == lax.axis_index("core"), top, other)[:, :TOPK]
    return (cand_scores, top_scores)


def solution(mesh):
    split = Mesh(mesh.devices.reshape(4, 2, 4, 2, 4), ALL)
    own = P(SHARD, "dim")
    return jax.shard_map(
        shards,
        mesh=split,
        in_specs=(P("dim", SHARD),) * 4,
        out_specs=(P("dim", SHARD), P("dim", None)),
        check_vma=False,
    )
```

time: 284 us -> 120 us (0.42)
  waiting for transfers between devices: 183 us -> 34.6 us
  other arithmetic: 49.8 us -> 1.7 us
  starting transfers between devices: 3.97 us -> 45 us
  Pallas kernels: 0 us -> 29.2 us
  matrix products: 23.2 us -> 0 us
  between operations: 13.8 us -> 0.69 us
    all_gather x3 -> x0, waiting for transfers between devices: 164 us -> none  [the longest x1 76.7 us: shards(): all_queries = lax.all_gather(queries, 'shard', axis=1, tiled=True)]
    top_k x1 -> x0, other arithmetic: 49.7 us -> none  [shards(): top_scores = lax.top_k(every_slot, TOPK)[0]]
    ppermute x0 -> x10, starting transfers between devices: none -> 32.4 us  [the longest x4 12.8 us: shards(): parts = jnp.stack([lax.ppermute(queries, ALL, moves[j]) for j in range(4)])]
    pallas_call x0 -> x3, Pallas kernels: none -> 29.2 us  [the longest x1 22.8 us: shards(): pl.pallas_call(score_kernel, out_shape=(jax.ShapeDtypeStruct((rows, slots...]
    dot_general x16 -> x0, matrix products: 23.2 us -> none  [the longest x8 19.9 us: score_block(): tokens = jnp.dot(query_block, doc_full, preferred_element_type=jnp.float32)]
    ppermute x0 -> x10, waiting for transfers between devices: none -> 18 us  [the longest x3 13.9 us: shards(): lax.ppermute(passages, 'dim', [(i, (i + k) % 4) for i in range(4)])]
    all_to_all x1 -> x2, starting transfers between devices: 3.89 us -> 12.6 us  [the longest x1 7.96 us: shards(): lax.all_to_all(jnp.broadcast_to(piece[None], (32,) + piece.shape), ('zh',...]
    all_to_all x1 -> x2, waiting for transfers between devices: 18.1 us -> 16.6 us  [the longest x1 16.6 us: shards(): lax.all_to_all(jnp.broadcast_to(piece[None], (32,) + piece.shape), ('zh',...]
  transfers between devices with their start and end apart: 4 -> 12, of which waited for: 4 -> 6; matrix products, arithmetic and copies ran while one was open for 1% -> 3% of each run, Pallas kernels for 0% -> 3%
where the time goes in v1:
time: 120 us
  starting transfers between devices  45 us (38%)
  waiting for transfers between devices  34.6 us (29%)
  Pallas kernels  29.2 us (24%)
  local copies, waits for them, and re-layouts  8.4 us (7%)
  other arithmetic  1.7 us (1%)
    pallas_call x1, Pallas kernels, shards(): pl.pallas_call(score_kernel, out_shape=(jax.ShapeDtypeStruct((rows, slots...  22.8 us
    all_to_all x1, waiting for transfers between devices, shards(): lax.all_to_all(jnp.broadcast_to(piece[None], (32,) + piece.shape), ('zh',...  16.6 us
    ppermute x3, waiting for transfers between devices, shards(): lax.ppermute(passages, 'dim', [(i, (i + k) % 4) for i in range(4)])  13.9 us
    ppermute x4, starting transfers between devices, shards(): parts = jnp.stack([lax.ppermute(queries, ALL, moves[j]) for j in range(4)])  12.8 us
    ppermute x3, starting transfers between devices, shards(): lax.ppermute(passages, 'dim', [(i, (i + k) % 4) for i in range(4)])  11.1 us
    all_to_all x1, starting transfers between devices, shards(): lax.all_to_all(jnp.broadcast_to(piece[None], (32,) + piece.shape), ('zh',...  7.96 us
    unnamed x18, local copies, waits for them, and re-layouts  6.66 us
    all_to_all x1, starting transfers between devices, shards(): lax.all_to_all(jnp.broadcast_to(parts[None], (8,) + parts.shape), ('zl',...  4.64 us
  transfers between devices with their start and end apart: 12, of which 6 were waited for; matrix products, arithmetic and copies ran while one was open for 3% of the time, Pallas kernels for 3%

profile of v1, /device:TPU:1, one launch (start us, length us, event | category | flops | bytes accessed | tf_op | source)
XLA Modules:
  0.0 119.6 jit_solution(14762016357430757072)
XLA Ops:
  0.6 6.9 %collective-permute-start.6 = (bf16[32,256]{1,0:T(8,128)(2,1)}, bf16[32,256]{1,0:T(8,128)(2,1)S(1)}, u32[]{:S(2)}, u32[]{:S(2)}) collective-permute-start(bf16[32,256]{1,0:T(8,128)(2,1)} %param.4), channel_id=1, source_target_pairs={{0,192},{1,0},{2,64},{3,128},{4,196},{5,4},{6,68},{7,132},{8,200},... | collective-permute-start | bytes 49160 | tf_op jit(solution)/shard_map/ppermute | solution.py:128
  7.6 4.5 %collective-permute-start.5 = (bf16[32,256]{1,0:T(8,128)(2,1)}, bf16[32,256]{1,0:T(8,128)(2,1)S(1)}, u32[]{:S(2)}, u32[]{:S(2)}) collective-permute-start(bf16[32,256]{1,0:T(8,128)(2,1)} %param.4), channel_id=1, source_target_pairs={{0,128},{1,192},{2,0},{3,64},{4,132},{5,196},{6,4},{7,68},{8,136},... | collective-permute-start | bytes 49160 | tf_op jit(solution)/shard_map/ppermute | solution.py:128
  12.1 0.0 collective-permute-start.4
  12.1 1.4 %collective-permute-start.3 = (bf16[32,256]{1,0:T(8,128)(2,1)}, bf16[32,256]{1,0:T(8,128)(2,1)S(1)}, u32[]{:S(2)}, u32[]{:S(2)}) collective-permute-start(bf16[32,256]{1,0:T(8,128)(2,1)} %param.4), channel_id=1, source_target_pairs={{0,0},{1,64},{2,128},{3,192},{4,4},{5,68},{6,132},{7,196},{8,8},{9... | collective-permute-start | bytes 49160 | tf_op jit(solution)/shard_map/ppermute | solution.py:128
  13.5 2.6 %collective-permute-done.4 = bf16[32,256]{1,0:T(8,128)(2,1)S(1)} collective-permute-done((bf16[32,256]{1,0:T(8,128)(2,1)}, bf16[32,256]{1,0:T(8,128)(2,1)S(1)}, u32[]{:S(2)}, u32[]{:S(2)}) %collective-permute-start.4) | collective-permute-done | bytes 16416 | tf_op jit(solution)/shard_map/ppermute | solution.py:128
  16.1 0.9 broadcast_in_dim.4
  17.0 4.6 %all-to-all-start = ((bf16[8,4,32,256]{3,2,1,0:T(8,128)(2,1)}), bf16[8,4,32,256]{3,2,1,0:T(8,128)(2,1)S(1)}, u32[]{:S(2)}, u32[]{:S(2)}) async-start(bf16[8,4,32,256]{3,2,1,0:T(8,128)(2,1)} %broadcast_in_dim.4), calls=%async_computation | async-start | bytes 1048576 | tf_op jit(solution)/shard_map/all_to_all | solution.py:132
  21.6 3.6 %collective-permute-start = (bf16[32,8192]{1,0:T(8,128)(2,1)}, bf16[32,8192]{1,0:T(8,128)(2,1)S(1)}, u32[]{:S(2)}, u32[]{:S(2)}) collective-permute-start(bf16[32,8192]{1,0:T(8,128)(2,1)} %d0.1), channel_id=1, source_target_pairs={{0,1},{1,2},{2,3},{3,0},{4,5},{5,6},{6,7},{7,4},{8,9},{9,10},{10,1... | collective-permute-start | bytes 1572872 | tf_op jit(solution)/shard_map/ppermute | solution.py:130
  25.3 5.5 %collective-permute-start.1 = (bf16[32,8192]{1,0:T(8,128)(2,1)}, bf16[32,8192]{1,0:T(8,128)(2,1)S(1)}, u32[]{:S(2)}, u32[]{:S(2)}) collective-permute-start(bf16[32,8192]{1,0:T(8,128)(2,1)} %d0.1), channel_id=1, source_target_pairs={{0,2},{1,3},{2,0},{3,1},{4,6},{5,7},{6,4},{7,5},{8,10},{9,11},{10,... | collective-permute-start | bytes 1572872 | tf_op jit(solution)/shard_map/ppermute | solution.py:130
  30.8 2.0 %collective-permute-start.2 = (bf16[32,8192]{1,0:T(8,128)(2,1)}, bf16[32,8192]{1,0:T(8,128)(2,1)S(1)}, u32[]{:S(2)}, u32[]{:S(2)}) collective-permute-start(bf16[32,8192]{1,0:T(8,128)(2,1)} %d0.1), channel_id=1, source_target_pairs={{0,3},{1,0},{2,1},{3,2},{4,7},{5,4},{6,5},{7,6},{8,11},{9,8},{10,9... | collective-permute-start | bytes 1572872 | tf_op jit(solution)/shard_map/ppermute | solution.py:130
  32.8 3.8 %collective-permute-start.7 = (bf16[8,4,32,256]{3,2,1,0:T(8,128)(2,1)S(1)}, bf16[8,4,32,256]{3,2,1,0:T(8,128)(2,1)S(1)}, u32[]{:S(2)}, u32[]{:S(2)}) collective-permute-start(bf16[8,4,32,256]{3,2,1,0:T(8,128)(2,1)S(1)} %all-to-all-done.qa), channel_id=1, source_target_pairs={{0,4},{4,0},{1,5},{5,1},{2,6},{6,2},{3,7},{7,3},{8,12},{12,8},{9,1... | collective-permute-start | bytes 1572872 | tf_op jit(solution)/shard_map/ppermute | solution.py:134
  36.5 1.4 %copy.6.ids = s32[128,32]{1,0:T(8,128)} copy(s32[128,32]{0,1:T(8,128)} %param.6) | data formatting | bytes 32768 | tf_op args[2]
  38.0 1.4 %copy.7.counts = s32[128,1]{1,0:T(8,128)} copy(s32[128,1]{0,1:T(1,128)} %param.7) | data formatting | bytes 1024 | tf_op args[3]
  39.4 12.0 %collective-permute-done.1.d2 = bf16[32,8192]{1,0:T(8,128)(2,1)S(1)} collective-permute-done((bf16[32,8192]{1,0:T(8,128)(2,1)}, bf16[32,8192]{1,0:T(8,128)(2,1)S(1)}, u32[]{:S(2)}, u32[]{:S(2)}) %collective-permute-start.1) | collective-permute-done | bytes 524320 | tf_op jit(solution)/shard_map/ppermute | solution.py:130
  51.4 1.9 %collective-permute-done.2.d3 = bf16[32,8192]{1,0:T(8,128)(2,1)S(1)} collective-permute-done((bf16[32,8192]{1,0:T(8,128)(2,1)}, bf16[32,8192]{1,0:T(8,128)(2,1)S(1)}, u32[]{:S(2)}, u32[]{:S(2)}) %collective-permute-start.2) | collective-permute-done | bytes 524320 | tf_op jit(solution)/shard_map/ppermute | solution.py:130
  53.3 0.8 copy-done.5
  54.1 3.4 %docs.1 = bf16[8192,128]{1,0:T(8,128)(2,1)} custom-call(bf16[32,8192]{1,0:T(8,128)(2,1)} %d0.1, bf16[32,8192]{1,0:T(8,128)(2,1)} %copy-done.3, bf16[32,8192]{1,0:T(8,128)(2,1)} %copy-done.4, bf16[32,8192]{1,0:T(8,128)(2,1)} %copy-done.5), custom_call_target="tpu_custom_call" | custom-call | tf_op jit(solution)/shard_map/docs/pallas_call | solution.py:136
  57.6 0.8 copy-done.2
  58.4 22.8 %score.1 = (f32[128,32]{1,0:T(8,128)}, f32[32,128]{1,0:T(8,128)}) custom-call(bf16[8192,128]{1,0:T(8,128)(2,1)} %docs.1, bf16[8,4,32,256]{3,2,1,0:T(8,128)(2,1)} %copy-done, bf16[8,4,32,256]{3,2,1,0:T(8,128)(2,1)} %copy-done.2, s32[128,32]{1,0:T(8,128)} %copy.6.ids, s32[128,1]{1,0:T(8,128)} %copy.7.counts), custom_call_target="tpu_custom_call" | custom-call | tf_op jit(solution)/shard_map/score/pallas_call | solution.py:145
  81.2 2.5 %collective-permute-start.8 = (f32[32,128]{1,0:T(8,128)}, f32[32,128]{1,0:T(8,128)S(1)}, u32[]{:S(2)}, u32[]{:S(2)}) collective-permute-start(f32[32,128]{1,0:T(8,128)} %get-tuple-element.5), channel_id=1, source_target_pairs={{0,4},{4,0},{1,5},{5,1},{2,6},{6,2},{3,7},{7,3},{8,12},{12,8},{9,1... | collective-permute-start | bytes 49160 | tf_op jit(solution)/shard_map/ppermute | solution.py:159
  83.7 1.0 collective-permute-done.8
  84.7 0.7 broadcast_select_fusion
  85.4 0.9 broadcast_in_dim.5
  86.3 8.0 %all-to-all-start.1 = ((f32[32,32,128]{2,1,0:T(8,128)}), f32[32,32,128]{2,1,0:T(8,128)S(1)}, u32[]{:S(2)}, u32[]{:S(2)}) async-start(f32[32,32,128]{2,1,0:T(8,128)} %broadcast_in_dim.5), calls=%async_computation.1 | async-start | bytes 1048576 | tf_op jit(solution)/shard_map/all_to_all | solution.py:162
  94.3 16.6 %all-to-all-done.1 = f32[32,32,128]{2,1,0:T(8,128)S(1)} async-done(((f32[32,32,128]{2,1,0:T(8,128)}), f32[32,32,128]{2,1,0:T(8,128)S(1)}, u32[]{:S(2)}, u32[]{:S(2)}) %all-to-all-start.1) | async-done | bytes 524320 | tf_op jit(solution)/shard_map/all_to_all | solution.py:162
  110.8 0.8 copy-done.1
  111.6 3.0 %top.1 = f32[128,128]{1,0:T(8,128)} custom-call(f32[128,8,128]{2,1,0:T(8,128)} %bitcast.5), custom_call_target="tpu_custom_call" | custom-call | tf_op jit(solution)/shard_map/top/pallas_call | solution.py:165
  114.6 2.2 %collective-permute-start.9 = (f32[128,128]{1,0:T(8,128)}, f32[128,128]{1,0:T(8,128)S(1)}, u32[]{:S(2)}, u32[]{:S(2)}) collective-permute-start(f32[128,128]{1,0:T(8,128)} %top.1), channel_id=1, source_target_pairs={{0,4},{4,0},{1,5},{5,1},{2,6},{6,2},{3,7},{7,3},{8,12},{12,8},{9,1... | collective-permute-start | bytes 196616 | tf_op jit(solution)/shard_map/ppermute | solution.py:172
  116.8 0.7 copy.8
  117.5 0.4 collective-permute-done.9
  117.9 1.0 slice_select_fusion
  118.9 0.7 copy.9
  (21 shorter events, 0.1 us)
Async XLA Ops:
  0.6 12.8 %collective-permute-start.6 = (bf16[32,256]{1,0:T(8,128)(2,1)}, bf16[32,256]{1,0:T(8,128)(2,1)S(1)}, u32[]{:S(2)}, u32[]{:S(2)}) collective-permute-start(bf16[32,256]{1,0:T(8,128)(2,1)} %param.4), channel_id=1, source_target_pairs={{0,192},{1,0},{2,64},{3,128},{4,196},{5,4},{6,68},{7,132},{8,200},... | collective-permute-start | bytes 49160 | tf_op jit(solution)/shard_map/ppermute | solution.py:128
  7.6 5.9 %collective-permute-start.5 = (bf16[32,256]{1,0:T(8,128)(2,1)}, bf16[32,256]{1,0:T(8,128)(2,1)S(1)}, u32[]{:S(2)}, u32[]{:S(2)}) collective-permute-start(bf16[32,256]{1,0:T(8,128)(2,1)} %param.4), channel_id=1, source_target_pairs={{0,128},{1,192},{2,0},{3,64},{4,132},{5,196},{6,4},{7,68},{8,136},... | collective-permute-start | bytes 49160 | tf_op jit(solution)/shard_map/ppermute | solution.py:128
  12.1 4.0 %collective-permute-start.4 = (bf16[32,256]{1,0:T(8,128)(2,1)}, bf16[32,256]{1,0:T(8,128)(2,1)S(1)}, u32[]{:S(2)}, u32[]{:S(2)}) collective-permute-start(bf16[32,256]{1,0:T(8,128)(2,1)} %param.4), channel_id=1, source_target_pairs={{0,64},{1,128},{2,192},{3,0},{4,68},{5,132},{6,196},{7,4},{8,72},{... | collective-permute-start | bytes 49160 | tf_op jit(solution)/shard_map/ppermute | solution.py:128
  12.1 4.0 %collective-permute-start.3 = (bf16[32,256]{1,0:T(8,128)(2,1)}, bf16[32,256]{1,0:T(8,128)(2,1)S(1)}, u32[]{:S(2)}, u32[]{:S(2)}) collective-permute-start(bf16[32,256]{1,0:T(8,128)(2,1)} %param.4), channel_id=1, source_target_pairs={{0,0},{1,64},{2,128},{3,192},{4,4},{5,68},{6,132},{7,196},{8,8},{9... | collective-permute-start | bytes 49160 | tf_op jit(solution)/shard_map/ppermute | solution.py:128
  17.0 15.8 %all-to-all-start = ((bf16[8,4,32,256]{3,2,1,0:T(8,128)(2,1)}), bf16[8,4,32,256]{3,2,1,0:T(8,128)(2,1)S(1)}, u32[]{:S(2)}, u32[]{:S(2)}) async-start(bf16[8,4,32,256]{3,2,1,0:T(8,128)(2,1)} %broadcast_in_dim.4), calls=%async_computation | async-start | bytes 1048576 | tf_op jit(solution)/shard_map/all_to_all | solution.py:132
  21.6 17.7 %collective-permute-start = (bf16[32,8192]{1,0:T(8,128)(2,1)}, bf16[32,8192]{1,0:T(8,128)(2,1)S(1)}, u32[]{:S(2)}, u32[]{:S(2)}) collective-permute-start(bf16[32,8192]{1,0:T(8,128)(2,1)} %d0.1), channel_id=1, source_target_pairs={{0,1},{1,2},{2,3},{3,0},{4,5},{5,6},{6,7},{7,4},{8,9},{9,10},{10,1... | collective-permute-start | bytes 1572872 | tf_op jit(solution)/shard_map/ppermute | solution.py:130
  25.3 26.1 %collective-permute-start.1 = (bf16[32,8192]{1,0:T(8,128)(2,1)}, bf16[32,8192]{1,0:T(8,128)(2,1)S(1)}, u32[]{:S(2)}, u32[]{:S(2)}) collective-permute-start(bf16[32,8192]{1,0:T(8,128)(2,1)} %d0.1), channel_id=1, source_target_pairs={{0,2},{1,3},{2,0},{3,1},{4,6},{5,7},{6,4},{7,5},{8,10},{9,11},{10,... | collective-permute-start | bytes 1572872 | tf_op jit(solution)/shard_map/ppermute | solution.py:130
  30.8 22.5 %collective-permute-start.2 = (bf16[32,8192]{1,0:T(8,128)(2,1)}, bf16[32,8192]{1,0:T(8,128)(2,1)S(1)}, u32[]{:S(2)}, u32[]{:S(2)}) collective-permute-start(bf16[32,8192]{1,0:T(8,128)(2,1)} %d0.1), channel_id=1, source_target_pairs={{0,3},{1,0},{2,1},{3,2},{4,7},{5,4},{6,5},{7,6},{8,11},{9,8},{10,9... | collective-permute-start | bytes 1572872 | tf_op jit(solution)/shard_map/ppermute | solution.py:130
  32.8 24.8 %copy-start = (bf16[8,4,32,256]{3,2,1,0:T(8,128)(2,1)}, bf16[8,4,32,256]{3,2,1,0:T(8,128)(2,1)S(1)}, u32[]{:S(2)}) copy-start(bf16[8,4,32,256]{3,2,1,0:T(8,128)(2,1)S(1)} %all-to-all-done.qa) | copy-start | bytes 1572868
  32.8 24.8 %collective-permute-start.7 = (bf16[8,4,32,256]{3,2,1,0:T(8,128)(2,1)S(1)}, bf16[8,4,32,256]{3,2,1,0:T(8,128)(2,1)S(1)}, u32[]{:S(2)}, u32[]{:S(2)}) collective-permute-start(bf16[8,4,32,256]{3,2,1,0:T(8,128)(2,1)S(1)} %all-to-all-done.qa), channel_id=1, source_target_pairs={{0,4},{4,0},{1,5},{5,1},{2,6},{6,2},{3,7},{7,3},{8,12},{12,8},{9,1... | collective-permute-start | bytes 1572872 | tf_op jit(solution)/shard_map/ppermute | solution.py:134
  39.4 13.9 %copy-start.3 = (bf16[32,8192]{1,0:T(8,128)(2,1)}, bf16[32,8192]{1,0:T(8,128)(2,1)S(1)}, u32[]{:S(2)}) copy-start(bf16[32,8192]{1,0:T(8,128)(2,1)S(1)} %collective-permute-done.d1) | copy-start | bytes 1572868
  51.4 1.9 %copy-start.4 = (bf16[32,8192]{1,0:T(8,128)(2,1)}, bf16[32,8192]{1,0:T(8,128)(2,1)S(1)}, u32[]{:S(2)}) copy-start(bf16[32,8192]{1,0:T(8,128)(2,1)S(1)} %collective-permute-done.1.d2) | copy-start | bytes 1572868
  53.3 0.8 copy-start.5
  57.6 0.8 copy-start.2
  81.2 35.7 %copy-start.6 = (f32[128,32]{1,0:T(8,128)S(1)}, f32[128,32]{1,0:T(8,128)}, u32[]{:S(2)}) copy-start(f32[128,32]{1,0:T(8,128)} %get-tuple-element.6) | copy-start | bytes 49156
  81.2 3.5 %collective-permute-start.8 = (f32[32,128]{1,0:T(8,128)}, f32[32,128]{1,0:T(8,128)S(1)}, u32[]{:S(2)}, u32[]{:S(2)}) collective-permute-start(f32[32,128]{1,0:T(8,128)} %get-tuple-element.5), channel_id=1, source_target_pairs={{0,4},{4,0},{1,5},{5,1},{2,6},{6,2},{3,7},{7,3},{8,12},{12,8},{9,1... | collective-permute-start | bytes 49160 | tf_op jit(solution)/shard_map/ppermute | solution.py:159
  86.3 24.5 %all-to-all-start.1 = ((f32[32,32,128]{2,1,0:T(8,128)}), f32[32,32,128]{2,1,0:T(8,128)S(1)}, u32[]{:S(2)}, u32[]{:S(2)}) async-start(f32[32,32,128]{2,1,0:T(8,128)} %broadcast_in_dim.5), calls=%async_computation.1 | async-start | bytes 1048576 | tf_op jit(solution)/shard_map/all_to_all | solution.py:162
  110.8 0.8 copy-start.1
  114.6 3.3 %collective-permute-start.9 = (f32[128,128]{1,0:T(8,128)}, f32[128,128]{1,0:T(8,128)S(1)}, u32[]{:S(2)}, u32[]{:S(2)}) collective-permute-start(f32[128,128]{1,0:T(8,128)} %top.1), channel_id=1, source_target_pairs={{0,4},{4,0},{1,5},{5,1},{2,6},{6,2},{3,7},{7,3},{8,12},{12,8},{9,1... | collective-permute-start | bytes 196616 | tf_op jit(solution)/shard_map/ppermute | solution.py:172

commit v2 on v1

v2 whole, which is shorter than its diff:
```python
import jax
import jax.numpy as jnp
from jax import lax
from jax.experimental import pallas as pl
from jax.experimental.pallas import tpu as pltpu
from jax.sharding import Mesh, PartitionSpec as P

DOC_TOK = 64
QTOK = 32
TOPK = 100
LOWEST = -1e30
SHARD = ("zh", "zl", "y", "core")
ALL = SHARD + ("dim",)


def repeat_kernel(a, b, c, d, near, far, out):
    for i in range(out.shape[0]):
        for j, part in enumerate((a, b, c, d)):
            out[i, j] = part[...]


def score_kernel(d0, d1, d2, d3, qa, qb, ids, counts, cand, send, docs, best, kept, picks):
    core = lax.axis_index("core")
    turn = lax.rem(lax.axis_index("zh") - lax.axis_index("dim") + 4, 4)
    docs_n = best.shape[0]
    sources = qa.shape[0]
    slots = ids.shape[0]
    tile = 512
    per = tile // DOC_TOK
    picks[...] = jnp.transpose(jnp.concatenate([ids[...], jnp.zeros((docs_n - slots, ids.shape[1]), jnp.int32)], axis=0))

    def one(source, q, side, first):
        weights = jnp.concatenate([q[source, lax.rem(turn + k, 4)] for k in range(4)], axis=0)
        for t in range(docs_n // per):
            span = slice(t * tile, (t + 1) * tile)
            if first:
                block = jnp.transpose(jnp.concatenate([d[:, span] for d in (d0, d1, d2, d3)], axis=0))
                docs[span, :] = block
            else:
                block = docs[span, :]
            tokens = jnp.dot(block, weights, preferred_element_type=jnp.float32)
            best[t * per : (t + 1) * per, :] = jnp.max(tokens.reshape(per, DOC_TOK, tokens.shape[1]), axis=1)
        turned = jnp.transpose(best[...])
        mean = jnp.sum(turned.reshape(-1, QTOK, docs_n), axis=1) * (1.0 / QTOK)
        queries = mean.shape[0]
        rows = pl.ds(pl.multiple_of((source * 2 + side) * queries, queries), queries)
        kept[rows, :] = jnp.take_along_axis(mean, picks[rows, :], axis=1)

    one(0, qa, core, True)
    one(0, qb, 1 - core, False)

    def pair(source, carry):
        one(source, qa, core, False)
        one(source, qb, 1 - core, False)
        return carry

    lax.fori_loop(1, sources, pair, 0)
    scores = jnp.transpose(kept[...])[:slots, :]
    live = lax.broadcasted_iota(jnp.int32, scores.shape, 0) < counts[...]
    cand[...] = jnp.where(live, scores, 0.0)
    masked = jnp.where(live, scores, LOWEST)
    for i in range(send.shape[0]):
        send[i] = masked


def exchange(values, i, j):
    a, b = values[i], values[j]
    values[i] = jnp.maximum(a, b)
    values[j] = jnp.minimum(a, b)


def odd_even_merge(values, lo, n, r):
    m = r * 2
    if m < n:
        odd_even_merge(values, lo, n, m)
        odd_even_merge(values, lo + r, n, m)
        for i in range(lo + r, lo + n - r, m):
            exchange(values, i, i + r)
    else:
        exchange(values, lo, lo + r)


def odd_even_sort(values, lo, n):
    if n > 1:
        m = n // 2
        odd_even_sort(values, lo, m)
        odd_even_sort(values, lo + m, m)
        odd_even_merge(values, lo, n, 1)


def clean(values, lo, n):
    if n > 1:
        m = n // 2
        for i in range(m):
            exchange(values, lo + i, lo + i + m)
        clean(values, lo, m)
        clean(values, lo + m, m)


def top_kernel(pieces, falling, rising):
    count = pieces.shape[0]
    values = [pieces[i] for i in range(count)]
    odd_even_sort(values, 0, count)
    for shift in (4, 2, 1):
        other = [pltpu.roll(v, shift, 0) for v in values]
        values = [jnp.maximum(values[i], other[count - 1 - i]) for i in range(count)]
        clean(values, 0, count)
    rows = [v[0:1, :] for v in values]
    falling[...] = jnp.concatenate(rows, axis=0)
    rising[...] = jnp.concatenate(rows[::-1], axis=0)


def merge_kernel(falling, rising, out):
    best = jnp.maximum(falling[...], rising[...])
    count = best.shape[0]
    values = [best[i : i + 8, :] for i in range(0, count, 8)]
    clean(values, 0, len(values))
    row = lax.broadcasted_iota(jnp.int32, values[0].shape, 0)
    for shift in (4, 2, 1):
        upper = (row & shift) == 0
        values = [
            jnp.where(upper, jnp.maximum(v, pltpu.roll(v, 8 - shift, 0)), jnp.minimum(v, pltpu.roll(v, shift, 0)))
            for v in values
        ]
    out[...] = jnp.concatenate(values, axis=0)[: out.shape[0], :]


def vmem(n):
    return [pl.BlockSpec(memory_space=pltpu.VMEM)] * n


def anywhere(n):
    return [pl.BlockSpec(memory_space=pl.ANY)] * n


def shards(queries, passages, cand_ids, counts):
    flat = lambda zh, x: zh * 4 + x
    moves = [[(flat(zh, x), flat((x + j) % 4, zh)) for zh in range(4) for x in range(4)] for j in range(4)]
    parts = [lax.ppermute(queries, ("zh", "dim"), moves[j]) for j in range(4)]
    round_dim = lambda k: lax.ppermute(passages, "dim", [(i, (i + k) % 4) for i in range(4)])
    d1, d3 = round_dim(1), round_dim(3)
    d2 = round_dim(2)
    repeated = pl.pallas_call(
        repeat_kernel,
        out_shape=jax.ShapeDtypeStruct((8, 4) + queries.shape, queries.dtype),
        in_specs=vmem(4) + anywhere(2),
        out_specs=vmem(1)[0],
        name="repeat",
    )(*parts, d1, d3)
    mine = lax.all_to_all(repeated, ("zl", "y"), 0, 0, tiled=True)
    swap = [(0, 1), (1, 0)]
    theirs = lax.ppermute(mine, "core", swap)
    width, doc_cols = 4 * passages.shape[0], passages.shape[1]
    rows, slots = cand_ids.shape
    doc_count = doc_cols // DOC_TOK
    cand_scores, send = pl.pallas_call(
        score_kernel,
        out_shape=(
            jax.ShapeDtypeStruct((slots, rows), jnp.float32),
            jax.ShapeDtypeStruct((32, slots, rows), jnp.float32),
        ),
        in_specs=vmem(8),
        out_specs=tuple(vmem(2)),
        scratch_shapes=[
            pltpu.VMEM((doc_cols, width), passages.dtype),
            pltpu.VMEM((doc_count, queries.shape[1]), jnp.float32),
            pltpu.VMEM((rows, doc_count), jnp.float32),
            pltpu.VMEM((rows, doc_count), jnp.int32),
        ],
        name="score",
    )(passages, d1, d2, d3, mine, theirs, jnp.transpose(cand_ids), jnp.transpose(counts))
    pieces = lax.all_to_all(send, ("zh", "zl", "y"), 0, 0, tiled=True)
    falling, rising = pl.pallas_call(
        top_kernel,
        out_shape=(jax.ShapeDtypeStruct((128, rows), jnp.float32),) * 2,
        in_specs=vmem(1),
        out_specs=tuple(vmem(2)),
        name="top",
    )(pieces.reshape(-1, 8, rows))
    other = lax.ppermute(rising, "core", swap)
    top_scores = pl.pallas_call(
        merge_kernel,
        out_shape=jax.ShapeDtypeStruct((TOPK, rows), jnp.float32),
        in_specs=vmem(2),
        out_specs=vmem(1)[0],
        name="merge",
    )(falling, other)
    return (jnp.transpose(cand_scores), jnp.transpose(top_scores))


def solution(mesh):
    split = Mesh(mesh.devices.reshape(4, 2, 4, 2, 4), ALL)
    return jax.shard_map(
        shards,
        mesh=split,
        in_specs=(P("dim", SHARD),) * 4,
        out_specs=(P("dim", SHARD), P("dim", None)),
        check_vma=False,
    )
```

time: 120 us -> 102 us (0.85)
  waiting for transfers between devices: 34.6 us -> 7.66 us
  blocking collectives: 0 us -> 22.1 us
  starting transfers between devices: 45 us -> 39.4 us
  local copies, waits for them, and re-layouts: 8.4 us -> 3.15 us
  other arithmetic: 1.7 us -> 0 us
    all_to_all x0 -> x1, blocking collectives: none -> 22.1 us  [shards(): pieces = lax.all_to_all(send, ('zh', 'zl', 'y'), 0, 0, tiled=True)]
    all_to_all x2 -> x1, waiting for transfers between devices: 16.6 us -> 2.17 us  [shards(): mine = lax.all_to_all(repeated, ('zl', 'y'), 0, 0, tiled=True)]
    ppermute x3, waiting for transfers between devices: 13.9 us -> 2.85 us  [shards(): lax.ppermute(passages, 'dim', [(i, (i + k) % 4) for i in range(4)])]
    all_to_all x2 -> x1, starting transfers between devices: 12.6 us -> 4.9 us  [shards(): mine = lax.all_to_all(repeated, ('zl', 'y'), 0, 0, tiled=True)]
    ppermute x6 -> x5, starting transfers between devices: 17.5 us -> 21.9 us  [the longest x4 15.5 us: shards(): parts = [lax.ppermute(queries, ('zh', 'dim'), moves[j]) for j in range(4)]]
    unnamed x18 -> x22, local copies, waits for them, and re-layouts: 6.66 us -> 3.15 us
    ppermute x3, starting transfers between devices: 11.1 us -> 8.44 us  [shards(): lax.ppermute(passages, 'dim', [(i, (i + k) % 4) for i in range(4)])]
    broadcast_in_dim x2 -> x0, local copies, waits for them, and re-layouts: 1.74 us -> none  [the longest x1 0.87 us: shards(): jnp.broadcast_to(piece[None], (32,) + piece.shape)]
  transfers between devices with their start and end apart: 12 -> 10, of which waited for: 6 -> 5; matrix products, arithmetic and copies ran while one was open for 3% -> 0% of each run, Pallas kernels for 3% -> 0%
where the time goes in v2:
time: 102 us
  starting transfers between devices  39.4 us (39%)
  Pallas kernels  28.9 us (28%)
  blocking collectives  22.1 us (22%)
  waiting for transfers between devices  7.66 us (8%)
  local copies, waits for them, and re-layouts  3.15 us (3%)
    pallas_call x1, Pallas kernels, shards(): pl.pallas_call(score_kernel, out_shape=(jax.ShapeDtypeStruct((slots, rows...  23 us
    all_to_all x1, blocking collectives, shards(): pieces = lax.all_to_all(send, ('zh', 'zl', 'y'), 0, 0, tiled=True)  22.1 us
    ppermute x4, starting transfers between devices, shards(): parts = [lax.ppermute(queries, ('zh', 'dim'), moves[j]) for j in range(4)]  15.5 us
    ppermute x3, starting transfers between devices, shards(): lax.ppermute(passages, 'dim', [(i, (i + k) % 4) for i in range(4)])  8.44 us
    ppermute x1, starting transfers between devices, shards(): other = lax.ppermute(rising, 'core', swap)  6.39 us
    all_to_all x1, starting transfers between devices, shards(): mine = lax.all_to_all(repeated, ('zl', 'y'), 0, 0, tiled=True)  4.9 us
    ppermute x1, starting transfers between devices, shards(): theirs = lax.ppermute(mine, 'core', swap)  4.13 us
    unnamed x22, local copies, waits for them, and re-layouts  3.15 us
  transfers between devices with their start and end apart: 10, of which 5 were waited for; matrix products, arithmetic and copies ran while one was open for 0% of the time, Pallas kernels for 0%

profile of v2, /device:TPU:1, one launch (start us, length us, event | category | flops | bytes accessed | tf_op | source)
XLA Modules:
  0.0 101.8 jit_solution(10797773563452247731)
XLA Ops:
  0.6 2.1 %collective-permute-start = (bf16[32,8192]{1,0:T(8,128)(2,1)}, bf16[32,8192]{1,0:T(8,128)(2,1)S(1)}, u32[]{:S(2)}, u32[]{:S(2)}) collective-permute-start(bf16[32,8192]{1,0:T(8,128)(2,1)} %d0.1), channel_id=1, source_target_pairs={{0,1},{1,2},{2,3},{3,0},{4,5},{5,6},{6,7},{7,4},{8,9},{9,10},{10,1... | collective-permute-start | bytes 1572872 | tf_op jit(solution)/shard_map/ppermute | solution.py:140
  2.7 1.4 %collective-permute-start.2 = (bf16[32,8192]{1,0:T(8,128)(2,1)}, bf16[32,8192]{1,0:T(8,128)(2,1)S(1)}, u32[]{:S(2)}, u32[]{:S(2)}) collective-permute-start(bf16[32,8192]{1,0:T(8,128)(2,1)} %d0.1), channel_id=1, source_target_pairs={{0,3},{1,0},{2,1},{3,2},{4,7},{5,4},{6,5},{7,6},{8,11},{9,8},{10,9... | collective-permute-start | bytes 1572872 | tf_op jit(solution)/shard_map/ppermute | solution.py:140
  4.1 3.1 %collective-permute-start.4 = (bf16[32,256]{1,0:T(8,128)(2,1)}, bf16[32,256]{1,0:T(8,128)(2,1)S(1)}, u32[]{:S(2)}, u32[]{:S(2)}) collective-permute-start(bf16[32,256]{1,0:T(8,128)(2,1)} %param.4), channel_id=1, source_target_pairs={{0,64},{1,128},{2,192},{3,0},{64,65},{65,129},{66,193},{67,1},{128... | collective-permute-start | bytes 49160 | tf_op jit(solution)/shard_map/ppermute | solution.py:139
  7.2 1.4 %collective-permute-start.3 = (bf16[32,256]{1,0:T(8,128)(2,1)}, bf16[32,256]{1,0:T(8,128)(2,1)S(1)}, u32[]{:S(2)}, u32[]{:S(2)}) collective-permute-start(bf16[32,256]{1,0:T(8,128)(2,1)} %param.4), channel_id=1, source_target_pairs={{0,0},{1,64},{2,128},{3,192},{64,1},{65,65},{66,129},{67,193},{128... | collective-permute-start | bytes 49160 | tf_op jit(solution)/shard_map/ppermute | solution.py:139
  8.6 4.9 %collective-permute-start.6 = (bf16[32,256]{1,0:T(8,128)(2,1)}, bf16[32,256]{1,0:T(8,128)(2,1)S(1)}, u32[]{:S(2)}, u32[]{:S(2)}) collective-permute-start(bf16[32,256]{1,0:T(8,128)(2,1)} %param.4), channel_id=1, source_target_pairs={{0,192},{1,0},{2,64},{3,128},{64,193},{65,1},{66,65},{67,129},{128... | collective-permute-start | bytes 49160 | tf_op jit(solution)/shard_map/ppermute | solution.py:139
  13.5 0.5 collective-permute-done.4.b
  13.9 6.2 %collective-permute-start.5 = (bf16[32,256]{1,0:T(8,128)(2,1)}, bf16[32,256]{1,0:T(8,128)(2,1)S(1)}, u32[]{:S(2)}, u32[]{:S(2)}) collective-permute-start(bf16[32,256]{1,0:T(8,128)(2,1)} %param.4), channel_id=1, source_target_pairs={{0,128},{1,192},{2,0},{3,64},{64,129},{65,193},{66,1},{67,65},{128... | collective-permute-start | bytes 49160 | tf_op jit(solution)/shard_map/ppermute | solution.py:139
  20.1 0.0 collective-permute-done.3.a
  20.1 0.0 collective-permute-done.6.d
  20.1 0.0 copy-start.9
  20.1 1.1 %collective-permute-done.5.c = bf16[32,256]{1,0:T(8,128)(2,1)S(1)} collective-permute-done((bf16[32,256]{1,0:T(8,128)(2,1)}, bf16[32,256]{1,0:T(8,128)(2,1)S(1)}, u32[]{:S(2)}, u32[]{:S(2)}) %collective-permute-start.5) | collective-permute-done | bytes 16416 | tf_op jit(solution)/shard_map/ppermute | solution.py:139
  21.2 0.0 collective-permute-done.near.d1
  21.2 0.0 collective-permute-done.2.far.d3
  21.2 0.6 copy-done.10
  21.8 0.2 copy-done
  22.0 0.8 copy-done.1
  22.8 1.6 %repeat.1 = bf16[8,4,32,256]{3,2,1,0:T(8,128)(2,1)} custom-call(bf16[32,256]{1,0:T(8,128)(2,1)} %copy-done.8, bf16[32,256]{1,0:T(8,128)(2,1)} %copy-done.7, bf16[32,256]{1,0:T(8,128)(2,1)} %copy-done.10, bf16[32,256]{1,0:T(8,128)(2,1)} %copy-done.9, bf16[32,8192]{1,0:T(8,128)(2,1)} %copy-done, bf16[32,8192]{1,0:T(8,128)(2,1)} %copy-done.1), custom_call_target="tpu_custom_call" | custom-call | tf_op jit(solution)/shard_map/repeat/pallas_call | solution.py:143
  24.4 4.9 %all-to-all-start = ((bf16[8,4,32,256]{3,2,1,0:T(8,128)(2,1)}), bf16[8,4,32,256]{3,2,1,0:T(8,128)(2,1)S(1)}, u32[]{:S(2)}, u32[]{:S(2)}) async-start(bf16[8,4,32,256]{3,2,1,0:T(8,128)(2,1)} %repeat.1), calls=%async_computation | async-start | bytes 1048576 | tf_op jit(solution)/shard_map/all_to_all | solution.py:150
  29.3 5.0 %collective-permute-start.1 = (bf16[32,8192]{1,0:T(8,128)(2,1)S(1)}, bf16[32,8192]{1,0:T(8,128)(2,1)S(1)}, u32[]{:S(2)}, u32[]{:S(2)}) collective-permute-start(bf16[32,8192]{1,0:T(8,128)(2,1)S(1)} %copy-done.3), channel_id=1, source_target_pairs={{0,2},{1,3},{2,0},{3,1},{4,6},{5,7},{6,4},{7,5},{8,10},{9,11},{10,... | collective-permute-start | bytes 1572872 | tf_op jit(solution)/shard_map/ppermute | solution.py:140
  34.3 2.2 %all-to-all-done.qa = bf16[8,4,32,256]{3,2,1,0:T(8,128)(2,1)S(1)} async-done(((bf16[8,4,32,256]{3,2,1,0:T(8,128)(2,1)}), bf16[8,4,32,256]{3,2,1,0:T(8,128)(2,1)S(1)}, u32[]{:S(2)}, u32[]{:S(2)}) %all-to-all-start) | async-done | bytes 524320 | tf_op jit(solution)/shard_map/all_to_all | solution.py:150
  36.4 4.1 %collective-permute-start.7 = (bf16[8,4,32,256]{3,2,1,0:T(8,128)(2,1)S(1)}, bf16[8,4,32,256]{3,2,1,0:T(8,128)(2,1)S(1)}, u32[]{:S(2)}, u32[]{:S(2)}) collective-permute-start(bf16[8,4,32,256]{3,2,1,0:T(8,128)(2,1)S(1)} %all-to-all-done.qa), channel_id=1, source_target_pairs={{0,4},{4,0},{1,5},{5,1},{2,6},{6,2},{3,7},{7,3},{8,12},{12,8},{9,1... | collective-permute-start | bytes 1572872 | tf_op jit(solution)/shard_map/ppermute | solution.py:152
  40.5 2.8 %collective-permute-done.1.d2 = bf16[32,8192]{1,0:T(8,128)(2,1)S(1)} collective-permute-done((bf16[32,8192]{1,0:T(8,128)(2,1)S(1)}, bf16[32,8192]{1,0:T(8,128)(2,1)S(1)}, u32[]{:S(2)}, u32[]{:S(2)}) %collective-permute-start.1) | collective-permute-done | bytes 524320 | tf_op jit(solution)/shard_map/ppermute | solution.py:140
  43.4 0.0 collective-permute-done.7.qb
  43.4 0.8 copy-done.4
  44.2 0.2 copy-done.5
  44.4 23.0 %score.1 = (f32[32,128]{1,0:T(8,128)}, f32[32,32,128]{2,1,0:T(8,128)}) custom-call(bf16[32,8192]{1,0:T(8,128)(2,1)} %d0.1, bf16[32,8192]{1,0:T(8,128)(2,1)} %copy-done, bf16[32,8192]{1,0:T(8,128)(2,1)} %copy-done.4, bf16[32,8192]{1,0:T(8,128)(2,1)} %copy-done.1, bf16[8,4,32,256]{3,2,1,0:T(8,128)(2,1)} %copy-done.2, bf16[8,4,32,256]{3,2,1,0:T(8,128)(2,1)} %copy-done.5, ...), custom_call_target="tpu_custom_call" | custom-call | tf_op jit(solution)/shard_map/score/pallas_call | solution.py:156
  67.3 22.1 %all_to_all.10 = f32[32,32,128]{2,1,0:T(8,128)} all-to-all(f32[32,32,128]{2,1,0:T(8,128)} %get-tuple-element.7), channel_id=1, replica_groups=mesh['zh'=4,'zl'=2,'y'=4,'core'=2,'dim'=4] {'zh','zl','y'}, dimensions={0} | all-to-all | bytes 1048576 | tf_op jit(solution)/shard_map/all_to_all | solution.py:172
  89.4 2.7 %top.1 = (f32[128,128]{1,0:T(8,128)}, f32[128,128]{1,0:T(8,128)}) custom-call(f32[128,8,128]{2,1,0:T(8,128)} %bitcast.5), custom_call_target="tpu_custom_call" | custom-call | tf_op jit(solution)/shard_map/top/pallas_call | solution.py:173
  92.2 6.4 %collective-permute-start.8 = (f32[128,128]{1,0:T(8,128)}, f32[128,128]{1,0:T(8,128)S(1)}, u32[]{:S(2)}, u32[]{:S(2)}) collective-permute-start(f32[128,128]{1,0:T(8,128)} %get-tuple-element.9), channel_id=1, source_target_pairs={{0,4},{4,0},{1,5},{5,1},{2,6},{6,2},{3,7},{7,3},{8,12},{12,8},{9,1... | collective-permute-start | bytes 196616 | tf_op jit(solution)/shard_map/ppermute | solution.py:180
  98.6 1.1 %collective-permute-done.8.rising = f32[128,128]{1,0:T(8,128)S(1)} collective-permute-done((f32[128,128]{1,0:T(8,128)}, f32[128,128]{1,0:T(8,128)S(1)}, u32[]{:S(2)}, u32[]{:S(2)}) %collective-permute-start.8) | collective-permute-done | bytes 65568 | tf_op jit(solution)/shard_map/ppermute | solution.py:180
  99.7 0.6 copy-done.6
  100.3 1.5 %merge.1 = f32[100,128]{1,0:T(8,128)} custom-call(f32[128,128]{1,0:T(8,128)} %get-tuple-element.8.falling, f32[128,128]{1,0:T(8,128)} %copy-done.6), custom_call_target="tpu_custom_call" | custom-call | tf_op jit(solution)/shard_map/merge/pallas_call | solution.py:181
  (15 shorter events, 0.0 us)
Async XLA Ops:
  0.6 20.6 %collective-permute-start = (bf16[32,8192]{1,0:T(8,128)(2,1)}, bf16[32,8192]{1,0:T(8,128)(2,1)S(1)}, u32[]{:S(2)}, u32[]{:S(2)}) collective-permute-start(bf16[32,8192]{1,0:T(8,128)(2,1)} %d0.1), channel_id=1, source_target_pairs={{0,1},{1,2},{2,3},{3,0},{4,5},{5,6},{6,7},{7,4},{8,9},{9,10},{10,1... | collective-permute-start | bytes 1572872 | tf_op jit(solution)/shard_map/ppermute | solution.py:140
  2.7 18.4 %collective-permute-start.2 = (bf16[32,8192]{1,0:T(8,128)(2,1)}, bf16[32,8192]{1,0:T(8,128)(2,1)S(1)}, u32[]{:S(2)}, u32[]{:S(2)}) collective-permute-start(bf16[32,8192]{1,0:T(8,128)(2,1)} %d0.1), channel_id=1, source_target_pairs={{0,3},{1,0},{2,1},{3,2},{4,7},{5,4},{6,5},{7,6},{8,11},{9,8},{10,9... | collective-permute-start | bytes 1572872 | tf_op jit(solution)/shard_map/ppermute | solution.py:140
  4.1 9.8 %collective-permute-start.4 = (bf16[32,256]{1,0:T(8,128)(2,1)}, bf16[32,256]{1,0:T(8,128)(2,1)S(1)}, u32[]{:S(2)}, u32[]{:S(2)}) collective-permute-start(bf16[32,256]{1,0:T(8,128)(2,1)} %param.4), channel_id=1, source_target_pairs={{0,64},{1,128},{2,192},{3,0},{64,65},{65,129},{66,193},{67,1},{128... | collective-permute-start | bytes 49160 | tf_op jit(solution)/shard_map/ppermute | solution.py:139
  7.2 12.9 %collective-permute-start.3 = (bf16[32,256]{1,0:T(8,128)(2,1)}, bf16[32,256]{1,0:T(8,128)(2,1)S(1)}, u32[]{:S(2)}, u32[]{:S(2)}) collective-permute-start(bf16[32,256]{1,0:T(8,128)(2,1)} %param.4), channel_id=1, source_target_pairs={{0,0},{1,64},{2,128},{3,192},{64,1},{65,65},{66,129},{67,193},{128... | collective-permute-start | bytes 49160 | tf_op jit(solution)/shard_map/ppermute | solution.py:139
  8.6 11.5 %collective-permute-start.6 = (bf16[32,256]{1,0:T(8,128)(2,1)}, bf16[32,256]{1,0:T(8,128)(2,1)S(1)}, u32[]{:S(2)}, u32[]{:S(2)}) collective-permute-start(bf16[32,256]{1,0:T(8,128)(2,1)} %param.4), channel_id=1, source_target_pairs={{0,192},{1,0},{2,64},{3,128},{64,193},{65,1},{66,65},{67,129},{128... | collective-permute-start | bytes 49160 | tf_op jit(solution)/shard_map/ppermute | solution.py:139
  13.9 7.3 %copy-start.7 = (bf16[32,256]{1,0:T(8,128)(2,1)}, bf16[32,256]{1,0:T(8,128)(2,1)S(1)}, u32[]{:S(2)}) copy-start(bf16[32,256]{1,0:T(8,128)(2,1)S(1)} %collective-permute-done.4.b) | copy-start | bytes 49156
  13.9 7.2 %collective-permute-start.5 = (bf16[32,256]{1,0:T(8,128)(2,1)}, bf16[32,256]{1,0:T(8,128)(2,1)S(1)}, u32[]{:S(2)}, u32[]{:S(2)}) collective-permute-start(bf16[32,256]{1,0:T(8,128)(2,1)} %param.4), channel_id=1, source_target_pairs={{0,128},{1,192},{2,0},{3,64},{64,129},{65,193},{66,1},{67,65},{128... | collective-permute-start | bytes 49160 | tf_op jit(solution)/shard_map/ppermute | solution.py:139
  20.1 1.1 %copy-start.8 = (bf16[32,256]{1,0:T(8,128)(2,1)}, bf16[32,256]{1,0:T(8,128)(2,1)S(1)}, u32[]{:S(2)}) copy-start(bf16[32,256]{1,0:T(8,128)(2,1)S(1)} %collective-permute-done.3.a) | copy-start | bytes 49156
  20.1 1.1 %copy-start.9 = (bf16[32,256]{1,0:T(8,128)(2,1)}, bf16[32,256]{1,0:T(8,128)(2,1)S(1)}, u32[]{:S(2)}) copy-start(bf16[32,256]{1,0:T(8,128)(2,1)S(1)} %collective-permute-done.6.d) | copy-start | bytes 49156
  21.2 0.6 copy-start.10
  21.2 0.8 copy-start
  22.0 0.8 copy-start.1
  24.4 4.9 %copy-start.3 = (bf16[32,8192]{1,0:T(8,128)(2,1)S(1)}, bf16[32,8192]{1,0:T(8,128)(2,1)}, u32[]{:S(2)}) copy-start(bf16[32,8192]{1,0:T(8,128)(2,1)} %d0.1) | copy-start | bytes 1572868
  24.4 12.0 %all-to-all-start = ((bf16[8,4,32,256]{3,2,1,0:T(8,128)(2,1)}), bf16[8,4,32,256]{3,2,1,0:T(8,128)(2,1)S(1)}, u32[]{:S(2)}, u32[]{:S(2)}) async-start(bf16[8,4,32,256]{3,2,1,0:T(8,128)(2,1)} %repeat.1), calls=%async_computation | async-start | bytes 1048576 | tf_op jit(solution)/shard_map/all_to_all | solution.py:150
  29.3 14.1 %collective-permute-start.1 = (bf16[32,8192]{1,0:T(8,128)(2,1)S(1)}, bf16[32,8192]{1,0:T(8,128)(2,1)S(1)}, u32[]{:S(2)}, u32[]{:S(2)}) collective-permute-start(bf16[32,8192]{1,0:T(8,128)(2,1)S(1)} %copy-done.3), channel_id=1, source_target_pairs={{0,2},{1,3},{2,0},{3,1},{4,6},{5,7},{6,4},{7,5},{8,10},{9,11},{10,... | collective-permute-start | bytes 1572872 | tf_op jit(solution)/shard_map/ppermute | solution.py:140
  36.4 7.0 %copy-start.2 = (bf16[8,4,32,256]{3,2,1,0:T(8,128)(2,1)}, bf16[8,4,32,256]{3,2,1,0:T(8,128)(2,1)S(1)}, u32[]{:S(2)}) copy-start(bf16[8,4,32,256]{3,2,1,0:T(8,128)(2,1)S(1)} %all-to-all-done.qa) | copy-start | bytes 1572868
  36.4 7.0 %collective-permute-start.7 = (bf16[8,4,32,256]{3,2,1,0:T(8,128)(2,1)S(1)}, bf16[8,4,32,256]{3,2,1,0:T(8,128)(2,1)S(1)}, u32[]{:S(2)}, u32[]{:S(2)}) collective-permute-start(bf16[8,4,32,256]{3,2,1,0:T(8,128)(2,1)S(1)} %all-to-all-done.qa), channel_id=1, source_target_pairs={{0,4},{4,0},{1,5},{5,1},{2,6},{6,2},{3,7},{7,3},{8,12},{12,8},{9,1... | collective-permute-start | bytes 1572872 | tf_op jit(solution)/shard_map/ppermute | solution.py:152
  43.4 0.8 copy-start.4
  43.4 1.0 copy-start.5
  92.2 7.5 %collective-permute-start.8 = (f32[128,128]{1,0:T(8,128)}, f32[128,128]{1,0:T(8,128)S(1)}, u32[]{:S(2)}, u32[]{:S(2)}) collective-permute-start(f32[128,128]{1,0:T(8,128)} %get-tuple-element.9), channel_id=1, source_target_pairs={{0,4},{4,0},{1,5},{5,1},{2,6},{6,2},{3,7},{7,3},{8,12},{12,8},{9,1... | collective-permute-start | bytes 196616 | tf_op jit(solution)/shard_map/ppermute | solution.py:180
  99.7 0.6 copy-start.6

commit v3 on v2

--- a/solution.py
+++ b/solution.py
@@ -8,6 +8,7 @@
 DOC_TOK = 64
 QTOK = 32
 TOPK = 100
+MIB = 1 << 20
 LOWEST = -1e30
 SHARD = ("zh", "zl", "y", "core")
 ALL = SHARD + ("dim",)
@@ -145,6 +146,7 @@
         out_shape=jax.ShapeDtypeStruct((8, 4) + queries.shape, queries.dtype),
         in_specs=vmem(4) + anywhere(2),
         out_specs=vmem(1)[0],
+        compiler_params=pltpu.CompilerParams(vmem_limit_bytes=4 * MIB),
         name="repeat",
     )(*parts, d1, d3)
     mine = lax.all_to_all(repeated, ("zl", "y"), 0, 0, tiled=True)
@@ -167,6 +169,7 @@
             pltpu.VMEM((rows, doc_count), jnp.float32),
             pltpu.VMEM((rows, doc_count), jnp.int32),
         ],
+        compiler_params=pltpu.CompilerParams(vmem_limit_bytes=24 * MIB),
         name="score",
     )(passages, d1, d2, d3, mine, theirs, jnp.transpose(cand_ids), jnp.transpose(counts))
     pieces = lax.all_to_all(send, ("zh", "zl", "y"), 0, 0, tiled=True)
@@ -175,6 +178,7 @@
         out_shape=(jax.ShapeDtypeStruct((128, rows), jnp.float32),) * 2,
         in_specs=vmem(1),
         out_specs=tuple(vmem(2)),
+        compiler_params=pltpu.CompilerParams(vmem_limit_bytes=8 * MIB),
         name="top",
     )(pieces.reshape(-1, 8, rows))
     other = lax.ppermute(rising, "core", swap)
@@ -183,6 +187,7 @@
         out_shape=jax.ShapeDtypeStruct((TOPK, rows), jnp.float32),
         in_specs=vmem(2),
         out_specs=vmem(1)[0],
+        compiler_params=pltpu.CompilerParams(vmem_limit_bytes=2 * MIB),
         name="merge",
     )(falling, other)
     return (jnp.transpose(cand_scores), jnp.transpose(top_scores))

time: 102 us -> 93.8 us (0.920)
  Pallas kernels: 28.9 us -> 23.5 us
  local copies, waits for them, and re-layouts: 3.15 us -> 0.66 us
    unnamed x22 -> x6, local copies, waits for them, and re-layouts: 3.15 us -> 0.66 us
    pallas_call x1, Pallas kernels: 23 us -> 20.9 us  [shards(): pl.pallas_call(score_kernel, out_shape=(jax.ShapeDtypeStruct((slots, rows...]
    pallas_call x1, Pallas kernels: 2.75 us -> 1.07 us  [shards(): pl.pallas_call(top_kernel, out_shape=(jax.ShapeDtypeStruct((128, rows), j...]
where the time goes in v3:
time: 93.8 us; the launch traced here: 93.5 us
  starting transfers between devices  39.4 us (42%)
  Pallas kernels  23.5 us (25%)
  blocking collectives  21.8 us (23%)
  waiting for transfers between devices  7.47 us (8%)
    all_to_all x1, blocking collectives, shards(): pieces = lax.all_to_all(send, ('zh', 'zl', 'y'), 0, 0, tiled=True)  21.8 us
    pallas_call x1, Pallas kernels, shards(): pl.pallas_call(score_kernel, out_shape=(jax.ShapeDtypeStruct((slots, rows...  20.9 us
    ppermute x4, starting transfers between devices, shards(): parts = [lax.ppermute(queries, ('zh', 'dim'), moves[j]) for j in range(4)]  15.5 us
    ppermute x3, starting transfers between devices, shards(): lax.ppermute(passages, 'dim', [(i, (i + k) % 4) for i in range(4)])  8.44 us
    ppermute x1, starting transfers between devices, shards(): other = lax.ppermute(rising, 'core', swap)  6.46 us
    all_to_all x1, starting transfers between devices, shards(): mine = lax.all_to_all(repeated, ('zl', 'y'), 0, 0, tiled=True)  4.91 us
    ppermute x1, starting transfers between devices, shards(): theirs = lax.ppermute(mine, 'core', swap)  4.13 us
    ppermute x3, waiting for transfers between devices, shards(): lax.ppermute(passages, 'dim', [(i, (i + k) % 4) for i in range(4)])  2.86 us
  transfers between devices with their start and end apart: 10, of which 5 were waited for; matrix products, arithmetic and copies ran while one was open for 0% of the time, Pallas kernels for 0%

profile of v3, /device:TPU:1, one launch (start us, length us, event | category | flops | bytes accessed | tf_op | source)
XLA Modules:
  0.0 93.5 jit_solution(9168468718461534010)
XLA Ops:
  0.6 2.1 %collective-permute-start = (bf16[32,8192]{1,0:T(8,128)(2,1)}, bf16[32,8192]{1,0:T(8,128)(2,1)S(1)}, u32[]{:S(2)}, u32[]{:S(2)}) collective-permute-start(bf16[32,8192]{1,0:T(8,128)(2,1)} %d0.1), channel_id=1, source_target_pairs={{0,1},{1,2},{2,3},{3,0},{4,5},{5,6},{6,7},{7,4},{8,9},{9,10},{10,1... | collective-permute-start | bytes 1572872 | tf_op jit(solution)/shard_map/ppermute | solution.py:141
  2.7 1.4 %collective-permute-start.2 = (bf16[32,8192]{1,0:T(8,128)(2,1)}, bf16[32,8192]{1,0:T(8,128)(2,1)S(1)}, u32[]{:S(2)}, u32[]{:S(2)}) collective-permute-start(bf16[32,8192]{1,0:T(8,128)(2,1)} %d0.1), channel_id=1, source_target_pairs={{0,3},{1,0},{2,1},{3,2},{4,7},{5,4},{6,5},{7,6},{8,11},{9,8},{10,9... | collective-permute-start | bytes 1572872 | tf_op jit(solution)/shard_map/ppermute | solution.py:141
  4.1 3.1 %collective-permute-start.4 = (bf16[32,256]{1,0:T(8,128)(2,1)}, bf16[32,256]{1,0:T(8,128)(2,1)S(1)}, u32[]{:S(2)}, u32[]{:S(2)}) collective-permute-start(bf16[32,256]{1,0:T(8,128)(2,1)} %param.4), channel_id=1, source_target_pairs={{0,64},{1,128},{2,192},{3,0},{64,65},{65,129},{66,193},{67,1},{128... | collective-permute-start | bytes 49160 | tf_op jit(solution)/shard_map/ppermute | solution.py:140
  7.2 1.4 %collective-permute-start.3 = (bf16[32,256]{1,0:T(8,128)(2,1)}, bf16[32,256]{1,0:T(8,128)(2,1)S(1)}, u32[]{:S(2)}, u32[]{:S(2)}) collective-permute-start(bf16[32,256]{1,0:T(8,128)(2,1)} %param.4), channel_id=1, source_target_pairs={{0,0},{1,64},{2,128},{3,192},{64,1},{65,65},{66,129},{67,193},{128... | collective-permute-start | bytes 49160 | tf_op jit(solution)/shard_map/ppermute | solution.py:140
  8.6 4.9 %collective-permute-start.6 = (bf16[32,256]{1,0:T(8,128)(2,1)}, bf16[32,256]{1,0:T(8,128)(2,1)S(1)}, u32[]{:S(2)}, u32[]{:S(2)}) collective-permute-start(bf16[32,256]{1,0:T(8,128)(2,1)} %param.4), channel_id=1, source_target_pairs={{0,192},{1,0},{2,64},{3,128},{64,193},{65,1},{66,65},{67,129},{128... | collective-permute-start | bytes 49160 | tf_op jit(solution)/shard_map/ppermute | solution.py:140
  13.5 0.5 collective-permute-done.4.b
  13.9 6.2 %collective-permute-start.5 = (bf16[32,256]{1,0:T(8,128)(2,1)}, bf16[32,256]{1,0:T(8,128)(2,1)S(1)}, u32[]{:S(2)}, u32[]{:S(2)}) collective-permute-start(bf16[32,256]{1,0:T(8,128)(2,1)} %param.4), channel_id=1, source_target_pairs={{0,128},{1,192},{2,0},{3,64},{64,129},{65,193},{66,1},{67,65},{128... | collective-permute-start | bytes 49160 | tf_op jit(solution)/shard_map/ppermute | solution.py:140
  20.1 0.0 collective-permute-done.3.a
  20.1 0.0 collective-permute-done.6.d
  20.1 1.1 %collective-permute-done.5.c = bf16[32,256]{1,0:T(8,128)(2,1)S(1)} collective-permute-done((bf16[32,256]{1,0:T(8,128)(2,1)}, bf16[32,256]{1,0:T(8,128)(2,1)S(1)}, u32[]{:S(2)}, u32[]{:S(2)}) %collective-permute-start.5) | collective-permute-done | bytes 16416 | tf_op jit(solution)/shard_map/ppermute | solution.py:140
  21.2 0.0 collective-permute-done.near.d1
  21.2 0.0 collective-permute-done.2.far.d3
  21.2 0.8 repeat.1
  22.0 0.0 copy-start
  22.0 0.0 copy-start.1
  22.0 4.9 %all-to-all-start = ((bf16[8,4,32,256]{3,2,1,0:T(8,128)(2,1)}), bf16[8,4,32,256]{3,2,1,0:T(8,128)(2,1)S(1)}, u32[]{:S(2)}, u32[]{:S(2)}) async-start(bf16[8,4,32,256]{3,2,1,0:T(8,128)(2,1)} %repeat.1), calls=%async_computation | async-start | bytes 1048576 | tf_op jit(solution)/shard_map/all_to_all | solution.py:152
  26.9 0.0 copy-done
  26.9 5.0 %collective-permute-start.1 = (bf16[32,8192]{1,0:T(8,128)(2,1)S(1)}, bf16[32,8192]{1,0:T(8,128)(2,1)S(1)}, u32[]{:S(2)}, u32[]{:S(2)}) collective-permute-start(bf16[32,8192]{1,0:T(8,128)(2,1)S(1)} %copy-done), channel_id=1, source_target_pairs={{0,2},{1,3},{2,0},{3,1},{4,6},{5,7},{6,4},{7,5},{8,10},{9,11},{10,... | collective-permute-start | bytes 1572872 | tf_op jit(solution)/shard_map/ppermute | solution.py:141
  31.9 2.2 %all-to-all-done.qa = bf16[8,4,32,256]{3,2,1,0:T(8,128)(2,1)S(1)} async-done(((bf16[8,4,32,256]{3,2,1,0:T(8,128)(2,1)}), bf16[8,4,32,256]{3,2,1,0:T(8,128)(2,1)S(1)}, u32[]{:S(2)}, u32[]{:S(2)}) %all-to-all-start) | async-done | bytes 524320 | tf_op jit(solution)/shard_map/all_to_all | solution.py:152
  34.0 4.1 %collective-permute-start.7 = (bf16[8,4,32,256]{3,2,1,0:T(8,128)(2,1)S(1)}, bf16[8,4,32,256]{3,2,1,0:T(8,128)(2,1)S(1)}, u32[]{:S(2)}, u32[]{:S(2)}) collective-permute-start(bf16[8,4,32,256]{3,2,1,0:T(8,128)(2,1)S(1)} %all-to-all-done.qa), channel_id=1, source_target_pairs={{0,4},{4,0},{1,5},{5,1},{2,6},{6,2},{3,7},{7,3},{8,12},{12,8},{9,1... | collective-permute-start | bytes 1572872 | tf_op jit(solution)/shard_map/ppermute | solution.py:154
  38.2 2.9 %collective-permute-done.1.d2 = bf16[32,8192]{1,0:T(8,128)(2,1)S(1)} collective-permute-done((bf16[32,8192]{1,0:T(8,128)(2,1)S(1)}, bf16[32,8192]{1,0:T(8,128)(2,1)S(1)}, u32[]{:S(2)}, u32[]{:S(2)}) %collective-permute-start.1) | collective-permute-done | bytes 524320 | tf_op jit(solution)/shard_map/ppermute | solution.py:141
  41.0 0.0 collective-permute-done.7.qb
  41.0 0.0 copy-start.2
  41.0 0.0 copy-done.1
  41.0 0.6 copy-done.2
  41.7 20.9 %score.1 = (f32[32,128]{1,0:T(8,128)}, f32[32,32,128]{2,1,0:T(8,128)S(1)}) custom-call(bf16[32,8192]{1,0:T(8,128)(2,1)S(1)} %copy-done, bf16[32,8192]{1,0:T(8,128)(2,1)S(1)} %collective-permute-done.near.d1, bf16[32,8192]{1,0:T(8,128)(2,1)S(1)} %collective-permute-done.1.d2, bf16[32,8192]{1,0:T(8,128)(2,1)S(1)} %collective-permute-done.2.far.d3, ...), custom_call_target="tpu_custom_call" | custom-call | tf_op jit(solution)/shard_map/score/pallas_call | solution.py:158
  62.6 21.8 %all_to_all.10 = f32[32,32,128]{2,1,0:T(8,128)S(1)} all-to-all(f32[32,32,128]{2,1,0:T(8,128)S(1)} %get-tuple-element.7), channel_id=1, replica_groups=mesh['zh'=4,'zl'=2,'y'=4,'core'=2,'dim'=4] {'zh','zl','y'}, dimensions={0} | all-to-all | bytes 1048576 | tf_op jit(solution)/shard_map/all_to_all | solution.py:175
  84.4 1.1 %top.1 = (f32[128,128]{1,0:T(8,128)S(1)}, f32[128,128]{1,0:T(8,128)S(1)}) custom-call(f32[128,8,128]{2,1,0:T(8,128)S(1)} %bitcast.5), custom_call_target="tpu_custom_call" | custom-call | tf_op jit(solution)/shard_map/top/pallas_call | solution.py:176
  85.5 6.5 %collective-permute-start.8 = (f32[128,128]{1,0:T(8,128)S(1)}, f32[128,128]{1,0:T(8,128)S(1)}, u32[]{:S(2)}, u32[]{:S(2)}) collective-permute-start(f32[128,128]{1,0:T(8,128)S(1)} %get-tuple-element.9), channel_id=1, source_target_pairs={{0,4},{4,0},{1,5},{5,1},{2,6},{6,2},{3,7},{7,3},{8,12},{12,8},{9,1... | collective-permute-start | bytes 196616 | tf_op jit(solution)/shard_map/ppermute | solution.py:184
  91.9 0.9 collective-permute-done.8.rising
  92.8 0.7 merge.1
Async XLA Ops:
  0.6 20.5 %collective-permute-start = (bf16[32,8192]{1,0:T(8,128)(2,1)}, bf16[32,8192]{1,0:T(8,128)(2,1)S(1)}, u32[]{:S(2)}, u32[]{:S(2)}) collective-permute-start(bf16[32,8192]{1,0:T(8,128)(2,1)} %d0.1), channel_id=1, source_target_pairs={{0,1},{1,2},{2,3},{3,0},{4,5},{5,6},{6,7},{7,4},{8,9},{9,10},{10,1... | collective-permute-start | bytes 1572872 | tf_op jit(solution)/shard_map/ppermute | solution.py:141
  2.7 18.4 %collective-permute-start.2 = (bf16[32,8192]{1,0:T(8,128)(2,1)}, bf16[32,8192]{1,0:T(8,128)(2,1)S(1)}, u32[]{:S(2)}, u32[]{:S(2)}) collective-permute-start(bf16[32,8192]{1,0:T(8,128)(2,1)} %d0.1), channel_id=1, source_target_pairs={{0,3},{1,0},{2,1},{3,2},{4,7},{5,4},{6,5},{7,6},{8,11},{9,8},{10,9... | collective-permute-start | bytes 1572872 | tf_op jit(solution)/shard_map/ppermute | solution.py:141
  4.1 9.8 %collective-permute-start.4 = (bf16[32,256]{1,0:T(8,128)(2,1)}, bf16[32,256]{1,0:T(8,128)(2,1)S(1)}, u32[]{:S(2)}, u32[]{:S(2)}) collective-permute-start(bf16[32,256]{1,0:T(8,128)(2,1)} %param.4), channel_id=1, source_target_pairs={{0,64},{1,128},{2,192},{3,0},{64,65},{65,129},{66,193},{67,1},{128... | collective-permute-start | bytes 49160 | tf_op jit(solution)/shard_map/ppermute | solution.py:140
  7.2 12.9 %collective-permute-start.3 = (bf16[32,256]{1,0:T(8,128)(2,1)}, bf16[32,256]{1,0:T(8,128)(2,1)S(1)}, u32[]{:S(2)}, u32[]{:S(2)}) collective-permute-start(bf16[32,256]{1,0:T(8,128)(2,1)} %param.4), channel_id=1, source_target_pairs={{0,0},{1,64},{2,128},{3,192},{64,1},{65,65},{66,129},{67,193},{128... | collective-permute-start | bytes 49160 | tf_op jit(solution)/shard_map/ppermute | solution.py:140
  8.6 11.5 %collective-permute-start.6 = (bf16[32,256]{1,0:T(8,128)(2,1)}, bf16[32,256]{1,0:T(8,128)(2,1)S(1)}, u32[]{:S(2)}, u32[]{:S(2)}) collective-permute-start(bf16[32,256]{1,0:T(8,128)(2,1)} %param.4), channel_id=1, source_target_pairs={{0,192},{1,0},{2,64},{3,128},{64,193},{65,1},{66,65},{67,129},{128... | collective-permute-start | bytes 49160 | tf_op jit(solution)/shard_map/ppermute | solution.py:140
  13.9 7.2 %collective-permute-start.5 = (bf16[32,256]{1,0:T(8,128)(2,1)}, bf16[32,256]{1,0:T(8,128)(2,1)S(1)}, u32[]{:S(2)}, u32[]{:S(2)}) collective-permute-start(bf16[32,256]{1,0:T(8,128)(2,1)} %param.4), channel_id=1, source_target_pairs={{0,128},{1,192},{2,0},{3,64},{64,129},{65,193},{66,1},{67,65},{128... | collective-permute-start | bytes 49160 | tf_op jit(solution)/shard_map/ppermute | solution.py:140
  22.0 4.9 %copy-start = (bf16[32,8192]{1,0:T(8,128)(2,1)S(1)}, bf16[32,8192]{1,0:T(8,128)(2,1)}, u32[]{:S(2)}) copy-start(bf16[32,8192]{1,0:T(8,128)(2,1)} %d0.1) | copy-start | bytes 1572868
  22.0 19.0 %copy-start.1 = (s32[128,32]{0,1:T(8,128)S(1)}, s32[128,32]{0,1:T(8,128)}, u32[]{:S(2)}) copy-start(s32[128,32]{0,1:T(8,128)} %param.6) | copy-start | bytes 49156
  22.0 12.0 %all-to-all-start = ((bf16[8,4,32,256]{3,2,1,0:T(8,128)(2,1)}), bf16[8,4,32,256]{3,2,1,0:T(8,128)(2,1)S(1)}, u32[]{:S(2)}, u32[]{:S(2)}) async-start(bf16[8,4,32,256]{3,2,1,0:T(8,128)(2,1)} %repeat.1), calls=%async_computation | async-start | bytes 1048576 | tf_op jit(solution)/shard_map/all_to_all | solution.py:152
  26.9 14.1 %collective-permute-start.1 = (bf16[32,8192]{1,0:T(8,128)(2,1)S(1)}, bf16[32,8192]{1,0:T(8,128)(2,1)S(1)}, u32[]{:S(2)}, u32[]{:S(2)}) collective-permute-start(bf16[32,8192]{1,0:T(8,128)(2,1)S(1)} %copy-done), channel_id=1, source_target_pairs={{0,2},{1,3},{2,0},{3,1},{4,6},{5,7},{6,4},{7,5},{8,10},{9,11},{10,... | collective-permute-start | bytes 1572872 | tf_op jit(solution)/shard_map/ppermute | solution.py:141
  34.0 7.0 %collective-permute-start.7 = (bf16[8,4,32,256]{3,2,1,0:T(8,128)(2,1)S(1)}, bf16[8,4,32,256]{3,2,1,0:T(8,128)(2,1)S(1)}, u32[]{:S(2)}, u32[]{:S(2)}) collective-permute-start(bf16[8,4,32,256]{3,2,1,0:T(8,128)(2,1)S(1)} %all-to-all-done.qa), channel_id=1, source_target_pairs={{0,4},{4,0},{1,5},{5,1},{2,6},{6,2},{3,7},{7,3},{8,12},{12,8},{9,1... | collective-permute-start | bytes 1572872 | tf_op jit(solution)/shard_map/ppermute | solution.py:154
  41.0 0.7 copy-start.2
  85.5 7.4 %collective-permute-start.8 = (f32[128,128]{1,0:T(8,128)S(1)}, f32[128,128]{1,0:T(8,128)S(1)}, u32[]{:S(2)}, u32[]{:S(2)}) collective-permute-start(f32[128,128]{1,0:T(8,128)S(1)} %get-tuple-element.9), channel_id=1, source_target_pairs={{0,4},{4,0},{1,5},{5,1},{2,6},{6,2},{3,7},{7,3},{8,12},{12,8},{9,1... | collective-permute-start | bytes 196616 | tf_op jit(solution)/shard_map/ppermute | solution.py:184

commit v4 on v3

--- a/solution.py
+++ b/solution.py
@@ -14,21 +14,24 @@
 ALL = SHARD + ("dim",)
 
 
-def repeat_kernel(a, b, c, d, near, far, out):
-    for i in range(out.shape[0]):
-        for j, part in enumerate((a, b, c, d)):
-            out[i, j] = part[...]
-
-
-def score_kernel(d0, d1, d2, d3, qa, qb, ids, counts, cand, send, docs, best, kept, picks):
+def hold_kernel(q, near, far, out):
+    pass
+
+
+def prepare_kernel(ids, counts, picks, live):
+    slots, rows = ids.shape
+    picks[...] = jnp.transpose(jnp.concatenate([ids[...], jnp.zeros((picks.shape[1] - slots, rows), jnp.int32)], axis=0))
+    live[...] = (lax.broadcasted_iota(jnp.int32, live.shape, 0) < counts[...]).astype(jnp.int32)
+
+
+def score_kernel(d0, d1, d2, d3, qa, qb, picks, live, cand, send, docs, best, kept):
     core = lax.axis_index("core")
     turn = lax.rem(lax.axis_index("zh") - lax.axis_index("dim") + 4, 4)
     docs_n = best.shape[0]
     sources = qa.shape[0]
-    slots = ids.shape[0]
+    slots = live.shape[0]
     tile = 512
     per = tile // DOC_TOK
-    picks[...] = jnp.transpose(jnp.concatenate([ids[...], jnp.zeros((docs_n - slots, ids.shape[1]), jnp.int32)], axis=0))
 
     def one(source, q, side, first):
         weights = jnp.concatenate([q[source, lax.rem(turn + k, 4)] for k in range(4)], axis=0)
@@ -47,21 +50,22 @@
         rows = pl.ds(pl.multiple_of((source * 2 + side) * queries, queries), queries)
         kept[rows, :] = jnp.take_along_axis(mean, picks[rows, :], axis=1)
 
-    one(0, qa, core, True)
-    one(0, qb, 1 - core, False)
-
-    def pair(source, carry):
-        one(source, qa, core, False)
-        one(source, qb, 1 - core, False)
+    def two(source, first):
+        for i in range(2):
+            one(source + i, qa, core, first and i == 0)
+            one(source + i, qb, 1 - core, False)
+
+    def step(i, carry):
+        two(2 * i, False)
         return carry
 
-    lax.fori_loop(1, sources, pair, 0)
+    two(0, True)
+    lax.fori_loop(1, sources // 2, step, 0)
     scores = jnp.transpose(kept[...])[:slots, :]
-    live = lax.broadcasted_iota(jnp.int32, scores.shape, 0) < counts[...]
-    cand[...] = jnp.where(live, scores, 0.0)
-    masked = jnp.where(live, scores, LOWEST)
-    for i in range(send.shape[0]):
-        send[i] = masked
+    alive = live[...] > 0
+    cand[...] = jnp.where(alive, scores, 0.0)
+    masked = jnp.where(alive, scores, LOWEST)
+    send[...] = masked
 
 
 def exchange(values, i, j):
@@ -141,25 +145,39 @@
     round_dim = lambda k: lax.ppermute(passages, "dim", [(i, (i + k) % 4) for i in range(4)])
     d1, d3 = round_dim(1), round_dim(3)
     d2 = round_dim(2)
-    repeated = pl.pallas_call(
-        repeat_kernel,
-        out_shape=jax.ShapeDtypeStruct((8, 4) + queries.shape, queries.dtype),
-        in_specs=vmem(4) + anywhere(2),
-        out_specs=vmem(1)[0],
-        compiler_params=pltpu.CompilerParams(vmem_limit_bytes=4 * MIB),
-        name="repeat",
-    )(*parts, d1, d3)
+    parts = jnp.stack(parts)
+    parts = pl.pallas_call(
+        hold_kernel,
+        out_shape=jax.ShapeDtypeStruct(parts.shape, parts.dtype),
+        in_specs=anywhere(3),
+        out_specs=anywhere(1)[0],
+        input_output_aliases={0: 0},
+        compiler_params=pltpu.CompilerParams(vmem_limit_bytes=MIB),
+        name="hold",
+    )(parts, d1, d3)
+    repeated = jnp.broadcast_to(parts[None], (8,) + parts.shape)
     mine = lax.all_to_all(repeated, ("zl", "y"), 0, 0, tiled=True)
     swap = [(0, 1), (1, 0)]
     theirs = lax.ppermute(mine, "core", swap)
     width, doc_cols = 4 * passages.shape[0], passages.shape[1]
     rows, slots = cand_ids.shape
     doc_count = doc_cols // DOC_TOK
+    picks, live = pl.pallas_call(
+        prepare_kernel,
+        out_shape=(
+            jax.ShapeDtypeStruct((rows, doc_count), jnp.int32),
+            jax.ShapeDtypeStruct((slots, rows), jnp.int32),
+        ),
+        in_specs=vmem(2),
+        out_specs=tuple(vmem(2)),
+        compiler_params=pltpu.CompilerParams(vmem_limit_bytes=MIB),
+        name="prepare",
+    )(jnp.transpose(cand_ids), jnp.transpose(counts))
     cand_scores, send = pl.pallas_call(
         score_kernel,
         out_shape=(
             jax.ShapeDtypeStruct((slots, rows), jnp.float32),
-            jax.ShapeDtypeStruct((32, slots, rows), jnp.float32),
+            jax.ShapeDtypeStruct((slots, rows), jnp.float32),
         ),
         in_specs=vmem(8),
         out_specs=tuple(vmem(2)),
@@ -167,12 +185,11 @@
             pltpu.VMEM((doc_cols, width), passages.dtype),
             pltpu.VMEM((doc_count, queries.shape[1]), jnp.float32),
             pltpu.VMEM((rows, doc_count), jnp.float32),
-            pltpu.VMEM((rows, doc_count), jnp.int32),
         ],
         compiler_params=pltpu.CompilerParams(vmem_limit_bytes=24 * MIB),
         name="score",
-    )(passages, d1, d2, d3, mine, theirs, jnp.transpose(cand_ids), jnp.transpose(counts))
-    pieces = lax.all_to_all(send, ("zh", "zl", "y"), 0, 0, tiled=True)
+    )(passages, d1, d2, d3, mine, theirs, picks, live)
+    pieces = lax.all_to_all(jnp.broadcast_to(send[None], (32,) + send.shape), ("zh", "zl", "y"), 0, 0, tiled=True)
     falling, rising = pl.pallas_call(
         top_kernel,
         out_shape=(jax.ShapeDtypeStruct((128, rows), jnp.float32),) * 2,

time: 93.8 us -> 91.9 us (0.980)
  Pallas kernels: 23.5 us -> 21.4 us
    pallas_call x1, Pallas kernels: 20.9 us -> 19.6 us  [shards(): pl.pallas_call(score_kernel, out_shape=(jax.ShapeDtypeStruct((slots, rows...]
where the time goes in v4:
time: 91.9 us; the launch traced here: 91.6 us
  starting transfers between devices  39.4 us (43%)
  blocking collectives  21.8 us (24%)
  Pallas kernels  21.4 us (23%)
  waiting for transfers between devices  6.71 us (7%)
  local copies, waits for them, and re-layouts  1.56 us (2%)
    all_to_all x1, blocking collectives, shards(): lax.all_to_all(jnp.broadcast_to(send[None], (32,) + send.shape), ('zh', '...  21.8 us
    pallas_call x1, Pallas kernels, shards(): pl.pallas_call(score_kernel, out_shape=(jax.ShapeDtypeStruct((slots, rows...  19.6 us
    ppermute x4, starting transfers between devices, shards(): parts = [lax.ppermute(queries, ('zh', 'dim'), moves[j]) for j in range(4)]  15.5 us
    ppermute x3, starting transfers between devices, shards(): lax.ppermute(passages, 'dim', [(i, (i + k) % 4) for i in range(4)])  8.44 us
    ppermute x1, starting transfers between devices, shards(): other = lax.ppermute(rising, 'core', swap)  6.45 us
    all_to_all x1, starting transfers between devices, shards(): mine = lax.all_to_all(repeated, ('zl', 'y'), 0, 0, tiled=True)  4.91 us
    ppermute x1, starting transfers between devices, shards(): theirs = lax.ppermute(mine, 'core', swap)  4.13 us
    all_to_all x1, waiting for transfers between devices, shards(): mine = lax.all_to_all(repeated, ('zl', 'y'), 0, 0, tiled=True)  2.17 us
  transfers between devices with their start and end apart: 10, of which 5 were waited for; matrix products, arithmetic and copies ran while one was open for 0% of the time, Pallas kernels for 0%

profile of v4, /device:TPU:1, one launch (start us, length us, event | category | flops | bytes accessed | tf_op | source)
XLA Modules:
  0.0 91.6 jit_solution(14197052037722139466)
XLA Ops:
  0.6 2.1 %collective-permute-start = (bf16[32,8192]{1,0:T(8,128)(2,1)}, bf16[32,8192]{1,0:T(8,128)(2,1)S(1)}, u32[]{:S(2)}, u32[]{:S(2)}) collective-permute-start(bf16[32,8192]{1,0:T(8,128)(2,1)} %d0.1), channel_id=1, source_target_pairs={{0,1},{1,2},{2,3},{3,0},{4,5},{5,6},{6,7},{7,4},{8,9},{9,10},{10,1... | collective-permute-start | bytes 1572872 | tf_op jit(solution)/shard_map/ppermute | solution.py:145
  2.7 1.4 %collective-permute-start.2 = (bf16[32,8192]{1,0:T(8,128)(2,1)}, bf16[32,8192]{1,0:T(8,128)(2,1)S(1)}, u32[]{:S(2)}, u32[]{:S(2)}) collective-permute-start(bf16[32,8192]{1,0:T(8,128)(2,1)} %d0.1), channel_id=1, source_target_pairs={{0,3},{1,0},{2,1},{3,2},{4,7},{5,4},{6,5},{7,6},{8,11},{9,8},{10,9... | collective-permute-start | bytes 1572872 | tf_op jit(solution)/shard_map/ppermute | solution.py:145
  4.1 3.1 %collective-permute-start.4 = (bf16[32,256]{1,0:T(8,128)(2,1)}, bf16[32,256]{1,0:T(8,128)(2,1)S(1)}, u32[]{:S(2)}, u32[]{:S(2)}) collective-permute-start(bf16[32,256]{1,0:T(8,128)(2,1)} %param.4), channel_id=1, source_target_pairs={{0,64},{1,128},{2,192},{3,0},{64,65},{65,129},{66,193},{67,1},{128... | collective-permute-start | bytes 49160 | tf_op jit(solution)/shard_map/ppermute | solution.py:144
  7.2 1.4 %collective-permute-start.3 = (bf16[32,256]{1,0:T(8,128)(2,1)}, bf16[32,256]{1,0:T(8,128)(2,1)S(1)}, u32[]{:S(2)}, u32[]{:S(2)}) collective-permute-start(bf16[32,256]{1,0:T(8,128)(2,1)} %param.4), channel_id=1, source_target_pairs={{0,0},{1,64},{2,128},{3,192},{64,1},{65,65},{66,129},{67,193},{128... | collective-permute-start | bytes 49160 | tf_op jit(solution)/shard_map/ppermute | solution.py:144
  8.6 4.9 %collective-permute-start.6 = (bf16[32,256]{1,0:T(8,128)(2,1)}, bf16[32,256]{1,0:T(8,128)(2,1)S(1)}, u32[]{:S(2)}, u32[]{:S(2)}) collective-permute-start(bf16[32,256]{1,0:T(8,128)(2,1)} %param.4), channel_id=1, source_target_pairs={{0,192},{1,0},{2,64},{3,128},{64,193},{65,1},{66,65},{67,129},{128... | collective-permute-start | bytes 49160 | tf_op jit(solution)/shard_map/ppermute | solution.py:144
  13.5 0.5 collective-permute-done.4
  13.9 6.2 %collective-permute-start.5 = (bf16[32,256]{1,0:T(8,128)(2,1)}, bf16[32,256]{1,0:T(8,128)(2,1)S(1)}, u32[]{:S(2)}, u32[]{:S(2)}) collective-permute-start(bf16[32,256]{1,0:T(8,128)(2,1)} %param.4), channel_id=1, source_target_pairs={{0,128},{1,192},{2,0},{3,64},{64,129},{65,193},{66,1},{67,65},{128... | collective-permute-start | bytes 49160 | tf_op jit(solution)/shard_map/ppermute | solution.py:144
  20.1 0.0 collective-permute-done.3
  20.1 0.0 collective-permute-done.6
  20.1 1.1 %collective-permute-done.5 = bf16[32,256]{1,0:T(8,128)(2,1)S(1)} collective-permute-done((bf16[32,256]{1,0:T(8,128)(2,1)}, bf16[32,256]{1,0:T(8,128)(2,1)S(1)}, u32[]{:S(2)}, u32[]{:S(2)}) %collective-permute-start.5) | collective-permute-done | bytes 16416 | tf_op jit(solution)/shard_map/ppermute | solution.py:144
  21.2 0.0 collective-permute-done.near.d1
  21.2 0.0 collective-permute-done.2.far.d3
  21.2 0.9 broadcast_in_dim.4
  22.1 0.0 copy-start
  22.1 0.0 copy-start.1
  22.1 4.9 %all-to-all-start = ((bf16[8,4,32,256]{3,2,1,0:T(8,128)(2,1)}), bf16[8,4,32,256]{3,2,1,0:T(8,128)(2,1)S(1)}, u32[]{:S(2)}, u32[]{:S(2)}) async-start(bf16[8,4,32,256]{3,2,1,0:T(8,128)(2,1)} %broadcast_in_dim.4), calls=%async_computation | async-start | bytes 1048576 | tf_op jit(solution)/shard_map/all_to_all | solution.py:159
  27.0 0.0 copy-done
  27.0 5.0 %collective-permute-start.1 = (bf16[32,8192]{1,0:T(8,128)(2,1)S(1)}, bf16[32,8192]{1,0:T(8,128)(2,1)S(1)}, u32[]{:S(2)}, u32[]{:S(2)}) collective-permute-start(bf16[32,8192]{1,0:T(8,128)(2,1)S(1)} %copy-done), channel_id=1, source_target_pairs={{0,2},{1,3},{2,0},{3,1},{4,6},{5,7},{6,4},{7,5},{8,10},{9,11},{10,... | collective-permute-start | bytes 1572872 | tf_op jit(solution)/shard_map/ppermute | solution.py:145
  31.9 2.2 %all-to-all-done.qa = bf16[8,4,32,256]{3,2,1,0:T(8,128)(2,1)S(1)} async-done(((bf16[8,4,32,256]{3,2,1,0:T(8,128)(2,1)}), bf16[8,4,32,256]{3,2,1,0:T(8,128)(2,1)S(1)}, u32[]{:S(2)}, u32[]{:S(2)}) %all-to-all-start) | async-done | bytes 524320 | tf_op jit(solution)/shard_map/all_to_all | solution.py:159
  34.1 4.1 %collective-permute-start.7 = (bf16[8,4,32,256]{3,2,1,0:T(8,128)(2,1)S(1)}, bf16[8,4,32,256]{3,2,1,0:T(8,128)(2,1)S(1)}, u32[]{:S(2)}, u32[]{:S(2)}) collective-permute-start(bf16[8,4,32,256]{3,2,1,0:T(8,128)(2,1)S(1)} %all-to-all-done.qa), channel_id=1, source_target_pairs={{0,4},{4,0},{1,5},{5,1},{2,6},{6,2},{3,7},{7,3},{8,12},{12,8},{9,1... | collective-permute-start | bytes 1572872 | tf_op jit(solution)/shard_map/ppermute | solution.py:161
  38.2 0.0 copy-start.2
  38.2 0.0 copy-done.1
  38.2 0.7 copy-done.2
  38.9 0.1 prepare.1
  39.0 2.1 %collective-permute-done.1.d2 = bf16[32,8192]{1,0:T(8,128)(2,1)S(1)} collective-permute-done((bf16[32,8192]{1,0:T(8,128)(2,1)S(1)}, bf16[32,8192]{1,0:T(8,128)(2,1)S(1)}, u32[]{:S(2)}, u32[]{:S(2)}) %collective-permute-start.1) | collective-permute-done | bytes 524320 | tf_op jit(solution)/shard_map/ppermute | solution.py:145
  41.1 0.0 collective-permute-done.7.qb
  41.1 19.6 %score.1 = (f32[32,128]{1,0:T(8,128)}, f32[32,128]{1,0:T(8,128)S(1)}) custom-call(bf16[32,8192]{1,0:T(8,128)(2,1)S(1)} %copy-done, bf16[32,8192]{1,0:T(8,128)(2,1)S(1)} %collective-permute-done.near.d1, bf16[32,8192]{1,0:T(8,128)(2,1)S(1)} %collective-permute-done.1.d2, bf16[32,8192]{1,0:T(8,128)(2,1)S(1)} %collective-permute-done.2.far.d3, ...), custom_call_target="tpu_custom_call" | custom-call | tf_op jit(solution)/shard_map/score/pallas_call | solution.py:176
  60.7 21.8 %all_to_all.10 = f32[32,32,128]{2,1,0:T(8,128)S(1)} all-to-all(f32[32,32,128]{2,1,0:T(8,128)S(1)} %broadcast_in_dim.5), channel_id=1, replica_groups=mesh['zh'=4,'zl'=2,'y'=4,'core'=2,'dim'=4] {'zh','zl','y'}, dimensions={0} | all-to-all | bytes 1048576 | tf_op jit(solution)/shard_map/all_to_all | solution.py:192
  82.5 1.1 %top.1 = (f32[128,128]{1,0:T(8,128)S(1)}, f32[128,128]{1,0:T(8,128)S(1)}) custom-call(f32[128,8,128]{2,1,0:T(8,128)S(1)} %bitcast.9), custom_call_target="tpu_custom_call" | custom-call | tf_op jit(solution)/shard_map/top/pallas_call | solution.py:193
  83.6 6.5 %collective-permute-start.8 = (f32[128,128]{1,0:T(8,128)S(1)}, f32[128,128]{1,0:T(8,128)S(1)}, u32[]{:S(2)}, u32[]{:S(2)}) collective-permute-start(f32[128,128]{1,0:T(8,128)S(1)} %get-tuple-element.13), channel_id=1, source_target_pairs={{0,4},{4,0},{1,5},{5,1},{2,6},{6,2},{3,7},{7,3},{8,12},{12,8},{9,1... | collective-permute-start | bytes 196616 | tf_op jit(solution)/shard_map/ppermute | solution.py:201
  90.0 0.9 collective-permute-done.8.rising
  91.0 0.7 merge.1
  (3 shorter events, 0.1 us)
Async XLA Ops:
  0.6 20.6 %collective-permute-start = (bf16[32,8192]{1,0:T(8,128)(2,1)}, bf16[32,8192]{1,0:T(8,128)(2,1)S(1)}, u32[]{:S(2)}, u32[]{:S(2)}) collective-permute-start(bf16[32,8192]{1,0:T(8,128)(2,1)} %d0.1), channel_id=1, source_target_pairs={{0,1},{1,2},{2,3},{3,0},{4,5},{5,6},{6,7},{7,4},{8,9},{9,10},{10,1... | collective-permute-start | bytes 1572872 | tf_op jit(solution)/shard_map/ppermute | solution.py:145
  2.7 18.5 %collective-permute-start.2 = (bf16[32,8192]{1,0:T(8,128)(2,1)}, bf16[32,8192]{1,0:T(8,128)(2,1)S(1)}, u32[]{:S(2)}, u32[]{:S(2)}) collective-permute-start(bf16[32,8192]{1,0:T(8,128)(2,1)} %d0.1), channel_id=1, source_target_pairs={{0,3},{1,0},{2,1},{3,2},{4,7},{5,4},{6,5},{7,6},{8,11},{9,8},{10,9... | collective-permute-start | bytes 1572872 | tf_op jit(solution)/shard_map/ppermute | solution.py:145
  4.1 9.8 %collective-permute-start.4 = (bf16[32,256]{1,0:T(8,128)(2,1)}, bf16[32,256]{1,0:T(8,128)(2,1)S(1)}, u32[]{:S(2)}, u32[]{:S(2)}) collective-permute-start(bf16[32,256]{1,0:T(8,128)(2,1)} %param.4), channel_id=1, source_target_pairs={{0,64},{1,128},{2,192},{3,0},{64,65},{65,129},{66,193},{67,1},{128... | collective-permute-start | bytes 49160 | tf_op jit(solution)/shard_map/ppermute | solution.py:144
  7.2 12.9 %collective-permute-start.3 = (bf16[32,256]{1,0:T(8,128)(2,1)}, bf16[32,256]{1,0:T(8,128)(2,1)S(1)}, u32[]{:S(2)}, u32[]{:S(2)}) collective-permute-start(bf16[32,256]{1,0:T(8,128)(2,1)} %param.4), channel_id=1, source_target_pairs={{0,0},{1,64},{2,128},{3,192},{64,1},{65,65},{66,129},{67,193},{128... | collective-permute-start | bytes 49160 | tf_op jit(solution)/shard_map/ppermute | solution.py:144
  8.6 11.5 %collective-permute-start.6 = (bf16[32,256]{1,0:T(8,128)(2,1)}, bf16[32,256]{1,0:T(8,128)(2,1)S(1)}, u32[]{:S(2)}, u32[]{:S(2)}) collective-permute-start(bf16[32,256]{1,0:T(8,128)(2,1)} %param.4), channel_id=1, source_target_pairs={{0,192},{1,0},{2,64},{3,128},{64,193},{65,1},{66,65},{67,129},{128... | collective-permute-start | bytes 49160 | tf_op jit(solution)/shard_map/ppermute | solution.py:144
  13.9 7.2 %collective-permute-start.5 = (bf16[32,256]{1,0:T(8,128)(2,1)}, bf16[32,256]{1,0:T(8,128)(2,1)S(1)}, u32[]{:S(2)}, u32[]{:S(2)}) collective-permute-start(bf16[32,256]{1,0:T(8,128)(2,1)} %param.4), channel_id=1, source_target_pairs={{0,128},{1,192},{2,0},{3,64},{64,129},{65,193},{66,1},{67,65},{128... | collective-permute-start | bytes 49160 | tf_op jit(solution)/shard_map/ppermute | solution.py:144
  22.1 4.9 %copy-start = (bf16[32,8192]{1,0:T(8,128)(2,1)S(1)}, bf16[32,8192]{1,0:T(8,128)(2,1)}, u32[]{:S(2)}) copy-start(bf16[32,8192]{1,0:T(8,128)(2,1)} %d0.1) | copy-start | bytes 1572868
  22.1 16.2 %copy-start.1 = (s32[128,32]{0,1:T(8,128)S(1)}, s32[128,32]{0,1:T(8,128)}, u32[]{:S(2)}) copy-start(s32[128,32]{0,1:T(8,128)} %param.6) | copy-start | bytes 49156
  22.1 12.0 %all-to-all-start = ((bf16[8,4,32,256]{3,2,1,0:T(8,128)(2,1)}), bf16[8,4,32,256]{3,2,1,0:T(8,128)(2,1)S(1)}, u32[]{:S(2)}, u32[]{:S(2)}) async-start(bf16[8,4,32,256]{3,2,1,0:T(8,128)(2,1)} %broadcast_in_dim.4), calls=%async_computation | async-start | bytes 1048576 | tf_op jit(solution)/shard_map/all_to_all | solution.py:159
  27.0 14.1 %collective-permute-start.1 = (bf16[32,8192]{1,0:T(8,128)(2,1)S(1)}, bf16[32,8192]{1,0:T(8,128)(2,1)S(1)}, u32[]{:S(2)}, u32[]{:S(2)}) collective-permute-start(bf16[32,8192]{1,0:T(8,128)(2,1)S(1)} %copy-done), channel_id=1, source_target_pairs={{0,2},{1,3},{2,0},{3,1},{4,6},{5,7},{6,4},{7,5},{8,10},{9,11},{10,... | collective-permute-start | bytes 1572872 | tf_op jit(solution)/shard_map/ppermute | solution.py:145
  34.1 7.0 %collective-permute-start.7 = (bf16[8,4,32,256]{3,2,1,0:T(8,128)(2,1)S(1)}, bf16[8,4,32,256]{3,2,1,0:T(8,128)(2,1)S(1)}, u32[]{:S(2)}, u32[]{:S(2)}) collective-permute-start(bf16[8,4,32,256]{3,2,1,0:T(8,128)(2,1)S(1)} %all-to-all-done.qa), channel_id=1, source_target_pairs={{0,4},{4,0},{1,5},{5,1},{2,6},{6,2},{3,7},{7,3},{8,12},{12,8},{9,1... | collective-permute-start | bytes 1572872 | tf_op jit(solution)/shard_map/ppermute | solution.py:161
  38.2 0.7 copy-start.2
  83.6 7.4 %collective-permute-start.8 = (f32[128,128]{1,0:T(8,128)S(1)}, f32[128,128]{1,0:T(8,128)S(1)}, u32[]{:S(2)}, u32[]{:S(2)}) collective-permute-start(f32[128,128]{1,0:T(8,128)S(1)} %get-tuple-element.13), channel_id=1, source_target_pairs={{0,4},{4,0},{1,5},{5,1},{2,6},{6,2},{3,7},{7,3},{8,12},{12,8},{9,1... | collective-permute-start | bytes 196616 | tf_op jit(solution)/shard_map/ppermute | solution.py:201

commit v5 on v4

--- a/solution.py
+++ b/solution.py
@@ -14,7 +14,7 @@
 ALL = SHARD + ("dim",)
 
 
-def hold_kernel(q, near, far, out):
+def hold_kernel(*refs):
     pass
 
 
@@ -24,7 +24,7 @@
     live[...] = (lax.broadcasted_iota(jnp.int32, live.shape, 0) < counts[...]).astype(jnp.int32)
 
 
-def score_kernel(d0, d1, d2, d3, qa, qb, picks, live, cand, send, docs, best, kept):
+def score_kernel(d0, d1, d2a, d2b, d3, qa, qb, picks, live, cand, send, docs, best, kept):
     core = lax.axis_index("core")
     turn = lax.rem(lax.axis_index("zh") - lax.axis_index("dim") + 4, 4)
     docs_n = best.shape[0]
@@ -38,7 +38,10 @@
         for t in range(docs_n // per):
             span = slice(t * tile, (t + 1) * tile)
             if first:
-                block = jnp.transpose(jnp.concatenate([d[:, span] for d in (d0, d1, d2, d3)], axis=0))
+                half = d2a.shape[1]
+                inner = slice(t * tile % half, t * tile % half + tile)
+                two = (d2a if t * tile < half else d2b)[:, inner]
+                block = jnp.transpose(jnp.concatenate([d0[:, span], d1[:, span], two, d3[:, span]], axis=0))
                 docs[span, :] = block
             else:
                 block = docs[span, :]
@@ -65,7 +68,12 @@
     alive = live[...] > 0
     cand[...] = jnp.where(alive, scores, 0.0)
     masked = jnp.where(alive, scores, LOWEST)
-    send[...] = masked
+    half = masked.shape[1] // 2
+    upper, lower = slice(0, slots // 2), slice(slots // 2, slots)
+    turned = pltpu.roll(masked, half, 1)
+    left = lax.broadcasted_iota(jnp.int32, (slots // 2, masked.shape[1]), 1) < half
+    send[0] = jnp.where(left, masked[upper, :], turned[lower, :])
+    send[1] = jnp.where(left, turned[upper, :], masked[lower, :])
 
 
 def exchange(values, i, j):
@@ -106,6 +114,9 @@
     count = pieces.shape[0]
     values = [pieces[i] for i in range(count)]
     odd_even_sort(values, 0, count)
+    values = values + [pltpu.roll(v, 64, 1) for v in values[::-1]]
+    count = len(values)
+    clean(values, 0, count)
     for shift in (4, 2, 1):
         other = [pltpu.roll(v, shift, 0) for v in values]
         values = [jnp.maximum(values[i], other[count - 1 - i]) for i in range(count)]
@@ -130,6 +141,12 @@
     out[...] = jnp.concatenate(values, axis=0)[: out.shape[0], :]
 
 
+def join_kernel(mine, theirs, out):
+    side = lax.broadcasted_iota(jnp.int32, out.shape, 1) // (out.shape[1] // 2)
+    rows = out.shape[0]
+    out[...] = jnp.where(side == lax.axis_index("zl"), mine[:rows, :], theirs[:rows, :])
+
+
 def vmem(n):
     return [pl.BlockSpec(memory_space=pltpu.VMEM)] * n
 
@@ -138,27 +155,19 @@
     return [pl.BlockSpec(memory_space=pl.ANY)] * n
 
 
-def shards(queries, passages, cand_ids, counts):
-    flat = lambda zh, x: zh * 4 + x
-    moves = [[(flat(zh, x), flat((x + j) % 4, zh)) for zh in range(4) for x in range(4)] for j in range(4)]
-    parts = [lax.ppermute(queries, ("zh", "dim"), moves[j]) for j in range(4)]
-    round_dim = lambda k: lax.ppermute(passages, "dim", [(i, (i + k) % 4) for i in range(4)])
-    d1, d3 = round_dim(1), round_dim(3)
-    d2 = round_dim(2)
-    parts = jnp.stack(parts)
-    parts = pl.pallas_call(
+def hold(q, *ready):
+    return pl.pallas_call(
         hold_kernel,
-        out_shape=jax.ShapeDtypeStruct(parts.shape, parts.dtype),
-        in_specs=anywhere(3),
+        out_shape=jax.ShapeDtypeStruct(q.shape, q.dtype),
+        in_specs=anywhere(1 + len(ready)),
         out_specs=anywhere(1)[0],
         input_output_aliases={0: 0},
         compiler_params=pltpu.CompilerParams(vmem_limit_bytes=MIB),
         name="hold",
-    )(parts, d1, d3)
-    repeated = jnp.broadcast_to(parts[None], (8,) + parts.shape)
-    mine = lax.all_to_all(repeated, ("zl", "y"), 0, 0, tiled=True)
-    swap = [(0, 1), (1, 0)]
-    theirs = lax.ppermute(mine, "core", swap)
+    )(q, *ready)
+
+
+def shards(queries, passages, cand_ids, counts):
     width, doc_cols = 4 * passages.shape[0], passages.shape[1]
     rows, slots = cand_ids.shape
     doc_count = doc_cols // DOC_TOK
@@ -173,13 +182,26 @@
         compiler_params=pltpu.CompilerParams(vmem_limit_bytes=MIB),
         name="prepare",
     )(jnp.transpose(cand_ids), jnp.transpose(counts))
+    flat = lambda zh, x: zh * 4 + x
+    moves = [[(flat(zh, x), flat((x + j) % 4, zh)) for zh in range(4) for x in range(4)] for j in range(4)]
+    parts = [lax.ppermute(queries, ("zh", "dim"), moves[j]) for j in range(4)]
+    round_dim = lambda array, k: lax.ppermute(array, "dim", [(i, (i + k) % 4) for i in range(4)])
+    d1, d3 = round_dim(passages, 1), round_dim(passages, 3)
+    half = passages.shape[1] // 2
+    d2a, d2b = round_dim(d1[:, :half], 1), round_dim(d3[:, half:], 3)
+    parts = jnp.stack(parts)
+    parts = hold(parts, d1, d3, picks, live)
+    repeated = jnp.broadcast_to(parts[None], (8,) + parts.shape)
+    mine = hold(lax.all_to_all(repeated, ("zl", "y"), 0, 0, tiled=True), d2a, d2b)
+    swap = [(0, 1), (1, 0)]
+    theirs = lax.ppermute(mine, "core", swap)
     cand_scores, send = pl.pallas_call(
         score_kernel,
         out_shape=(
             jax.ShapeDtypeStruct((slots, rows), jnp.float32),
-            jax.ShapeDtypeStruct((slots, rows), jnp.float32),
+            jax.ShapeDtypeStruct((2, slots // 2, rows), jnp.float32),
         ),
-        in_specs=vmem(8),
+        in_specs=vmem(9),
         out_specs=tuple(vmem(2)),
         scratch_shapes=[
             pltpu.VMEM((doc_cols, width), passages.dtype),
@@ -188,8 +210,9 @@
         ],
         compiler_params=pltpu.CompilerParams(vmem_limit_bytes=24 * MIB),
         name="score",
-    )(passages, d1, d2, d3, mine, theirs, picks, live)
-    pieces = lax.all_to_all(jnp.broadcast_to(send[None], (32,) + send.shape), ("zh", "zl", "y"), 0, 0, tiled=True)
+    )(passages, d1, d2a, d2b, d3, mine, theirs, picks, live)
+    pieces = jnp.broadcast_to(send[None, :, None], (4, 2, 4) + send.shape[1:]).reshape(32, slots // 2, rows)
+    pieces = lax.all_to_all(pieces, ("zh", "zl", "y"), 0, 0, tiled=True)
     falling, rising = pl.pallas_call(
         top_kernel,
         out_shape=(jax.ShapeDtypeStruct((128, rows), jnp.float32),) * 2,
@@ -199,14 +222,22 @@
         name="top",
     )(pieces.reshape(-1, 8, rows))
     other = lax.ppermute(rising, "core", swap)
-    top_scores = pl.pallas_call(
+    merged = pl.pallas_call(
         merge_kernel,
-        out_shape=jax.ShapeDtypeStruct((TOPK, rows), jnp.float32),
+        out_shape=jax.ShapeDtypeStruct((104, rows), jnp.float32),
         in_specs=vmem(2),
         out_specs=vmem(1)[0],
         compiler_params=pltpu.CompilerParams(vmem_limit_bytes=2 * MIB),
         name="merge",
     )(falling, other)
+    top_scores = pl.pallas_call(
+        join_kernel,
+        out_shape=jax.ShapeDtypeStruct((TOPK, rows), jnp.float32),
+        in_specs=vmem(2),
+        out_specs=vmem(1)[0],
+        compiler_params=pltpu.CompilerParams(vmem_limit_bytes=2 * MIB),
+        name="join",
+    )(merged, lax.ppermute(merged, "zl", swap))
     return (jnp.transpose(cand_scores), jnp.transpose(top_scores))
 
 

time: 91.9 us -> 91.4 us (level)
  blocking collectives: 21.8 us -> 19.3 us
  waiting for transfers between devices: 6.71 us -> 8.79 us
  starting transfers between devices: 39.4 us -> 38.3 us
    ppermute x1, starting transfers between devices: 6.45 us -> 2.39 us  [shards(): other = lax.ppermute(rising, 'core', swap)]
    ppermute x3 -> x5, waiting for transfers between devices: 2.1 us -> 5.88 us  [the longest x4 3.64 us: shards(): lax.ppermute(array, 'dim', [(i, (i + k) % 4) for i in range(4)])]
    ppermute x3 -> x5, starting transfers between devices: 8.44 us -> 11.1 us  [the longest x4 10.2 us: shards(): lax.ppermute(array, 'dim', [(i, (i + k) % 4) for i in range(4)])]
    all_to_all x1, blocking collectives: 21.8 us -> 19.3 us  [shards(): pieces = lax.all_to_all(pieces, ('zh', 'zl', 'y'), 0, 0, tiled=True)]
    all_to_all x1, waiting for transfers between devices: 2.17 us -> 0.01 us  [shards(): lax.all_to_all(repeated, ('zl', 'y'), 0, 0, tiled=True)]
    ppermute x1, waiting for transfers between devices: 0.01 us -> 1.54 us  [shards(): theirs = lax.ppermute(mine, 'core', swap)]
    ppermute x4, waiting for transfers between devices: 1.54 us -> 0.47 us  [shards(): parts = [lax.ppermute(queries, ('zh', 'dim'), moves[j]) for j in range(4)]]
  transfers between devices with their start and end apart: 10 -> 12, of which waited for: 5 -> 5; matrix products, arithmetic and copies ran while one was open for 0% -> 0% of each run, Pallas kernels for 0% -> 0%
where the time goes in v5:
time: 91.4 us; the launch traced here: 90.7 us
  starting transfers between devices  38.3 us (42%)
  Pallas kernels  21.3 us (23%)
  blocking collectives  19.3 us (21%)
  waiting for transfers between devices  8.79 us (10%)
  local copies, waits for them, and re-layouts  2.3 us (3%)
    pallas_call x1, Pallas kernels, shards(): pl.pallas_call(score_kernel, out_shape=(jax.ShapeDtypeStruct((slots, rows...  19.6 us
    all_to_all x1, blocking collectives, shards(): pieces = lax.all_to_all(pieces, ('zh', 'zl', 'y'), 0, 0, tiled=True)  19.3 us
    ppermute x4, starting transfers between devices, shards(): parts = [lax.ppermute(queries, ('zh', 'dim'), moves[j]) for j in range(4)]  15.5 us
    ppermute x4, starting transfers between devices, shards(): lax.ppermute(array, 'dim', [(i, (i + k) % 4) for i in range(4)])  10.2 us
    all_to_all x1, starting transfers between devices, shards(): lax.all_to_all(repeated, ('zl', 'y'), 0, 0, tiled=True)  4.64 us
    ppermute x1, starting transfers between devices, shards(): theirs = lax.ppermute(mine, 'core', swap)  4.64 us
    ppermute x4, waiting for transfers between devices, shards(): lax.ppermute(array, 'dim', [(i, (i + k) % 4) for i in range(4)])  3.64 us
    ppermute x1, starting transfers between devices, shards(): other = lax.ppermute(rising, 'core', swap)  2.39 us
  transfers between devices with their start and end apart: 12, of which 5 were waited for; matrix products, arithmetic and copies ran while one was open for 0% of the time, Pallas kernels for 0%

profile of v5, /device:TPU:1, one launch (start us, length us, event | category | flops | bytes accessed | tf_op | source)
XLA Modules:
  0.0 90.7 jit_solution(1130293373750349321)
XLA Ops:
  0.6 2.1 %collective-permute-start = (bf16[32,8192]{1,0:T(8,128)(2,1)}, bf16[32,8192]{1,0:T(8,128)(2,1)S(1)}, u32[]{:S(2)}, u32[]{:S(2)}) collective-permute-start(bf16[32,8192]{1,0:T(8,128)(2,1)} %d0.1), channel_id=1, source_target_pairs={{0,1},{1,2},{2,3},{3,0},{4,5},{5,6},{6,7},{7,4},{8,9},{9,10},{10,1... | collective-permute-start | bytes 1572872 | tf_op jit(solution)/shard_map/ppermute | solution.py:188
  2.7 1.4 %collective-permute-start.2 = (bf16[32,8192]{1,0:T(8,128)(2,1)}, bf16[32,8192]{1,0:T(8,128)(2,1)S(1)}, u32[]{:S(2)}, u32[]{:S(2)}) collective-permute-start(bf16[32,8192]{1,0:T(8,128)(2,1)} %d0.1), channel_id=1, source_target_pairs={{0,3},{1,0},{2,1},{3,2},{4,7},{5,4},{6,5},{7,6},{8,11},{9,8},{10,9... | collective-permute-start | bytes 1572872 | tf_op jit(solution)/shard_map/ppermute | solution.py:188
  4.1 3.1 %collective-permute-start.5 = (bf16[32,256]{1,0:T(8,128)(2,1)}, bf16[32,256]{1,0:T(8,128)(2,1)S(1)}, u32[]{:S(2)}, u32[]{:S(2)}) collective-permute-start(bf16[32,256]{1,0:T(8,128)(2,1)} %param.4), channel_id=1, source_target_pairs={{0,64},{1,128},{2,192},{3,0},{64,65},{65,129},{66,193},{67,1},{128... | collective-permute-start | bytes 49160 | tf_op jit(solution)/shard_map/ppermute | solution.py:187
  7.2 1.4 %collective-permute-start.4 = (bf16[32,256]{1,0:T(8,128)(2,1)}, bf16[32,256]{1,0:T(8,128)(2,1)S(1)}, u32[]{:S(2)}, u32[]{:S(2)}) collective-permute-start(bf16[32,256]{1,0:T(8,128)(2,1)} %param.4), channel_id=1, source_target_pairs={{0,0},{1,64},{2,128},{3,192},{64,1},{65,65},{66,129},{67,193},{128... | collective-permute-start | bytes 49160 | tf_op jit(solution)/shard_map/ppermute | solution.py:187
  8.6 4.9 %collective-permute-start.7 = (bf16[32,256]{1,0:T(8,128)(2,1)}, bf16[32,256]{1,0:T(8,128)(2,1)S(1)}, u32[]{:S(2)}, u32[]{:S(2)}) collective-permute-start(bf16[32,256]{1,0:T(8,128)(2,1)} %param.4), channel_id=1, source_target_pairs={{0,192},{1,0},{2,64},{3,128},{64,193},{65,1},{66,65},{67,129},{128... | collective-permute-start | bytes 49160 | tf_op jit(solution)/shard_map/ppermute | solution.py:187
  13.5 0.5 collective-permute-done.5
  13.9 6.2 %collective-permute-start.6 = (bf16[32,256]{1,0:T(8,128)(2,1)}, bf16[32,256]{1,0:T(8,128)(2,1)S(1)}, u32[]{:S(2)}, u32[]{:S(2)}) collective-permute-start(bf16[32,256]{1,0:T(8,128)(2,1)} %param.4), channel_id=1, source_target_pairs={{0,128},{1,192},{2,0},{3,64},{64,129},{65,193},{66,1},{67,65},{128... | collective-permute-start | bytes 49160 | tf_op jit(solution)/shard_map/ppermute | solution.py:187
  20.1 0.7 copy-done.2
  20.8 0.7 copy-done.1
  21.5 0.1 prepare.1
  21.6 0.0 collective-permute-done.4
  21.6 0.0 collective-permute-done.7
  21.6 0.0 collective-permute-done.6
  21.6 0.0 collective-permute-done.refs_1_.d1
  21.6 0.9 broadcast_in_dim.4
  22.5 4.6 %all-to-all-start = ((bf16[8,4,32,256]{3,2,1,0:T(8,128)(2,1)}), bf16[8,4,32,256]{3,2,1,0:T(8,128)(2,1)S(1)}, u32[]{:S(2)}, u32[]{:S(2)}) async-start(bf16[8,4,32,256]{3,2,1,0:T(8,128)(2,1)} %broadcast_in_dim.4), calls=%async_computation | async-start | bytes 1048576 | tf_op jit(solution)/shard_map/all_to_all | solution.py:195
  27.2 0.1 collective-permute-start.1
  27.3 0.0 copy-start
  27.3 6.7 %collective-permute-start.3 = (bf16[32,4096]{1,0:T(8,128)(2,1)S(1)}, bf16[32,4096]{1,0:T(8,128)(2,1)S(1)}, u32[]{:S(2)}, u32[]{:S(2)}) collective-permute-start(bf16[32,4096]{1,0:T(8,128)(2,1)S(1)} %slice.9), channel_id=1, source_target_pairs={{0,3},{1,0},{2,1},{3,2},{4,7},{5,4},{6,5},{7,6},{8,11},{9,8},{10,9... | collective-permute-start | bytes 786440 | tf_op jit(solution)/shard_map/ppermute | solution.py:188
  34.0 3.6 %collective-permute-done.1.refs_1_.d2a = bf16[32,4096]{1,0:T(8,128)(2,1)S(1)} collective-permute-done((bf16[32,4096]{1,0:T(8,128)(2,1)S(1)}, bf16[32,4096]{1,0:T(8,128)(2,1)S(1)}, u32[]{:S(2)}, u32[]{:S(2)}) %collective-permute-start.1) | collective-permute-done | bytes 262176 | tf_op jit(solution)/shard_map/ppermute | solution.py:188
  37.6 0.0 collective-permute-done.3.refs_2_.d2b
  37.6 0.0 all-to-all-done.refs_0_
  37.6 4.6 %collective-permute-start.8 = (bf16[8,4,32,256]{3,2,1,0:T(8,128)(2,1)S(1)}, bf16[8,4,32,256]{3,2,1,0:T(8,128)(2,1)S(1)}, u32[]{:S(2)}, u32[]{:S(2)}) collective-permute-start(bf16[8,4,32,256]{3,2,1,0:T(8,128)(2,1)S(1)} %hold.3.qa), channel_id=1, source_target_pairs={{0,4},{4,0},{1,5},{5,1},{2,6},{6,2},{3,7},{7,3},{8,12},{12,8},{9,1... | collective-permute-start | bytes 1572872 | tf_op jit(solution)/shard_map/ppermute | solution.py:197
  42.3 1.5 %collective-permute-done.8.qb = bf16[8,4,32,256]{3,2,1,0:T(8,128)(2,1)S(1)} collective-permute-done((bf16[8,4,32,256]{3,2,1,0:T(8,128)(2,1)S(1)}, bf16[8,4,32,256]{3,2,1,0:T(8,128)(2,1)S(1)}, u32[]{:S(2)}, u32[]{:S(2)}) %collective-permute-start.8) | collective-permute-done | bytes 524320 | tf_op jit(solution)/shard_map/ppermute | solution.py:197
  43.8 19.6 %score.1 = (f32[32,128]{1,0:T(8,128)}, f32[2,16,128]{2,1,0:T(8,128)S(1)}) custom-call(bf16[32,8192]{1,0:T(8,128)(2,1)S(1)} %copy-done, bf16[32,8192]{1,0:T(8,128)(2,1)S(1)} %collective-permute-done.refs_1_.d1, bf16[32,4096]{1,0:T(8,128)(2,1)S(1)} %collective-permute-done.1.refs_1_.d2a, bf16[32,4096]{1,0:T(8,128)(2,1)S(1)} %collective-permute-done.3.refs_2_.d2b, ...), custom_call_target="tpu_custom_call" | custom-call | tf_op jit(solution)/shard_map/score/pallas_call | solution.py:198
  63.4 19.3 %all_to_all.10 = f32[32,16,128]{2,1,0:T(8,128)S(1)} all-to-all(f32[32,16,128]{2,1,0:T(8,128)S(1)} %bitcast.13), channel_id=1, replica_groups=mesh['zh'=4,'zl'=2,'y'=4,'core'=2,'dim'=4] {'zh','zl','y'}, dimensions={0} | all-to-all | bytes 524288 | tf_op jit(solution)/shard_map/all_to_all | solution.py:215
  82.7 1.0 %top.1 = (f32[128,128]{1,0:T(8,128)S(1)}, f32[128,128]{1,0:T(8,128)S(1)}) custom-call(f32[64,8,128]{2,1,0:T(8,128)S(1)} %bitcast.10), custom_call_target="tpu_custom_call" | custom-call | tf_op jit(solution)/shard_map/top/pallas_call | solution.py:216
  83.7 2.4 %collective-permute-start.9 = (f32[128,128]{1,0:T(8,128)S(1)}, f32[128,128]{1,0:T(8,128)S(1)}, u32[]{:S(2)}, u32[]{:S(2)}) collective-permute-start(f32[128,128]{1,0:T(8,128)S(1)} %get-tuple-element.13), channel_id=1, source_target_pairs={{0,4},{4,0},{1,5},{5,1},{2,6},{6,2},{3,7},{7,3},{8,12},{12,8},{9,1... | collective-permute-start | bytes 196616 | tf_op jit(solution)/shard_map/ppermute | solution.py:224
  86.1 0.9 collective-permute-done.9.rising
  87.0 0.8 collective-permute-start.10
  87.8 2.2 %collective-permute-done.10.theirs = f32[104,128]{1,0:T(8,128)S(1)} collective-permute-done((f32[104,128]{1,0:T(8,128)S(1)}, f32[104,128]{1,0:T(8,128)S(1)}, u32[]{:S(2)}, u32[]{:S(2)}) %collective-permute-start.10) | collective-permute-done | bytes 53280 | tf_op jit(solution)/shard_map/ppermute | solution.py:240
  90.1 0.6 join.1
  (11 shorter events, 0.1 us)
Async XLA Ops:
  0.6 21.0 %collective-permute-start = (bf16[32,8192]{1,0:T(8,128)(2,1)}, bf16[32,8192]{1,0:T(8,128)(2,1)S(1)}, u32[]{:S(2)}, u32[]{:S(2)}) collective-permute-start(bf16[32,8192]{1,0:T(8,128)(2,1)} %d0.1), channel_id=1, source_target_pairs={{0,1},{1,2},{2,3},{3,0},{4,5},{5,6},{6,7},{7,4},{8,9},{9,10},{10,1... | collective-permute-start | bytes 1572872 | tf_op jit(solution)/shard_map/ppermute | solution.py:188
  2.7 18.9 %collective-permute-start.2 = (bf16[32,8192]{1,0:T(8,128)(2,1)}, bf16[32,8192]{1,0:T(8,128)(2,1)S(1)}, u32[]{:S(2)}, u32[]{:S(2)}) collective-permute-start(bf16[32,8192]{1,0:T(8,128)(2,1)} %d0.1), channel_id=1, source_target_pairs={{0,3},{1,0},{2,1},{3,2},{4,7},{5,4},{6,5},{7,6},{8,11},{9,8},{10,9... | collective-permute-start | bytes 1572872 | tf_op jit(solution)/shard_map/ppermute | solution.py:188
  4.1 9.8 %collective-permute-start.5 = (bf16[32,256]{1,0:T(8,128)(2,1)}, bf16[32,256]{1,0:T(8,128)(2,1)S(1)}, u32[]{:S(2)}, u32[]{:S(2)}) collective-permute-start(bf16[32,256]{1,0:T(8,128)(2,1)} %param.4), channel_id=1, source_target_pairs={{0,64},{1,128},{2,192},{3,0},{64,65},{65,129},{66,193},{67,1},{128... | collective-permute-start | bytes 49160 | tf_op jit(solution)/shard_map/ppermute | solution.py:187
  7.2 14.4 %collective-permute-start.4 = (bf16[32,256]{1,0:T(8,128)(2,1)}, bf16[32,256]{1,0:T(8,128)(2,1)S(1)}, u32[]{:S(2)}, u32[]{:S(2)}) collective-permute-start(bf16[32,256]{1,0:T(8,128)(2,1)} %param.4), channel_id=1, source_target_pairs={{0,0},{1,64},{2,128},{3,192},{64,1},{65,65},{66,129},{67,193},{128... | collective-permute-start | bytes 49160 | tf_op jit(solution)/shard_map/ppermute | solution.py:187
  8.6 13.0 %collective-permute-start.7 = (bf16[32,256]{1,0:T(8,128)(2,1)}, bf16[32,256]{1,0:T(8,128)(2,1)S(1)}, u32[]{:S(2)}, u32[]{:S(2)}) collective-permute-start(bf16[32,256]{1,0:T(8,128)(2,1)} %param.4), channel_id=1, source_target_pairs={{0,192},{1,0},{2,64},{3,128},{64,193},{65,1},{66,65},{67,129},{128... | collective-permute-start | bytes 49160 | tf_op jit(solution)/shard_map/ppermute | solution.py:187
  13.9 7.6 %collective-permute-start.6 = (bf16[32,256]{1,0:T(8,128)(2,1)}, bf16[32,256]{1,0:T(8,128)(2,1)S(1)}, u32[]{:S(2)}, u32[]{:S(2)}) collective-permute-start(bf16[32,256]{1,0:T(8,128)(2,1)} %param.4), channel_id=1, source_target_pairs={{0,128},{1,192},{2,0},{3,64},{64,129},{65,193},{66,1},{67,65},{128... | collective-permute-start | bytes 49160 | tf_op jit(solution)/shard_map/ppermute | solution.py:187
  20.1 0.7 copy-start.2
  20.7 0.7 copy-start.1
  22.5 15.1 %all-to-all-start = ((bf16[8,4,32,256]{3,2,1,0:T(8,128)(2,1)}), bf16[8,4,32,256]{3,2,1,0:T(8,128)(2,1)S(1)}, u32[]{:S(2)}, u32[]{:S(2)}) async-start(bf16[8,4,32,256]{3,2,1,0:T(8,128)(2,1)} %broadcast_in_dim.4), calls=%async_computation | async-start | bytes 1048576 | tf_op jit(solution)/shard_map/all_to_all | solution.py:195
  27.2 10.4 %collective-permute-start.1 = (bf16[32,4096]{1,0:T(8,128)(2,1)S(1)}, bf16[32,4096]{1,0:T(8,128)(2,1)S(1)}, u32[]{:S(2)}, u32[]{:S(2)}) collective-permute-start(bf16[32,4096]{1,0:T(8,128)(2,1)S(1)} %slice.8), channel_id=1, source_target_pairs={{0,1},{1,2},{2,3},{3,0},{4,5},{5,6},{6,7},{7,4},{8,9},{9,10},{10,1... | collective-permute-start | bytes 786440 | tf_op jit(solution)/shard_map/ppermute | solution.py:188
  27.3 16.5 %copy-start = (bf16[32,8192]{1,0:T(8,128)(2,1)S(1)}, bf16[32,8192]{1,0:T(8,128)(2,1)}, u32[]{:S(2)}) copy-start(bf16[32,8192]{1,0:T(8,128)(2,1)} %d0.1) | copy-start | bytes 1572868
  27.3 10.3 %collective-permute-start.3 = (bf16[32,4096]{1,0:T(8,128)(2,1)S(1)}, bf16[32,4096]{1,0:T(8,128)(2,1)S(1)}, u32[]{:S(2)}, u32[]{:S(2)}) collective-permute-start(bf16[32,4096]{1,0:T(8,128)(2,1)S(1)} %slice.9), channel_id=1, source_target_pairs={{0,3},{1,0},{2,1},{3,2},{4,7},{5,4},{6,5},{7,6},{8,11},{9,8},{10,9... | collective-permute-start | bytes 786440 | tf_op jit(solution)/shard_map/ppermute | solution.py:188
  37.6 6.2 %collective-permute-start.8 = (bf16[8,4,32,256]{3,2,1,0:T(8,128)(2,1)S(1)}, bf16[8,4,32,256]{3,2,1,0:T(8,128)(2,1)S(1)}, u32[]{:S(2)}, u32[]{:S(2)}) collective-permute-start(bf16[8,4,32,256]{3,2,1,0:T(8,128)(2,1)S(1)} %hold.3.qa), channel_id=1, source_target_pairs={{0,4},{4,0},{1,5},{5,1},{2,6},{6,2},{3,7},{7,3},{8,12},{12,8},{9,1... | collective-permute-start | bytes 1572872 | tf_op jit(solution)/shard_map/ppermute | solution.py:197
  83.7 3.3 %collective-permute-start.9 = (f32[128,128]{1,0:T(8,128)S(1)}, f32[128,128]{1,0:T(8,128)S(1)}, u32[]{:S(2)}, u32[]{:S(2)}) collective-permute-start(f32[128,128]{1,0:T(8,128)S(1)} %get-tuple-element.13), channel_id=1, source_target_pairs={{0,4},{4,0},{1,5},{5,1},{2,6},{6,2},{3,7},{7,3},{8,12},{12,8},{9,1... | collective-permute-start | bytes 196616 | tf_op jit(solution)/shard_map/ppermute | solution.py:224
  87.0 3.1 %collective-permute-start.10 = (f32[104,128]{1,0:T(8,128)S(1)}, f32[104,128]{1,0:T(8,128)S(1)}, u32[]{:S(2)}, u32[]{:S(2)}) collective-permute-start(f32[104,128]{1,0:T(8,128)S(1)} %merge.1.mine), channel_id=1, source_target_pairs={{0,32},{32,0},{1,33},{33,1},{2,34},{34,2},{3,35},{35,3},{4,36},{36... | collective-permute-start | bytes 159752 | tf_op jit(solution)/shard_map/ppermute | solution.py:240

commit v6 on v5

--- a/solution.py
+++ b/solution.py
@@ -24,17 +24,16 @@
     live[...] = (lax.broadcasted_iota(jnp.int32, live.shape, 0) < counts[...]).astype(jnp.int32)
 
 
-def score_kernel(d0, d1, d2a, d2b, d3, qa, qb, picks, live, cand, send, docs, best, kept):
+def score_queries(passages, qa, qb, zl, picks, docs, best, kept):
+    d0, d1, d2a, d2b, d3 = passages
     core = lax.axis_index("core")
     turn = lax.rem(lax.axis_index("zh") - lax.axis_index("dim") + 4, 4)
     docs_n = best.shape[0]
-    sources = qa.shape[0]
-    slots = live.shape[0]
     tile = 512
     per = tile // DOC_TOK
 
-    def one(source, q, side, first):
-        weights = jnp.concatenate([q[source, lax.rem(turn + k, 4)] for k in range(4)], axis=0)
+    def one(y, q, side, first):
+        weights = jnp.concatenate([q[y, lax.rem(turn + k, 4)] for k in range(4)], axis=0)
         for t in range(docs_n // per):
             span = slice(t * tile, (t + 1) * tile)
             if first:
@@ -50,21 +49,30 @@
         turned = jnp.transpose(best[...])
         mean = jnp.sum(turned.reshape(-1, QTOK, docs_n), axis=1) * (1.0 / QTOK)
         queries = mean.shape[0]
-        rows = pl.ds(pl.multiple_of((source * 2 + side) * queries, queries), queries)
-        kept[rows, :] = jnp.take_along_axis(mean, picks[rows, :], axis=1)
-
-    def two(source, first):
+        row = (y * 2 + side) * queries
+        chosen = picks[pl.ds(pl.multiple_of(zl * kept.shape[0] + row, queries), queries), :]
+        kept[pl.ds(pl.multiple_of(row, queries), queries), :] = jnp.take_along_axis(mean, chosen, axis=1)
+
+    def two(y, first):
         for i in range(2):
-            one(source + i, qa, core, first and i == 0)
-            one(source + i, qb, 1 - core, False)
-
-    def step(i, carry):
-        two(2 * i, False)
-        return carry
+            one(y + i, qa, core, first and i == 0)
+            one(y + i, qb, 1 - core, False)
 
     two(0, True)
-    lax.fori_loop(1, sources // 2, step, 0)
-    scores = jnp.transpose(kept[...])[:slots, :]
+    two(2, False)
+
+
+def near_kernel(d0, d1, d2a, d2b, d3, qa, qb, picks, kept, docs, best):
+    score_queries((d0, d1, d2a, d2b, d3), qa, qb, lax.axis_index("zl"), picks, docs, best, kept)
+
+
+def far_kernel(d0, d1, d2a, d2b, d3, qa, qb, picks, near, live, cand, send, docs, best, kept):
+    zl = lax.axis_index("zl")
+    slots = live.shape[0]
+    score_queries((d0, d1, d2a, d2b, d3), qa, qb, 1 - zl, picks, docs, best, kept)
+    a, b = near[...], kept[...]
+    scores = jnp.concatenate([jnp.where(zl == 0, a, b), jnp.where(zl == 0, b, a)], axis=0)
+    scores = jnp.transpose(scores)[:slots, :]
     alive = live[...] > 0
     cand[...] = jnp.where(alive, scores, 0.0)
     masked = jnp.where(alive, scores, LOWEST)
@@ -191,26 +199,42 @@
     d2a, d2b = round_dim(d1[:, :half], 1), round_dim(d3[:, half:], 3)
     parts = jnp.stack(parts)
     parts = hold(parts, d1, d3, picks, live)
-    repeated = jnp.broadcast_to(parts[None], (8,) + parts.shape)
-    mine = hold(lax.all_to_all(repeated, ("zl", "y"), 0, 0, tiled=True), d2a, d2b)
+    repeated = jnp.broadcast_to(parts[None], (4,) + parts.shape)
     swap = [(0, 1), (1, 0)]
+    mine = hold(lax.all_to_all(repeated, "y", 0, 0, tiled=True), d2a, d2b)
     theirs = lax.ppermute(mine, "core", swap)
+    mine_far = lax.ppermute(mine, "zl", swap)
+    cost = pl.CostEstimate(flops=rows * QTOK * doc_cols * width, bytes_accessed=1 << 20, transcendentals=0)
+    scratch = [
+        pltpu.VMEM((doc_cols, width), passages.dtype),
+        pltpu.VMEM((doc_count, queries.shape[1]), jnp.float32),
+    ]
+    all_passages = (passages, d1, d2a, d2b, d3)
+    near = pl.pallas_call(
+        near_kernel,
+        out_shape=jax.ShapeDtypeStruct((rows // 2, doc_count), jnp.float32),
+        in_specs=vmem(8),
+        out_specs=vmem(1)[0],
+        scratch_shapes=scratch,
+        cost_estimate=cost,
+        compiler_params=pltpu.CompilerParams(vmem_limit_bytes=20 * MIB),
+        name="near",
+    )(*all_passages, mine, theirs, picks)
+    mine_far = hold(mine_far, near)
+    theirs_far = lax.ppermute(mine_far, "core", swap)
     cand_scores, send = pl.pallas_call(
-        score_kernel,
+        far_kernel,
         out_shape=(
             jax.ShapeDtypeStruct((slots, rows), jnp.float32),
             jax.ShapeDtypeStruct((2, slots // 2, rows), jnp.float32),
         ),
-        in_specs=vmem(9),
+        in_specs=vmem(10),
         out_specs=tuple(vmem(2)),
-        scratch_shapes=[
-            pltpu.VMEM((doc_cols, width), passages.dtype),
-            pltpu.VMEM((doc_count, queries.shape[1]), jnp.float32),
-            pltpu.VMEM((rows, doc_count), jnp.float32),
-        ],
-        compiler_params=pltpu.CompilerParams(vmem_limit_bytes=24 * MIB),
-        name="score",
-    )(passages, d1, d2a, d2b, d3, mine, theirs, picks, live)
+        scratch_shapes=scratch + [pltpu.VMEM((rows // 2, doc_count), jnp.float32)],
+        cost_estimate=cost,
+        compiler_params=pltpu.CompilerParams(vmem_limit_bytes=20 * MIB),
+        name="far",
+    )(*all_passages, mine_far, theirs_far, picks, near, live)
     pieces = jnp.broadcast_to(send[None, :, None], (4, 2, 4) + send.shape[1:]).reshape(32, slots // 2, rows)
     pieces = lax.all_to_all(pieces, ("zh", "zl", "y"), 0, 0, tiled=True)
     falling, rising = pl.pallas_call(

time: 91.4 us -> 86.8 us (0.950)
  blocking collectives: 19.3 us -> 27 us
  starting transfers between devices: 38.3 us -> 31.5 us
  waiting for transfers between devices: 8.79 us -> 4.99 us
    all_to_all x0 -> x1, blocking collectives: none -> 9.51 us  [shards(): mine = hold(lax.all_to_all(repeated, 'y', 0, 0, tiled=True), d2a, d2b)]
    ppermute x4, starting transfers between devices: 10.2 us -> 5 us  [shards(): lax.ppermute(array, 'dim', [(i, (i + k) % 4) for i in range(4)])]
    all_to_all x1 -> x0, starting transfers between devices: 4.64 us -> none  [shards(): lax.all_to_all(repeated, ('zl', 'y'), 0, 0, tiled=True)]
    ppermute x4, waiting for transfers between devices: 3.64 us -> 0.25 us  [shards(): lax.ppermute(array, 'dim', [(i, (i + k) % 4) for i in range(4)])]
    ppermute x4, starting transfers between devices: 15.5 us -> 17.9 us  [shards(): parts = [lax.ppermute(queries, ('zh', 'dim'), moves[j]) for j in range(4)]]
    all_to_all x1, blocking collectives: 19.3 us -> 17.5 us  [shards(): pieces = lax.all_to_all(pieces, ('zh', 'zl', 'y'), 0, 0, tiled=True)]
    ppermute x0 -> x2, starting transfers between devices: none -> 1.4 us  [the longest x1 0.74 us: shards(): mine_far = lax.ppermute(mine, 'zl', swap)]
    ppermute x0 -> x2, waiting for transfers between devices: none -> 1.17 us  [the longest x1 1.16 us: shards(): theirs_far = lax.ppermute(mine_far, 'core', swap)]
  transfers between devices with their start and end apart: 12 -> 13, of which waited for: 5 -> 5; matrix products, arithmetic and copies ran while one was open for 0% -> 0% of each run, Pallas kernels for 0% -> 11%
where the time goes in v6:
time: 86.8 us; the launch traced here: 86.3 us
  starting transfers between devices  31.5 us (36%)
  blocking collectives  27 us (31%)
  Pallas kernels  20.7 us (24%)
  waiting for transfers between devices  4.99 us (6%)
  local copies, waits for them, and re-layouts  1.45 us (2%)
    ppermute x4, starting transfers between devices, shards(): parts = [lax.ppermute(queries, ('zh', 'dim'), moves[j]) for j in range(4)]  17.9 us
    all_to_all x1, blocking collectives, shards(): pieces = lax.all_to_all(pieces, ('zh', 'zl', 'y'), 0, 0, tiled=True)  17.5 us
    pallas_call x1, Pallas kernels, shards(): pl.pallas_call(far_kernel, out_shape=(jax.ShapeDtypeStruct((slots, rows),...  9.82 us
    all_to_all x1, blocking collectives, shards(): mine = hold(lax.all_to_all(repeated, 'y', 0, 0, tiled=True), d2a, d2b)  9.51 us
    pallas_call x1, Pallas kernels, shards(): pl.pallas_call(near_kernel, out_shape=jax.ShapeDtypeStruct((rows // 2, do...  9.13 us
    ppermute x4, starting transfers between devices, shards(): lax.ppermute(array, 'dim', [(i, (i + k) % 4) for i in range(4)])  5 us
    ppermute x1, starting transfers between devices, shards(): theirs = lax.ppermute(mine, 'core', swap)  3.9 us
    ppermute x1, starting transfers between devices, shards(): other = lax.ppermute(rising, 'core', swap)  2.4 us
  transfers between devices with their start and end apart: 13, of which 5 were waited for; matrix products, arithmetic and copies ran while one was open for 0% of the time, Pallas kernels for 11%

profile of v6, /device:TPU:1, one launch (start us, length us, event | category | flops | bytes accessed | tf_op | source)
XLA Modules:
  0.0 86.3 jit_solution(12796770324513534610)
XLA Ops:
  0.6 3.4 %collective-permute-start.2 = (bf16[32,8192]{1,0:T(8,128)(2,1)}, bf16[32,8192]{1,0:T(8,128)(2,1)S(1)}, u32[]{:S(2)}, u32[]{:S(2)}) collective-permute-start(bf16[32,8192]{1,0:T(8,128)(2,1)} %d0.3), channel_id=1, source_target_pairs={{0,3},{1,0},{2,1},{3,2},{4,7},{5,4},{6,5},{7,6},{8,11},{9,8},{10,9... | collective-permute-start | bytes 1572872 | tf_op jit(solution)/shard_map/ppermute | solution.py:196
  4.0 0.0 collective-permute-start
  4.0 3.0 %collective-permute-start.5 = (bf16[32,256]{1,0:T(8,128)(2,1)}, bf16[32,256]{1,0:T(8,128)(2,1)S(1)}, u32[]{:S(2)}, u32[]{:S(2)}) collective-permute-start(bf16[32,256]{1,0:T(8,128)(2,1)} %param.4), channel_id=1, source_target_pairs={{0,64},{1,128},{2,192},{3,0},{64,65},{65,129},{66,193},{67,1},{128... | collective-permute-start | bytes 49160 | tf_op jit(solution)/shard_map/ppermute | solution.py:195
  7.0 1.4 %collective-permute-start.4 = (bf16[32,256]{1,0:T(8,128)(2,1)}, bf16[32,256]{1,0:T(8,128)(2,1)S(1)}, u32[]{:S(2)}, u32[]{:S(2)}) collective-permute-start(bf16[32,256]{1,0:T(8,128)(2,1)} %param.4), channel_id=1, source_target_pairs={{0,0},{1,64},{2,128},{3,192},{64,1},{65,65},{66,129},{67,193},{128... | collective-permute-start | bytes 49160 | tf_op jit(solution)/shard_map/ppermute | solution.py:195
  8.4 6.3 %collective-permute-start.7 = (bf16[32,256]{1,0:T(8,128)(2,1)}, bf16[32,256]{1,0:T(8,128)(2,1)S(1)}, u32[]{:S(2)}, u32[]{:S(2)}) collective-permute-start(bf16[32,256]{1,0:T(8,128)(2,1)} %param.4), channel_id=1, source_target_pairs={{0,192},{1,0},{2,64},{3,128},{64,193},{65,1},{66,65},{67,129},{128... | collective-permute-start | bytes 49160 | tf_op jit(solution)/shard_map/ppermute | solution.py:195
  14.7 0.2 collective-permute-done.2.refs_2_.d3
  14.9 7.3 %collective-permute-start.6 = (bf16[32,256]{1,0:T(8,128)(2,1)}, bf16[32,256]{1,0:T(8,128)(2,1)S(1)}, u32[]{:S(2)}, u32[]{:S(2)}) collective-permute-start(bf16[32,256]{1,0:T(8,128)(2,1)} %param.4), channel_id=1, source_target_pairs={{0,128},{1,192},{2,0},{3,64},{64,129},{65,193},{66,1},{67,65},{128... | collective-permute-start | bytes 49160 | tf_op jit(solution)/shard_map/ppermute | solution.py:195
  22.2 0.7 copy-done.1
  22.8 0.7 copy-done
  23.6 0.1 prepare.1
  23.7 0.0 collective-permute-done.refs_1_.d1
  23.7 0.1 collective-permute-start.3
  23.8 0.0 collective-permute-done.5
  23.8 1.5 %collective-permute-start.1 = (bf16[32,4096]{1,0:T(8,128)(2,1)S(1)}, bf16[32,4096]{1,0:T(8,128)(2,1)S(1)}, u32[]{:S(2)}, u32[]{:S(2)}) collective-permute-start(bf16[32,4096]{1,0:T(8,128)(2,1)S(1)} %slice.8), channel_id=1, source_target_pairs={{0,1},{1,2},{2,3},{3,0},{4,5},{5,6},{6,7},{7,4},{8,9},{9,10},{10,1... | collective-permute-start | bytes 786440 | tf_op jit(solution)/shard_map/ppermute | solution.py:196
  25.3 0.0 collective-permute-done.4
  25.3 0.0 collective-permute-done.7
  25.4 9.5 %all_to_all.10.refs_0_ = bf16[4,4,32,256]{3,2,1,0:T(8,128)(2,1)S(1)} all-to-all(bf16[4,4,32,256]{3,2,1,0:T(8,128)(2,1)S(1)} %broadcast_in_dim.4), channel_id=1, replica_groups=mesh['zh'=4,'zl'=2,'y'=4,'core'=2,'dim'=4] {'y'}, dimensions={0} | all-to-all | bytes 524288 | tf_op jit(solution)/shard_map/all_to_all | solution.py:204
  34.9 3.9 %collective-permute-start.9 = (bf16[4,4,32,256]{3,2,1,0:T(8,128)(2,1)S(1)}, bf16[4,4,32,256]{3,2,1,0:T(8,128)(2,1)S(1)}, u32[]{:S(2)}, u32[]{:S(2)}) collective-permute-start(bf16[4,4,32,256]{3,2,1,0:T(8,128)(2,1)S(1)} %hold.4.qa), channel_id=1, source_target_pairs={{0,4},{4,0},{1,5},{5,1},{2,6},{6,2},{3,7},{7,3},{8,12},{12,8},{9,1... | collective-permute-start | bytes 786440 | tf_op jit(solution)/shard_map/ppermute | solution.py:205
  38.9 0.7 collective-permute-start.8
  39.6 0.4 collective-permute-done.9.qb
  40.0 9.1 %near.1.refs_1_ = f32[64,128]{1,0:T(8,128)S(1)} custom-call(bf16[32,8192]{1,0:T(8,128)(2,1)S(1)} %copy-done.2, bf16[32,8192]{1,0:T(8,128)(2,1)S(1)} %collective-permute-done.refs_1_.d1, bf16[32,4096]{1,0:T(8,128)(2,1)S(1)} %collective-permute-done.1.refs_1_.d2a, bf16[32,4096]{1,0:T(8,128)(2,1)S(1)} %collective-permute-done.3.refs_2_.d2b, ...), custom_call_target="tpu_custom_call" | custom-call | flops 4294967296 | bytes 1048576 | tf_op jit(solution)/shard_map/near/pallas_call | solution.py:213
  49.1 0.0 collective-permute-done.8.refs_0_
  49.2 0.7 collective-permute-start.10
  49.8 1.2 %collective-permute-done.10.qb = bf16[4,4,32,256]{3,2,1,0:T(8,128)(2,1)S(1)} collective-permute-done((bf16[4,4,32,256]{3,2,1,0:T(8,128)(2,1)S(1)}, bf16[4,4,32,256]{3,2,1,0:T(8,128)(2,1)S(1)}, u32[]{:S(2)}, u32[]{:S(2)}) %collective-permute-start.10) | collective-permute-done | bytes 262176 | tf_op jit(solution)/shard_map/ppermute | solution.py:224
  51.0 9.8 %far.1 = (f32[32,128]{1,0:T(8,128)}, f32[2,16,128]{2,1,0:T(8,128)S(1)}) custom-call(bf16[32,8192]{1,0:T(8,128)(2,1)S(1)} %copy-done.2, bf16[32,8192]{1,0:T(8,128)(2,1)S(1)} %collective-permute-done.refs_1_.d1, bf16[32,4096]{1,0:T(8,128)(2,1)S(1)} %collective-permute-done.1.refs_1_.d2a, bf16[32,4096]{1,0:T(8,128)(2,1)S(1)} %collective-permute-done.3.refs_2_.d2b, ...), custom_call_target="tpu_custom_call" | custom-call | flops 4294967296 | bytes 1048576 | tf_op jit(solution)/shard_map/far/pallas_call | solution.py:225
  60.8 17.5 %all_to_all.11 = f32[32,16,128]{2,1,0:T(8,128)S(1)} all-to-all(f32[32,16,128]{2,1,0:T(8,128)S(1)} %bitcast.13), channel_id=1, replica_groups=mesh['zh'=4,'zl'=2,'y'=4,'core'=2,'dim'=4] {'zh','zl','y'}, dimensions={0} | all-to-all | bytes 524288 | tf_op jit(solution)/shard_map/all_to_all | solution.py:239
  78.3 1.0 %top.1 = (f32[128,128]{1,0:T(8,128)S(1)}, f32[128,128]{1,0:T(8,128)S(1)}) custom-call(f32[64,8,128]{2,1,0:T(8,128)S(1)} %bitcast.10), custom_call_target="tpu_custom_call" | custom-call | tf_op jit(solution)/shard_map/top/pallas_call | solution.py:240
  79.3 2.4 %collective-permute-start.11 = (f32[128,128]{1,0:T(8,128)S(1)}, f32[128,128]{1,0:T(8,128)S(1)}, u32[]{:S(2)}, u32[]{:S(2)}) collective-permute-start(f32[128,128]{1,0:T(8,128)S(1)} %get-tuple-element.13), channel_id=1, source_target_pairs={{0,4},{4,0},{1,5},{5,1},{2,6},{6,2},{3,7},{7,3},{8,12},{12,8},{9,1... | collective-permute-start | bytes 196616 | tf_op jit(solution)/shard_map/ppermute | solution.py:248
  81.7 0.9 %collective-permute-done.11.rising = f32[128,128]{1,0:T(8,128)S(1)} collective-permute-done((f32[128,128]{1,0:T(8,128)S(1)}, f32[128,128]{1,0:T(8,128)S(1)}, u32[]{:S(2)}, u32[]{:S(2)}) %collective-permute-start.11) | collective-permute-done | bytes 65568 | tf_op jit(solution)/shard_map/ppermute | solution.py:248
  82.6 0.8 collective-permute-start.12
  83.5 2.2 %collective-permute-done.12.theirs = f32[104,128]{1,0:T(8,128)S(1)} collective-permute-done((f32[104,128]{1,0:T(8,128)S(1)}, f32[104,128]{1,0:T(8,128)S(1)}, u32[]{:S(2)}, u32[]{:S(2)}) %collective-permute-start.12) | collective-permute-done | bytes 53280 | tf_op jit(solution)/shard_map/ppermute | solution.py:264
  85.7 0.6 join.1
  (16 shorter events, 0.1 us)
Async XLA Ops:
  0.6 14.3 %collective-permute-start.2 = (bf16[32,8192]{1,0:T(8,128)(2,1)}, bf16[32,8192]{1,0:T(8,128)(2,1)S(1)}, u32[]{:S(2)}, u32[]{:S(2)}) collective-permute-start(bf16[32,8192]{1,0:T(8,128)(2,1)} %d0.3), channel_id=1, source_target_pairs={{0,3},{1,0},{2,1},{3,2},{4,7},{5,4},{6,5},{7,6},{8,11},{9,8},{10,9... | collective-permute-start | bytes 1572872 | tf_op jit(solution)/shard_map/ppermute | solution.py:196
  4.0 19.7 %collective-permute-start = (bf16[32,8192]{1,0:T(8,128)(2,1)}, bf16[32,8192]{1,0:T(8,128)(2,1)S(1)}, u32[]{:S(2)}, u32[]{:S(2)}) collective-permute-start(bf16[32,8192]{1,0:T(8,128)(2,1)} %d0.3), channel_id=1, source_target_pairs={{0,1},{1,2},{2,3},{3,0},{4,5},{5,6},{6,7},{7,4},{8,9},{9,10},{10,1... | collective-permute-start | bytes 1572872 | tf_op jit(solution)/shard_map/ppermute | solution.py:196
  4.0 19.8 %collective-permute-start.5 = (bf16[32,256]{1,0:T(8,128)(2,1)}, bf16[32,256]{1,0:T(8,128)(2,1)S(1)}, u32[]{:S(2)}, u32[]{:S(2)}) collective-permute-start(bf16[32,256]{1,0:T(8,128)(2,1)} %param.4), channel_id=1, source_target_pairs={{0,64},{1,128},{2,192},{3,0},{64,65},{65,129},{66,193},{67,1},{128... | collective-permute-start | bytes 49160 | tf_op jit(solution)/shard_map/ppermute | solution.py:195
  7.0 18.3 %collective-permute-start.4 = (bf16[32,256]{1,0:T(8,128)(2,1)}, bf16[32,256]{1,0:T(8,128)(2,1)S(1)}, u32[]{:S(2)}, u32[]{:S(2)}) collective-permute-start(bf16[32,256]{1,0:T(8,128)(2,1)} %param.4), channel_id=1, source_target_pairs={{0,0},{1,64},{2,128},{3,192},{64,1},{65,65},{66,129},{67,193},{128... | collective-permute-start | bytes 49160 | tf_op jit(solution)/shard_map/ppermute | solution.py:195
  8.4 17.0 %collective-permute-start.7 = (bf16[32,256]{1,0:T(8,128)(2,1)}, bf16[32,256]{1,0:T(8,128)(2,1)S(1)}, u32[]{:S(2)}, u32[]{:S(2)}) collective-permute-start(bf16[32,256]{1,0:T(8,128)(2,1)} %param.4), channel_id=1, source_target_pairs={{0,192},{1,0},{2,64},{3,128},{64,193},{65,1},{66,65},{67,129},{128... | collective-permute-start | bytes 49160 | tf_op jit(solution)/shard_map/ppermute | solution.py:195
  14.9 10.4 %collective-permute-start.6 = (bf16[32,256]{1,0:T(8,128)(2,1)}, bf16[32,256]{1,0:T(8,128)(2,1)S(1)}, u32[]{:S(2)}, u32[]{:S(2)}) collective-permute-start(bf16[32,256]{1,0:T(8,128)(2,1)} %param.4), channel_id=1, source_target_pairs={{0,128},{1,192},{2,0},{3,64},{64,129},{65,193},{66,1},{67,65},{128... | collective-permute-start | bytes 49160 | tf_op jit(solution)/shard_map/ppermute | solution.py:195
  22.2 0.7 copy-start.1
  22.8 0.7 copy-start
  23.7 11.2 %collective-permute-start.3 = (bf16[32,4096]{1,0:T(8,128)(2,1)S(1)}, bf16[32,4096]{1,0:T(8,128)(2,1)S(1)}, u32[]{:S(2)}, u32[]{:S(2)}) collective-permute-start(bf16[32,4096]{1,0:T(8,128)(2,1)S(1)} %slice.9), channel_id=1, source_target_pairs={{0,3},{1,0},{2,1},{3,2},{4,7},{5,4},{6,5},{7,6},{8,11},{9,8},{10,9... | collective-permute-start | bytes 786440 | tf_op jit(solution)/shard_map/ppermute | solution.py:196
  23.8 11.1 %collective-permute-start.1 = (bf16[32,4096]{1,0:T(8,128)(2,1)S(1)}, bf16[32,4096]{1,0:T(8,128)(2,1)S(1)}, u32[]{:S(2)}, u32[]{:S(2)}) collective-permute-start(bf16[32,4096]{1,0:T(8,128)(2,1)S(1)} %slice.8), channel_id=1, source_target_pairs={{0,1},{1,2},{2,3},{3,0},{4,5},{5,6},{6,7},{7,4},{8,9},{9,10},{10,1... | collective-permute-start | bytes 786440 | tf_op jit(solution)/shard_map/ppermute | solution.py:196
  34.9 5.1 %copy-start.2 = (bf16[32,8192]{1,0:T(8,128)(2,1)S(1)}, bf16[32,8192]{1,0:T(8,128)(2,1)}, u32[]{:S(2)}) copy-start(bf16[32,8192]{1,0:T(8,128)(2,1)} %d0.3) | copy-start | bytes 1572868
  34.9 5.1 %collective-permute-start.9 = (bf16[4,4,32,256]{3,2,1,0:T(8,128)(2,1)S(1)}, bf16[4,4,32,256]{3,2,1,0:T(8,128)(2,1)S(1)}, u32[]{:S(2)}, u32[]{:S(2)}) collective-permute-start(bf16[4,4,32,256]{3,2,1,0:T(8,128)(2,1)S(1)} %hold.4.qa), channel_id=1, source_target_pairs={{0,4},{4,0},{1,5},{5,1},{2,6},{6,2},{3,7},{7,3},{8,12},{12,8},{9,1... | collective-permute-start | bytes 786440 | tf_op jit(solution)/shard_map/ppermute | solution.py:205
  38.9 10.3 %collective-permute-start.8 = (bf16[4,4,32,256]{3,2,1,0:T(8,128)(2,1)S(1)}, bf16[4,4,32,256]{3,2,1,0:T(8,128)(2,1)S(1)}, u32[]{:S(2)}, u32[]{:S(2)}) collective-permute-start(bf16[4,4,32,256]{3,2,1,0:T(8,128)(2,1)S(1)} %hold.4.qa), channel_id=1, source_target_pairs={{0,32},{32,0},{1,33},{33,1},{2,34},{34,2},{3,35},{35,3},{4,36},{36... | collective-permute-start | bytes 786440 | tf_op jit(solution)/shard_map/ppermute | solution.py:206
  49.2 1.8 %collective-permute-start.10 = (bf16[4,4,32,256]{3,2,1,0:T(8,128)(2,1)S(1)}, bf16[4,4,32,256]{3,2,1,0:T(8,128)(2,1)S(1)}, u32[]{:S(2)}, u32[]{:S(2)}) collective-permute-start(bf16[4,4,32,256]{3,2,1,0:T(8,128)(2,1)S(1)} %hold.5.qa), channel_id=1, source_target_pairs={{0,4},{4,0},{1,5},{5,1},{2,6},{6,2},{3,7},{7,3},{8,12},{12,8},{9,1... | collective-permute-start | bytes 786440 | tf_op jit(solution)/shard_map/ppermute | solution.py:224
  79.3 3.3 %collective-permute-start.11 = (f32[128,128]{1,0:T(8,128)S(1)}, f32[128,128]{1,0:T(8,128)S(1)}, u32[]{:S(2)}, u32[]{:S(2)}) collective-permute-start(f32[128,128]{1,0:T(8,128)S(1)} %get-tuple-element.13), channel_id=1, source_target_pairs={{0,4},{4,0},{1,5},{5,1},{2,6},{6,2},{3,7},{7,3},{8,12},{12,8},{9,1... | collective-permute-start | bytes 196616 | tf_op jit(solution)/shard_map/ppermute | solution.py:248
  82.6 3.1 %collective-permute-start.12 = (f32[104,128]{1,0:T(8,128)S(1)}, f32[104,128]{1,0:T(8,128)S(1)}, u32[]{:S(2)}, u32[]{:S(2)}) collective-permute-start(f32[104,128]{1,0:T(8,128)S(1)} %merge.1.mine), channel_id=1, source_target_pairs={{0,32},{32,0},{1,33},{33,1},{2,34},{34,2},{3,35},{35,3},{4,36},{36... | collective-permute-start | bytes 159752 | tf_op jit(solution)/shard_map/ppermute | solution.py:264

commit v7 on v6

--- a/solution.py
+++ b/solution.py
@@ -24,9 +24,8 @@
     live[...] = (lax.broadcasted_iota(jnp.int32, live.shape, 0) < counts[...]).astype(jnp.int32)
 
 
-def score_queries(passages, qa, qb, zl, picks, docs, best, kept):
+def score_queries(passages, sources, zl, picks, docs, best, kept):
     d0, d1, d2a, d2b, d3 = passages
-    core = lax.axis_index("core")
     turn = lax.rem(lax.axis_index("zh") - lax.axis_index("dim") + 4, 4)
     docs_n = best.shape[0]
     tile = 512
@@ -53,24 +52,31 @@
         chosen = picks[pl.ds(pl.multiple_of(zl * kept.shape[0] + row, queries), queries), :]
         kept[pl.ds(pl.multiple_of(row, queries), queries), :] = jnp.take_along_axis(mean, chosen, axis=1)
 
-    def two(y, first):
-        for i in range(2):
-            one(y + i, qa, core, first and i == 0)
-            one(y + i, qb, 1 - core, False)
-
-    two(0, True)
-    two(2, False)
+    first = True
+    for y in range(sources[0][0].shape[0]):
+        for q, side in sources:
+            one(y, q, side, first)
+            first = False
 
 
 def near_kernel(d0, d1, d2a, d2b, d3, qa, qb, picks, kept, docs, best):
-    score_queries((d0, d1, d2a, d2b, d3), qa, qb, lax.axis_index("zl"), picks, docs, best, kept)
-
-
-def far_kernel(d0, d1, d2a, d2b, d3, qa, qb, picks, near, live, cand, send, docs, best, kept):
-    zl = lax.axis_index("zl")
+    core = lax.axis_index("core")
+    sources = ((qa, core), (qb, 1 - core))
+    score_queries((d0, d1, d2a, d2b, d3), sources, lax.axis_index("zl"), picks, docs, best, kept)
+
+
+def far_kernel(d0, d1, d2a, d2b, d3, qa, picks, kept, docs, best):
+    kept[...] = jnp.zeros_like(kept)
+    sources = ((qa, lax.axis_index("core")),)
+    score_queries((d0, d1, d2a, d2b, d3), sources, 1 - lax.axis_index("zl"), picks, docs, best, kept)
+
+
+def last_kernel(d0, d1, d2a, d2b, d3, qb, picks, near, far, live, cand, send, docs, best, kept):
+    core, zl = lax.axis_index("core"), lax.axis_index("zl")
     slots = live.shape[0]
-    score_queries((d0, d1, d2a, d2b, d3), qa, qb, 1 - zl, picks, docs, best, kept)
-    a, b = near[...], kept[...]
+    score_queries((d0, d1, d2a, d2b, d3), ((qb, 1 - core),), 1 - zl, picks, docs, best, kept)
+    group = lax.broadcasted_iota(jnp.int32, kept.shape, 0) // 8
+    a, b = near[...], jnp.where(lax.rem(group, 2) == core, far[...], kept[...])
     scores = jnp.concatenate([jnp.where(zl == 0, a, b), jnp.where(zl == 0, b, a)], axis=0)
     scores = jnp.transpose(scores)[:slots, :]
     alive = live[...] > 0
@@ -222,8 +228,19 @@
     )(*all_passages, mine, theirs, picks)
     mine_far = hold(mine_far, near)
     theirs_far = lax.ppermute(mine_far, "core", swap)
+    less = pl.CostEstimate(flops=cost.flops // 2, bytes_accessed=1 << 20, transcendentals=0)
+    far = pl.pallas_call(
+        far_kernel,
+        out_shape=jax.ShapeDtypeStruct((rows // 2, doc_count), jnp.float32),
+        in_specs=vmem(7),
+        out_specs=vmem(1)[0],
+        scratch_shapes=scratch,
+        cost_estimate=less,
+        compiler_params=pltpu.CompilerParams(vmem_limit_bytes=20 * MIB),
+        name="far",
+    )(*all_passages, mine_far, picks)
     cand_scores, send = pl.pallas_call(
-        far_kernel,
+        last_kernel,
         out_shape=(
             jax.ShapeDtypeStruct((slots, rows), jnp.float32),
             jax.ShapeDtypeStruct((2, slots // 2, rows), jnp.float32),
@@ -231,10 +248,10 @@
         in_specs=vmem(10),
         out_specs=tuple(vmem(2)),
         scratch_shapes=scratch + [pltpu.VMEM((rows // 2, doc_count), jnp.float32)],
-        cost_estimate=cost,
+        cost_estimate=less,
         compiler_params=pltpu.CompilerParams(vmem_limit_bytes=20 * MIB),
-        name="far",
-    )(*all_passages, mine_far, theirs_far, picks, near, live)
+        name="last",
+    )(*all_passages, theirs_far, picks, near, far, live)
     pieces = jnp.broadcast_to(send[None, :, None], (4, 2, 4) + send.shape[1:]).reshape(32, slots // 2, rows)
     pieces = lax.all_to_all(pieces, ("zh", "zl", "y"), 0, 0, tiled=True)
     falling, rising = pl.pallas_call(

time: 86.8 us -> 86.1 us (level)
  waiting for transfers between devices: 4.99 us -> 3.95 us
    ppermute x1, waiting for transfers between devices: 1.16 us -> 0.01 us  [shards(): theirs_far = lax.ppermute(mine_far, 'core', swap)]
    pallas_call x1 -> x2, Pallas kernels: 9.82 us -> 10.2 us  [the longest x1 5.42 us: shards(): pl.pallas_call(last_kernel, out_shape=(jax.ShapeDtypeStruct((slots, rows)...]
  transfers between devices with their start and end apart: 13 -> 13, of which waited for: 5 -> 4; matrix products, arithmetic and copies ran while one was open for 0% -> 0% of each run, Pallas kernels for 11% -> 16%
where the time goes in v7:
time: 86.1 us; the launch traced here: 85.6 us
  starting transfers between devices  31.2 us (36%)
  blocking collectives  27.3 us (32%)
  Pallas kernels  21.1 us (25%)
  waiting for transfers between devices  3.95 us (5%)
  local copies, waits for them, and re-layouts  1.45 us (2%)
    ppermute x4, starting transfers between devices, shards(): parts = [lax.ppermute(queries, ('zh', 'dim'), moves[j]) for j in range(4)]  17.9 us
    all_to_all x1, blocking collectives, shards(): pieces = lax.all_to_all(pieces, ('zh', 'zl', 'y'), 0, 0, tiled=True)  17.7 us
    all_to_all x1, blocking collectives, shards(): mine = hold(lax.all_to_all(repeated, 'y', 0, 0, tiled=True), d2a, d2b)  9.51 us
    pallas_call x1, Pallas kernels, shards(): pl.pallas_call(near_kernel, out_shape=jax.ShapeDtypeStruct((rows // 2, do...  9.13 us
    pallas_call x1, Pallas kernels, shards(): pl.pallas_call(last_kernel, out_shape=(jax.ShapeDtypeStruct((slots, rows)...  5.42 us
    ppermute x4, starting transfers between devices, shards(): lax.ppermute(array, 'dim', [(i, (i + k) % 4) for i in range(4)])  5 us
    pallas_call x1, Pallas kernels, shards(): pl.pallas_call(far_kernel, out_shape=jax.ShapeDtypeStruct((rows // 2, doc...  4.76 us
    ppermute x1, starting transfers between devices, shards(): theirs = lax.ppermute(mine, 'core', swap)  3.9 us
  transfers between devices with their start and end apart: 13, of which 4 were waited for; matrix products, arithmetic and copies ran while one was open for 0% of the time, Pallas kernels for 16%

profile of v7, /device:TPU:1, one launch (start us, length us, event | category | flops | bytes accessed | tf_op | source)
XLA Modules:
  0.0 85.6 jit_solution(3843148205973480607)
XLA Ops:
  0.6 3.4 %collective-permute-start.2 = (bf16[32,8192]{1,0:T(8,128)(2,1)}, bf16[32,8192]{1,0:T(8,128)(2,1)S(1)}, u32[]{:S(2)}, u32[]{:S(2)}) collective-permute-start(bf16[32,8192]{1,0:T(8,128)(2,1)} %d0.5), channel_id=1, source_target_pairs={{0,3},{1,0},{2,1},{3,2},{4,7},{5,4},{6,5},{7,6},{8,11},{9,8},{10,9... | collective-permute-start | bytes 1572872 | tf_op jit(solution)/shard_map/ppermute | solution.py:202
  4.0 0.0 collective-permute-start
  4.0 3.0 %collective-permute-start.5 = (bf16[32,256]{1,0:T(8,128)(2,1)}, bf16[32,256]{1,0:T(8,128)(2,1)S(1)}, u32[]{:S(2)}, u32[]{:S(2)}) collective-permute-start(bf16[32,256]{1,0:T(8,128)(2,1)} %param.4), channel_id=1, source_target_pairs={{0,64},{1,128},{2,192},{3,0},{64,65},{65,129},{66,193},{67,1},{128... | collective-permute-start | bytes 49160 | tf_op jit(solution)/shard_map/ppermute | solution.py:201
  7.0 1.4 %collective-permute-start.4 = (bf16[32,256]{1,0:T(8,128)(2,1)}, bf16[32,256]{1,0:T(8,128)(2,1)S(1)}, u32[]{:S(2)}, u32[]{:S(2)}) collective-permute-start(bf16[32,256]{1,0:T(8,128)(2,1)} %param.4), channel_id=1, source_target_pairs={{0,0},{1,64},{2,128},{3,192},{64,1},{65,65},{66,129},{67,193},{128... | collective-permute-start | bytes 49160 | tf_op jit(solution)/shard_map/ppermute | solution.py:201
  8.4 6.3 %collective-permute-start.7 = (bf16[32,256]{1,0:T(8,128)(2,1)}, bf16[32,256]{1,0:T(8,128)(2,1)S(1)}, u32[]{:S(2)}, u32[]{:S(2)}) collective-permute-start(bf16[32,256]{1,0:T(8,128)(2,1)} %param.4), channel_id=1, source_target_pairs={{0,192},{1,0},{2,64},{3,128},{64,193},{65,1},{66,65},{67,129},{128... | collective-permute-start | bytes 49160 | tf_op jit(solution)/shard_map/ppermute | solution.py:201
  14.7 0.2 collective-permute-done.2.refs_2_.d3
  14.9 7.3 %collective-permute-start.6 = (bf16[32,256]{1,0:T(8,128)(2,1)}, bf16[32,256]{1,0:T(8,128)(2,1)S(1)}, u32[]{:S(2)}, u32[]{:S(2)}) collective-permute-start(bf16[32,256]{1,0:T(8,128)(2,1)} %param.4), channel_id=1, source_target_pairs={{0,128},{1,192},{2,0},{3,64},{64,129},{65,193},{66,1},{67,65},{128... | collective-permute-start | bytes 49160 | tf_op jit(solution)/shard_map/ppermute | solution.py:201
  22.2 0.7 copy-done.1
  22.8 0.7 copy-done
  23.6 0.1 prepare.1
  23.7 0.0 collective-permute-done.refs_1_.d1
  23.7 0.1 collective-permute-start.3
  23.8 0.0 collective-permute-done.5
  23.8 1.5 %collective-permute-start.1 = (bf16[32,4096]{1,0:T(8,128)(2,1)S(1)}, bf16[32,4096]{1,0:T(8,128)(2,1)S(1)}, u32[]{:S(2)}, u32[]{:S(2)}) collective-permute-start(bf16[32,4096]{1,0:T(8,128)(2,1)S(1)} %slice.8), channel_id=1, source_target_pairs={{0,1},{1,2},{2,3},{3,0},{4,5},{5,6},{6,7},{7,4},{8,9},{9,10},{10,1... | collective-permute-start | bytes 786440 | tf_op jit(solution)/shard_map/ppermute | solution.py:202
  25.3 0.0 collective-permute-done.4
  25.4 9.5 %all_to_all.10.refs_0_ = bf16[4,4,32,256]{3,2,1,0:T(8,128)(2,1)S(1)} all-to-all(bf16[4,4,32,256]{3,2,1,0:T(8,128)(2,1)S(1)} %broadcast_in_dim.4), channel_id=1, replica_groups=mesh['zh'=4,'zl'=2,'y'=4,'core'=2,'dim'=4] {'y'}, dimensions={0} | all-to-all | bytes 524288 | tf_op jit(solution)/shard_map/all_to_all | solution.py:210
  34.9 3.9 %collective-permute-start.9 = (bf16[4,4,32,256]{3,2,1,0:T(8,128)(2,1)S(1)}, bf16[4,4,32,256]{3,2,1,0:T(8,128)(2,1)S(1)}, u32[]{:S(2)}, u32[]{:S(2)}) collective-permute-start(bf16[4,4,32,256]{3,2,1,0:T(8,128)(2,1)S(1)} %hold.4.qa), channel_id=1, source_target_pairs={{0,4},{4,0},{1,5},{5,1},{2,6},{6,2},{3,7},{7,3},{8,12},{12,8},{9,1... | collective-permute-start | bytes 786440 | tf_op jit(solution)/shard_map/ppermute | solution.py:211
  38.9 0.7 collective-permute-start.8
  39.6 0.4 collective-permute-done.9.qb
  40.0 9.1 %near.1.refs_1_ = f32[64,128]{1,0:T(8,128)S(1)} custom-call(bf16[32,8192]{1,0:T(8,128)(2,1)S(1)} %copy-done.2, bf16[32,8192]{1,0:T(8,128)(2,1)S(1)} %collective-permute-done.refs_1_.d1, bf16[32,4096]{1,0:T(8,128)(2,1)S(1)} %collective-permute-done.1.refs_1_.d2a, bf16[32,4096]{1,0:T(8,128)(2,1)S(1)} %collective-permute-done.3.refs_2_.d2b, ...), custom_call_target="tpu_custom_call" | custom-call | flops 4294967296 | bytes 1048576 | tf_op jit(solution)/shard_map/near/pallas_call | solution.py:219
  49.1 0.0 collective-permute-done.8.refs_0_
  49.2 0.7 collective-permute-start.10
  49.8 4.8 %far.1 = f32[64,128]{1,0:T(8,128)S(1)} custom-call(bf16[32,8192]{1,0:T(8,128)(2,1)S(1)} %copy-done.2, bf16[32,8192]{1,0:T(8,128)(2,1)S(1)} %collective-permute-done.refs_1_.d1, bf16[32,4096]{1,0:T(8,128)(2,1)S(1)} %collective-permute-done.1.refs_1_.d2a, bf16[32,4096]{1,0:T(8,128)(2,1)S(1)} %collective-permute-done.3.refs_2_.d2b, ...), custom_call_target="tpu_custom_call" | custom-call | flops 2147483648 | bytes 1048576 | tf_op jit(solution)/shard_map/far/pallas_call | solution.py:232
  54.6 0.0 collective-permute-done.10.qb
  54.6 5.4 %last.1 = (f32[32,128]{1,0:T(8,128)}, f32[2,16,128]{2,1,0:T(8,128)S(1)}) custom-call(bf16[32,8192]{1,0:T(8,128)(2,1)S(1)} %copy-done.2, bf16[32,8192]{1,0:T(8,128)(2,1)S(1)} %collective-permute-done.refs_1_.d1, bf16[32,4096]{1,0:T(8,128)(2,1)S(1)} %collective-permute-done.1.refs_1_.d2a, bf16[32,4096]{1,0:T(8,128)(2,1)S(1)} %collective-permute-done.3.refs_2_.d2b, ...), custom_call_target="tpu_custom_call" | custom-call | flops 2147483648 | bytes 1048576 | tf_op jit(solution)/shard_map/last/pallas_call | solution.py:242
  60.0 17.7 %all_to_all.11 = f32[32,16,128]{2,1,0:T(8,128)S(1)} all-to-all(f32[32,16,128]{2,1,0:T(8,128)S(1)} %bitcast.13), channel_id=1, replica_groups=mesh['zh'=4,'zl'=2,'y'=4,'core'=2,'dim'=4] {'zh','zl','y'}, dimensions={0} | all-to-all | bytes 524288 | tf_op jit(solution)/shard_map/all_to_all | solution.py:256
  77.8 1.0 %top.1 = (f32[128,128]{1,0:T(8,128)S(1)}, f32[128,128]{1,0:T(8,128)S(1)}) custom-call(f32[64,8,128]{2,1,0:T(8,128)S(1)} %bitcast.10), custom_call_target="tpu_custom_call" | custom-call | tf_op jit(solution)/shard_map/top/pallas_call | solution.py:257
  78.7 2.2 %collective-permute-start.11 = (f32[128,128]{1,0:T(8,128)S(1)}, f32[128,128]{1,0:T(8,128)S(1)}, u32[]{:S(2)}, u32[]{:S(2)}) collective-permute-start(f32[128,128]{1,0:T(8,128)S(1)} %get-tuple-element.13), channel_id=1, source_target_pairs={{0,4},{4,0},{1,5},{5,1},{2,6},{6,2},{3,7},{7,3},{8,12},{12,8},{9,1... | collective-permute-start | bytes 196616 | tf_op jit(solution)/shard_map/ppermute | solution.py:265
  81.0 0.9 %collective-permute-done.11.rising = f32[128,128]{1,0:T(8,128)S(1)} collective-permute-done((f32[128,128]{1,0:T(8,128)S(1)}, f32[128,128]{1,0:T(8,128)S(1)}, u32[]{:S(2)}, u32[]{:S(2)}) %collective-permute-start.11) | collective-permute-done | bytes 65568 | tf_op jit(solution)/shard_map/ppermute | solution.py:265
  81.9 0.7 collective-permute-start.12
  82.6 2.4 %collective-permute-done.12.theirs = f32[104,128]{1,0:T(8,128)S(1)} collective-permute-done((f32[104,128]{1,0:T(8,128)S(1)}, f32[104,128]{1,0:T(8,128)S(1)}, u32[]{:S(2)}, u32[]{:S(2)}) %collective-permute-start.12) | collective-permute-done | bytes 53280 | tf_op jit(solution)/shard_map/ppermute | solution.py:281
  85.0 0.6 join.1
  (17 shorter events, 0.2 us)
Async XLA Ops:
  0.6 14.3 %collective-permute-start.2 = (bf16[32,8192]{1,0:T(8,128)(2,1)}, bf16[32,8192]{1,0:T(8,128)(2,1)S(1)}, u32[]{:S(2)}, u32[]{:S(2)}) collective-permute-start(bf16[32,8192]{1,0:T(8,128)(2,1)} %d0.5), channel_id=1, source_target_pairs={{0,3},{1,0},{2,1},{3,2},{4,7},{5,4},{6,5},{7,6},{8,11},{9,8},{10,9... | collective-permute-start | bytes 1572872 | tf_op jit(solution)/shard_map/ppermute | solution.py:202
  4.0 19.7 %collective-permute-start = (bf16[32,8192]{1,0:T(8,128)(2,1)}, bf16[32,8192]{1,0:T(8,128)(2,1)S(1)}, u32[]{:S(2)}, u32[]{:S(2)}) collective-permute-start(bf16[32,8192]{1,0:T(8,128)(2,1)} %d0.5), channel_id=1, source_target_pairs={{0,1},{1,2},{2,3},{3,0},{4,5},{5,6},{6,7},{7,4},{8,9},{9,10},{10,1... | collective-permute-start | bytes 1572872 | tf_op jit(solution)/shard_map/ppermute | solution.py:202
  4.0 19.8 %collective-permute-start.5 = (bf16[32,256]{1,0:T(8,128)(2,1)}, bf16[32,256]{1,0:T(8,128)(2,1)S(1)}, u32[]{:S(2)}, u32[]{:S(2)}) collective-permute-start(bf16[32,256]{1,0:T(8,128)(2,1)} %param.4), channel_id=1, source_target_pairs={{0,64},{1,128},{2,192},{3,0},{64,65},{65,129},{66,193},{67,1},{128... | collective-permute-start | bytes 49160 | tf_op jit(solution)/shard_map/ppermute | solution.py:201
  7.0 18.3 %collective-permute-start.4 = (bf16[32,256]{1,0:T(8,128)(2,1)}, bf16[32,256]{1,0:T(8,128)(2,1)S(1)}, u32[]{:S(2)}, u32[]{:S(2)}) collective-permute-start(bf16[32,256]{1,0:T(8,128)(2,1)} %param.4), channel_id=1, source_target_pairs={{0,0},{1,64},{2,128},{3,192},{64,1},{65,65},{66,129},{67,193},{128... | collective-permute-start | bytes 49160 | tf_op jit(solution)/shard_map/ppermute | solution.py:201
  8.4 17.0 %collective-permute-start.7 = (bf16[32,256]{1,0:T(8,128)(2,1)}, bf16[32,256]{1,0:T(8,128)(2,1)S(1)}, u32[]{:S(2)}, u32[]{:S(2)}) collective-permute-start(bf16[32,256]{1,0:T(8,128)(2,1)} %param.4), channel_id=1, source_target_pairs={{0,192},{1,0},{2,64},{3,128},{64,193},{65,1},{66,65},{67,129},{128... | collective-permute-start | bytes 49160 | tf_op jit(solution)/shard_map/ppermute | solution.py:201
  14.9 10.4 %collective-permute-start.6 = (bf16[32,256]{1,0:T(8,128)(2,1)}, bf16[32,256]{1,0:T(8,128)(2,1)S(1)}, u32[]{:S(2)}, u32[]{:S(2)}) collective-permute-start(bf16[32,256]{1,0:T(8,128)(2,1)} %param.4), channel_id=1, source_target_pairs={{0,128},{1,192},{2,0},{3,64},{64,129},{65,193},{66,1},{67,65},{128... | collective-permute-start | bytes 49160 | tf_op jit(solution)/shard_map/ppermute | solution.py:201
  22.2 0.7 copy-start.1
  22.8 0.7 copy-start
  23.7 11.2 %collective-permute-start.3 = (bf16[32,4096]{1,0:T(8,128)(2,1)S(1)}, bf16[32,4096]{1,0:T(8,128)(2,1)S(1)}, u32[]{:S(2)}, u32[]{:S(2)}) collective-permute-start(bf16[32,4096]{1,0:T(8,128)(2,1)S(1)} %slice.9), channel_id=1, source_target_pairs={{0,3},{1,0},{2,1},{3,2},{4,7},{5,4},{6,5},{7,6},{8,11},{9,8},{10,9... | collective-permute-start | bytes 786440 | tf_op jit(solution)/shard_map/ppermute | solution.py:202
  23.8 11.1 %collective-permute-start.1 = (bf16[32,4096]{1,0:T(8,128)(2,1)S(1)}, bf16[32,4096]{1,0:T(8,128)(2,1)S(1)}, u32[]{:S(2)}, u32[]{:S(2)}) collective-permute-start(bf16[32,4096]{1,0:T(8,128)(2,1)S(1)} %slice.8), channel_id=1, source_target_pairs={{0,1},{1,2},{2,3},{3,0},{4,5},{5,6},{6,7},{7,4},{8,9},{9,10},{10,1... | collective-permute-start | bytes 786440 | tf_op jit(solution)/shard_map/ppermute | solution.py:202
  34.9 5.1 %copy-start.2 = (bf16[32,8192]{1,0:T(8,128)(2,1)S(1)}, bf16[32,8192]{1,0:T(8,128)(2,1)}, u32[]{:S(2)}) copy-start(bf16[32,8192]{1,0:T(8,128)(2,1)} %d0.5) | copy-start | bytes 1572868
  34.9 5.1 %collective-permute-start.9 = (bf16[4,4,32,256]{3,2,1,0:T(8,128)(2,1)S(1)}, bf16[4,4,32,256]{3,2,1,0:T(8,128)(2,1)S(1)}, u32[]{:S(2)}, u32[]{:S(2)}) collective-permute-start(bf16[4,4,32,256]{3,2,1,0:T(8,128)(2,1)S(1)} %hold.4.qa), channel_id=1, source_target_pairs={{0,4},{4,0},{1,5},{5,1},{2,6},{6,2},{3,7},{7,3},{8,12},{12,8},{9,1... | collective-permute-start | bytes 786440 | tf_op jit(solution)/shard_map/ppermute | solution.py:211
  38.9 10.3 %collective-permute-start.8 = (bf16[4,4,32,256]{3,2,1,0:T(8,128)(2,1)S(1)}, bf16[4,4,32,256]{3,2,1,0:T(8,128)(2,1)S(1)}, u32[]{:S(2)}, u32[]{:S(2)}) collective-permute-start(bf16[4,4,32,256]{3,2,1,0:T(8,128)(2,1)S(1)} %hold.4.qa), channel_id=1, source_target_pairs={{0,32},{32,0},{1,33},{33,1},{2,34},{34,2},{3,35},{35,3},{4,36},{36... | collective-permute-start | bytes 786440 | tf_op jit(solution)/shard_map/ppermute | solution.py:212
  49.2 5.4 %collective-permute-start.10 = (bf16[4,4,32,256]{3,2,1,0:T(8,128)(2,1)S(1)}, bf16[4,4,32,256]{3,2,1,0:T(8,128)(2,1)S(1)}, u32[]{:S(2)}, u32[]{:S(2)}) collective-permute-start(bf16[4,4,32,256]{3,2,1,0:T(8,128)(2,1)S(1)} %hold.5.qa), channel_id=1, source_target_pairs={{0,4},{4,0},{1,5},{5,1},{2,6},{6,2},{3,7},{7,3},{8,12},{12,8},{9,1... | collective-permute-start | bytes 786440 | tf_op jit(solution)/shard_map/ppermute | solution.py:230
  78.7 3.1 %collective-permute-start.11 = (f32[128,128]{1,0:T(8,128)S(1)}, f32[128,128]{1,0:T(8,128)S(1)}, u32[]{:S(2)}, u32[]{:S(2)}) collective-permute-start(f32[128,128]{1,0:T(8,128)S(1)} %get-tuple-element.13), channel_id=1, source_target_pairs={{0,4},{4,0},{1,5},{5,1},{2,6},{6,2},{3,7},{7,3},{8,12},{12,8},{9,1... | collective-permute-start | bytes 196616 | tf_op jit(solution)/shard_map/ppermute | solution.py:265
  81.9 3.1 %collective-permute-start.12 = (f32[104,128]{1,0:T(8,128)S(1)}, f32[104,128]{1,0:T(8,128)S(1)}, u32[]{:S(2)}, u32[]{:S(2)}) collective-permute-start(f32[104,128]{1,0:T(8,128)S(1)} %merge.1.mine), channel_id=1, source_target_pairs={{0,32},{32,0},{1,33},{33,1},{2,34},{34,2},{3,35},{35,3},{4,36},{36... | collective-permute-start | bytes 159752 | tf_op jit(solution)/shard_map/ppermute | solution.py:281

commit v8 on v7

--- a/solution.py
+++ b/solution.py
@@ -204,7 +204,7 @@
     half = passages.shape[1] // 2
     d2a, d2b = round_dim(d1[:, :half], 1), round_dim(d3[:, half:], 3)
     parts = jnp.stack(parts)
-    parts = hold(parts, d1, d3, picks, live)
+    parts = hold(parts, d1, d3)
     repeated = jnp.broadcast_to(parts[None], (4,) + parts.shape)
     swap = [(0, 1), (1, 0)]
     mine = hold(lax.all_to_all(repeated, "y", 0, 0, tiled=True), d2a, d2b)

time: 86.1 us -> 86.8 us (level)
  blocking collectives: 27.3 us -> 28.7 us
    all_to_all x1, blocking collectives: 17.7 us -> 19.2 us  [shards(): pieces = lax.all_to_all(pieces, ('zh', 'zl', 'y'), 0, 0, tiled=True)]
  transfers between devices with their start and end apart: 13 -> 13, of which waited for: 4 -> 3; matrix products, arithmetic and copies ran while one was open for 0% -> 0% of each run, Pallas kernels for 16% -> 16%
where the time goes in v8:
time: 86.8 us; the launch traced here: 86.2 us
  starting transfers between devices  31.4 us (36%)
  blocking collectives  28.7 us (33%)
  Pallas kernels  21.1 us (24%)
  waiting for transfers between devices  3.52 us (4%)
    all_to_all x1, blocking collectives, shards(): pieces = lax.all_to_all(pieces, ('zh', 'zl', 'y'), 0, 0, tiled=True)  19.2 us
    ppermute x4, starting transfers between devices, shards(): parts = [lax.ppermute(queries, ('zh', 'dim'), moves[j]) for j in range(4)]  17.9 us
    all_to_all x1, blocking collectives, shards(): mine = hold(lax.all_to_all(repeated, 'y', 0, 0, tiled=True), d2a, d2b)  9.51 us
    pallas_call x1, Pallas kernels, shards(): pl.pallas_call(near_kernel, out_shape=jax.ShapeDtypeStruct((rows // 2, do...  9.13 us
    pallas_call x1, Pallas kernels, shards(): pl.pallas_call(last_kernel, out_shape=(jax.ShapeDtypeStruct((slots, rows)...  5.42 us
    ppermute x4, starting transfers between devices, shards(): lax.ppermute(array, 'dim', [(i, (i + k) % 4) for i in range(4)])  5 us
    pallas_call x1, Pallas kernels, shards(): pl.pallas_call(far_kernel, out_shape=jax.ShapeDtypeStruct((rows // 2, doc...  4.76 us
    ppermute x1, starting transfers between devices, shards(): theirs = lax.ppermute(mine, 'core', swap)  3.9 us
  transfers between devices with their start and end apart: 13, of which 3 were waited for; matrix products, arithmetic and copies ran while one was open for 0% of the time, Pallas kernels for 16%

profile of v8, /device:TPU:1, one launch (start us, length us, event | category | flops | bytes accessed | tf_op | source)
XLA Modules:
  0.0 86.2 jit_solution(3313093961822545600)
XLA Ops:
  0.6 3.4 %collective-permute-start.2 = (bf16[32,8192]{1,0:T(8,128)(2,1)}, bf16[32,8192]{1,0:T(8,128)(2,1)S(1)}, u32[]{:S(2)}, u32[]{:S(2)}) collective-permute-start(bf16[32,8192]{1,0:T(8,128)(2,1)} %d0.5), channel_id=1, source_target_pairs={{0,3},{1,0},{2,1},{3,2},{4,7},{5,4},{6,5},{7,6},{8,11},{9,8},{10,9... | collective-permute-start | bytes 1572872 | tf_op jit(solution)/shard_map/ppermute | solution.py:202
  4.0 0.0 collective-permute-start
  4.0 3.0 %collective-permute-start.5 = (bf16[32,256]{1,0:T(8,128)(2,1)}, bf16[32,256]{1,0:T(8,128)(2,1)S(1)}, u32[]{:S(2)}, u32[]{:S(2)}) collective-permute-start(bf16[32,256]{1,0:T(8,128)(2,1)} %param.4), channel_id=1, source_target_pairs={{0,64},{1,128},{2,192},{3,0},{64,65},{65,129},{66,193},{67,1},{128... | collective-permute-start | bytes 49160 | tf_op jit(solution)/shard_map/ppermute | solution.py:201
  7.0 1.4 %collective-permute-start.4 = (bf16[32,256]{1,0:T(8,128)(2,1)}, bf16[32,256]{1,0:T(8,128)(2,1)S(1)}, u32[]{:S(2)}, u32[]{:S(2)}) collective-permute-start(bf16[32,256]{1,0:T(8,128)(2,1)} %param.4), channel_id=1, source_target_pairs={{0,0},{1,64},{2,128},{3,192},{64,1},{65,65},{66,129},{67,193},{128... | collective-permute-start | bytes 49160 | tf_op jit(solution)/shard_map/ppermute | solution.py:201
  8.4 6.3 %collective-permute-start.7 = (bf16[32,256]{1,0:T(8,128)(2,1)}, bf16[32,256]{1,0:T(8,128)(2,1)S(1)}, u32[]{:S(2)}, u32[]{:S(2)}) collective-permute-start(bf16[32,256]{1,0:T(8,128)(2,1)} %param.4), channel_id=1, source_target_pairs={{0,192},{1,0},{2,64},{3,128},{64,193},{65,1},{66,65},{67,129},{128... | collective-permute-start | bytes 49160 | tf_op jit(solution)/shard_map/ppermute | solution.py:201
  14.7 0.2 collective-permute-done.2.refs_2_.d3
  14.9 7.3 %collective-permute-start.6 = (bf16[32,256]{1,0:T(8,128)(2,1)}, bf16[32,256]{1,0:T(8,128)(2,1)S(1)}, u32[]{:S(2)}, u32[]{:S(2)}) collective-permute-start(bf16[32,256]{1,0:T(8,128)(2,1)} %param.4), channel_id=1, source_target_pairs={{0,128},{1,192},{2,0},{3,64},{64,129},{65,193},{66,1},{67,65},{128... | collective-permute-start | bytes 49160 | tf_op jit(solution)/shard_map/ppermute | solution.py:201
  22.2 0.0 collective-permute-done.refs_1_.d1
  22.2 0.1 collective-permute-start.3
  22.3 0.0 collective-permute-done.5
  22.3 1.5 %collective-permute-start.1 = (bf16[32,4096]{1,0:T(8,128)(2,1)S(1)}, bf16[32,4096]{1,0:T(8,128)(2,1)S(1)}, u32[]{:S(2)}, u32[]{:S(2)}) collective-permute-start(bf16[32,4096]{1,0:T(8,128)(2,1)S(1)} %slice.8), channel_id=1, source_target_pairs={{0,1},{1,2},{2,3},{3,0},{4,5},{5,6},{6,7},{7,4},{8,9},{9,10},{10,1... | collective-permute-start | bytes 786440 | tf_op jit(solution)/shard_map/ppermute | solution.py:202
  23.9 0.0 collective-permute-done.6
  23.9 9.5 %all_to_all.10.refs_0_ = bf16[4,4,32,256]{3,2,1,0:T(8,128)(2,1)S(1)} all-to-all(bf16[4,4,32,256]{3,2,1,0:T(8,128)(2,1)S(1)} %broadcast_in_dim.4), channel_id=1, replica_groups=mesh['zh'=4,'zl'=2,'y'=4,'core'=2,'dim'=4] {'y'}, dimensions={0} | all-to-all | bytes 524288 | tf_op jit(solution)/shard_map/all_to_all | solution.py:210
  33.5 0.0 collective-permute-done.3.refs_2_.d2b
  33.5 0.0 collective-permute-done.1.refs_1_.d2a
  33.5 3.9 %collective-permute-start.9 = (bf16[4,4,32,256]{3,2,1,0:T(8,128)(2,1)S(1)}, bf16[4,4,32,256]{3,2,1,0:T(8,128)(2,1)S(1)}, u32[]{:S(2)}, u32[]{:S(2)}) collective-permute-start(bf16[4,4,32,256]{3,2,1,0:T(8,128)(2,1)S(1)} %hold.4.qa), channel_id=1, source_target_pairs={{0,4},{4,0},{1,5},{5,1},{2,6},{6,2},{3,7},{7,3},{8,12},{12,8},{9,1... | collective-permute-start | bytes 786440 | tf_op jit(solution)/shard_map/ppermute | solution.py:211
  37.4 0.7 copy-done.1
  38.0 0.1 prepare.1
  38.1 1.0 %collective-permute-start.8 = (bf16[4,4,32,256]{3,2,1,0:T(8,128)(2,1)S(1)}, bf16[4,4,32,256]{3,2,1,0:T(8,128)(2,1)S(1)}, u32[]{:S(2)}, u32[]{:S(2)}) collective-permute-start(bf16[4,4,32,256]{3,2,1,0:T(8,128)(2,1)S(1)} %hold.4.qa), channel_id=1, source_target_pairs={{0,32},{32,0},{1,33},{33,1},{2,34},{34,2},{3,35},{35,3},{4,36},{36... | collective-permute-start | bytes 786440 | tf_op jit(solution)/shard_map/ppermute | solution.py:212
  39.1 0.0 collective-permute-done.9.qb
  39.1 9.1 %near.1.refs_1_ = f32[64,128]{1,0:T(8,128)S(1)} custom-call(bf16[32,8192]{1,0:T(8,128)(2,1)S(1)} %copy-done.2, bf16[32,8192]{1,0:T(8,128)(2,1)S(1)} %collective-permute-done.refs_1_.d1, bf16[32,4096]{1,0:T(8,128)(2,1)S(1)} %collective-permute-done.1.refs_1_.d2a, bf16[32,4096]{1,0:T(8,128)(2,1)S(1)} %collective-permute-done.3.refs_2_.d2b, ...), custom_call_target="tpu_custom_call" | custom-call | flops 4294967296 | bytes 1048576 | tf_op jit(solution)/shard_map/near/pallas_call | solution.py:219
  48.3 0.0 collective-permute-done.8.refs_0_
  48.3 0.6 collective-permute-start.10
  48.9 4.8 %far.1 = f32[64,128]{1,0:T(8,128)S(1)} custom-call(bf16[32,8192]{1,0:T(8,128)(2,1)S(1)} %copy-done.2, bf16[32,8192]{1,0:T(8,128)(2,1)S(1)} %collective-permute-done.refs_1_.d1, bf16[32,4096]{1,0:T(8,128)(2,1)S(1)} %collective-permute-done.1.refs_1_.d2a, bf16[32,4096]{1,0:T(8,128)(2,1)S(1)} %collective-permute-done.3.refs_2_.d2b, ...), custom_call_target="tpu_custom_call" | custom-call | flops 2147483648 | bytes 1048576 | tf_op jit(solution)/shard_map/far/pallas_call | solution.py:232
  53.7 5.4 %last.1 = (f32[32,128]{1,0:T(8,128)}, f32[2,16,128]{2,1,0:T(8,128)S(1)}) custom-call(bf16[32,8192]{1,0:T(8,128)(2,1)S(1)} %copy-done.2, bf16[32,8192]{1,0:T(8,128)(2,1)S(1)} %collective-permute-done.refs_1_.d1, bf16[32,4096]{1,0:T(8,128)(2,1)S(1)} %collective-permute-done.1.refs_1_.d2a, bf16[32,4096]{1,0:T(8,128)(2,1)S(1)} %collective-permute-done.3.refs_2_.d2b, ...), custom_call_target="tpu_custom_call" | custom-call | flops 2147483648 | bytes 1048576 | tf_op jit(solution)/shard_map/last/pallas_call | solution.py:242
  59.1 19.2 %all_to_all.11 = f32[32,16,128]{2,1,0:T(8,128)S(1)} all-to-all(f32[32,16,128]{2,1,0:T(8,128)S(1)} %bitcast.13), channel_id=1, replica_groups=mesh['zh'=4,'zl'=2,'y'=4,'core'=2,'dim'=4] {'zh','zl','y'}, dimensions={0} | all-to-all | bytes 524288 | tf_op jit(solution)/shard_map/all_to_all | solution.py:256
  78.3 1.0 %top.1 = (f32[128,128]{1,0:T(8,128)S(1)}, f32[128,128]{1,0:T(8,128)S(1)}) custom-call(f32[64,8,128]{2,1,0:T(8,128)S(1)} %bitcast.10), custom_call_target="tpu_custom_call" | custom-call | tf_op jit(solution)/shard_map/top/pallas_call | solution.py:257
  79.3 2.2 %collective-permute-start.11 = (f32[128,128]{1,0:T(8,128)S(1)}, f32[128,128]{1,0:T(8,128)S(1)}, u32[]{:S(2)}, u32[]{:S(2)}) collective-permute-start(f32[128,128]{1,0:T(8,128)S(1)} %get-tuple-element.13), channel_id=1, source_target_pairs={{0,4},{4,0},{1,5},{5,1},{2,6},{6,2},{3,7},{7,3},{8,12},{12,8},{9,1... | collective-permute-start | bytes 196616 | tf_op jit(solution)/shard_map/ppermute | solution.py:265
  81.6 0.9 %collective-permute-done.11.rising = f32[128,128]{1,0:T(8,128)S(1)} collective-permute-done((f32[128,128]{1,0:T(8,128)S(1)}, f32[128,128]{1,0:T(8,128)S(1)}, u32[]{:S(2)}, u32[]{:S(2)}) %collective-permute-start.11) | collective-permute-done | bytes 65568 | tf_op jit(solution)/shard_map/ppermute | solution.py:265
  82.5 0.7 collective-permute-start.12
  83.2 2.4 %collective-permute-done.12.theirs = f32[104,128]{1,0:T(8,128)S(1)} collective-permute-done((f32[104,128]{1,0:T(8,128)S(1)}, f32[104,128]{1,0:T(8,128)S(1)}, u32[]{:S(2)}, u32[]{:S(2)}) %collective-permute-start.12) | collective-permute-done | bytes 53280 | tf_op jit(solution)/shard_map/ppermute | solution.py:281
  85.6 0.6 join.1
  (17 shorter events, 0.2 us)
Async XLA Ops:
  0.6 14.3 %collective-permute-start.2 = (bf16[32,8192]{1,0:T(8,128)(2,1)}, bf16[32,8192]{1,0:T(8,128)(2,1)S(1)}, u32[]{:S(2)}, u32[]{:S(2)}) collective-permute-start(bf16[32,8192]{1,0:T(8,128)(2,1)} %d0.5), channel_id=1, source_target_pairs={{0,3},{1,0},{2,1},{3,2},{4,7},{5,4},{6,5},{7,6},{8,11},{9,8},{10,9... | collective-permute-start | bytes 1572872 | tf_op jit(solution)/shard_map/ppermute | solution.py:202
  4.0 18.2 %collective-permute-start = (bf16[32,8192]{1,0:T(8,128)(2,1)}, bf16[32,8192]{1,0:T(8,128)(2,1)S(1)}, u32[]{:S(2)}, u32[]{:S(2)}) collective-permute-start(bf16[32,8192]{1,0:T(8,128)(2,1)} %d0.5), channel_id=1, source_target_pairs={{0,1},{1,2},{2,3},{3,0},{4,5},{5,6},{6,7},{7,4},{8,9},{9,10},{10,1... | collective-permute-start | bytes 1572872 | tf_op jit(solution)/shard_map/ppermute | solution.py:202
  4.0 18.3 %collective-permute-start.5 = (bf16[32,256]{1,0:T(8,128)(2,1)}, bf16[32,256]{1,0:T(8,128)(2,1)S(1)}, u32[]{:S(2)}, u32[]{:S(2)}) collective-permute-start(bf16[32,256]{1,0:T(8,128)(2,1)} %param.4), channel_id=1, source_target_pairs={{0,64},{1,128},{2,192},{3,0},{64,65},{65,129},{66,193},{67,1},{128... | collective-permute-start | bytes 49160 | tf_op jit(solution)/shard_map/ppermute | solution.py:201
  7.0 16.9 %collective-permute-start.4 = (bf16[32,256]{1,0:T(8,128)(2,1)}, bf16[32,256]{1,0:T(8,128)(2,1)S(1)}, u32[]{:S(2)}, u32[]{:S(2)}) collective-permute-start(bf16[32,256]{1,0:T(8,128)(2,1)} %param.4), channel_id=1, source_target_pairs={{0,0},{1,64},{2,128},{3,192},{64,1},{65,65},{66,129},{67,193},{128... | collective-permute-start | bytes 49160 | tf_op jit(solution)/shard_map/ppermute | solution.py:201
  8.4 15.5 %collective-permute-start.7 = (bf16[32,256]{1,0:T(8,128)(2,1)}, bf16[32,256]{1,0:T(8,128)(2,1)S(1)}, u32[]{:S(2)}, u32[]{:S(2)}) collective-permute-start(bf16[32,256]{1,0:T(8,128)(2,1)} %param.4), channel_id=1, source_target_pairs={{0,192},{1,0},{2,64},{3,128},{64,193},{65,1},{66,65},{67,129},{128... | collective-permute-start | bytes 49160 | tf_op jit(solution)/shard_map/ppermute | solution.py:201
  14.9 9.0 %collective-permute-start.6 = (bf16[32,256]{1,0:T(8,128)(2,1)}, bf16[32,256]{1,0:T(8,128)(2,1)S(1)}, u32[]{:S(2)}, u32[]{:S(2)}) collective-permute-start(bf16[32,256]{1,0:T(8,128)(2,1)} %param.4), channel_id=1, source_target_pairs={{0,128},{1,192},{2,0},{3,64},{64,129},{65,193},{66,1},{67,65},{128... | collective-permute-start | bytes 49160 | tf_op jit(solution)/shard_map/ppermute | solution.py:201
  22.2 11.2 %collective-permute-start.3 = (bf16[32,4096]{1,0:T(8,128)(2,1)S(1)}, bf16[32,4096]{1,0:T(8,128)(2,1)S(1)}, u32[]{:S(2)}, u32[]{:S(2)}) collective-permute-start(bf16[32,4096]{1,0:T(8,128)(2,1)S(1)} %slice.9), channel_id=1, source_target_pairs={{0,3},{1,0},{2,1},{3,2},{4,7},{5,4},{6,5},{7,6},{8,11},{9,8},{10,9... | collective-permute-start | bytes 786440 | tf_op jit(solution)/shard_map/ppermute | solution.py:202
  22.3 11.1 %collective-permute-start.1 = (bf16[32,4096]{1,0:T(8,128)(2,1)S(1)}, bf16[32,4096]{1,0:T(8,128)(2,1)S(1)}, u32[]{:S(2)}, u32[]{:S(2)}) collective-permute-start(bf16[32,4096]{1,0:T(8,128)(2,1)S(1)} %slice.8), channel_id=1, source_target_pairs={{0,1},{1,2},{2,3},{3,0},{4,5},{5,6},{6,7},{7,4},{8,9},{9,10},{10,1... | collective-permute-start | bytes 786440 | tf_op jit(solution)/shard_map/ppermute | solution.py:202
  33.5 3.9 %copy-start = (s32[128,32]{0,1:T(8,128)S(1)}, s32[128,32]{0,1:T(8,128)}, u32[]{:S(2)}) copy-start(s32[128,32]{0,1:T(8,128)} %param.6) | copy-start | bytes 49156
  33.5 5.7 %copy-start.2 = (bf16[32,8192]{1,0:T(8,128)(2,1)S(1)}, bf16[32,8192]{1,0:T(8,128)(2,1)}, u32[]{:S(2)}) copy-start(bf16[32,8192]{1,0:T(8,128)(2,1)} %d0.5) | copy-start | bytes 1572868
  33.5 5.7 %collective-permute-start.9 = (bf16[4,4,32,256]{3,2,1,0:T(8,128)(2,1)S(1)}, bf16[4,4,32,256]{3,2,1,0:T(8,128)(2,1)S(1)}, u32[]{:S(2)}, u32[]{:S(2)}) collective-permute-start(bf16[4,4,32,256]{3,2,1,0:T(8,128)(2,1)S(1)} %hold.4.qa), channel_id=1, source_target_pairs={{0,4},{4,0},{1,5},{5,1},{2,6},{6,2},{3,7},{7,3},{8,12},{12,8},{9,1... | collective-permute-start | bytes 786440 | tf_op jit(solution)/shard_map/ppermute | solution.py:211
  37.4 0.7 copy-start.1
  38.1 10.1 %collective-permute-start.8 = (bf16[4,4,32,256]{3,2,1,0:T(8,128)(2,1)S(1)}, bf16[4,4,32,256]{3,2,1,0:T(8,128)(2,1)S(1)}, u32[]{:S(2)}, u32[]{:S(2)}) collective-permute-start(bf16[4,4,32,256]{3,2,1,0:T(8,128)(2,1)S(1)} %hold.4.qa), channel_id=1, source_target_pairs={{0,32},{32,0},{1,33},{33,1},{2,34},{34,2},{3,35},{35,3},{4,36},{36... | collective-permute-start | bytes 786440 | tf_op jit(solution)/shard_map/ppermute | solution.py:212
  48.3 5.4 %collective-permute-start.10 = (bf16[4,4,32,256]{3,2,1,0:T(8,128)(2,1)S(1)}, bf16[4,4,32,256]{3,2,1,0:T(8,128)(2,1)S(1)}, u32[]{:S(2)}, u32[]{:S(2)}) collective-permute-start(bf16[4,4,32,256]{3,2,1,0:T(8,128)(2,1)S(1)} %hold.5.qa), channel_id=1, source_target_pairs={{0,4},{4,0},{1,5},{5,1},{2,6},{6,2},{3,7},{7,3},{8,12},{12,8},{9,1... | collective-permute-start | bytes 786440 | tf_op jit(solution)/shard_map/ppermute | solution.py:230
  79.3 3.1 %collective-permute-start.11 = (f32[128,128]{1,0:T(8,128)S(1)}, f32[128,128]{1,0:T(8,128)S(1)}, u32[]{:S(2)}, u32[]{:S(2)}) collective-permute-start(f32[128,128]{1,0:T(8,128)S(1)} %get-tuple-element.13), channel_id=1, source_target_pairs={{0,4},{4,0},{1,5},{5,1},{2,6},{6,2},{3,7},{7,3},{8,12},{12,8},{9,1... | collective-permute-start | bytes 196616 | tf_op jit(solution)/shard_map/ppermute | solution.py:265
  82.5 3.1 %collective-permute-start.12 = (f32[104,128]{1,0:T(8,128)S(1)}, f32[104,128]{1,0:T(8,128)S(1)}, u32[]{:S(2)}, u32[]{:S(2)}) collective-permute-start(f32[104,128]{1,0:T(8,128)S(1)} %merge.1.mine), channel_id=1, source_target_pairs={{0,32},{32,0},{1,33},{33,1},{2,34},{34,2},{3,35},{35,3},{4,36},{36... | collective-permute-start | bytes 159752 | tf_op jit(solution)/shard_map/ppermute | solution.py:281
